TPU v7x, 512 devices: a whole 4x4x16 slice. The times are simulated.
512 devices in a mesh: ctx: 64 (over z, x), ch: 8 (over y, core).
Axes of the slice: x: 4, y: 4, z: 16, core: 2. Of those that a mesh axis runs over, the one named last changes fastest.
Arguments:
- stream: bfloat16 [8192, 4096], P('ctx', 'ch'), may hold values from -1200 to 1200
- norm_gain: float32 [4096], P('ch'), may hold values from 0.5 to 1.5
- short_filter: float32 [3, 3, 4096], P(None, None, 'ch'), may hold values from -3 to 3
- decay_rate: float32 [4096, 16], P('ch'), may hold values from 0 to 1, as said below
- residue: float32 [4096, 16], P('ch'), may hold values from -1 to 1
Outputs:
- mixed: bfloat16 [8192, 4096], P('ctx', 'ch')
Inputs may be any that keep to these rules, and one draw needn't show every extreme that they name: `decay_rate`: decay per position of each mode, positive.
All inputs are finite; a program needn't handle non-finite values.
Results may differ from a plain program's by a relative error of at most 0.01155.
Values may be sent and summed in bfloat16 or wider, within the bound.
No kernel may reach another device: no remote copies, remote signals or barrier semaphores. Data moves between devices by JAX's collectives and lax.ppermute only.
A program may use at most 64 MiB of HBM per device.

v0:
```python
import math

import jax
import jax.numpy as jnp
from jax import lax
from jax.sharding import PartitionSpec as P

EXACT = lax.Precision.HIGHEST
EPSILON = 1e-05


def from_behind(array, axis, by):
    count = lax.axis_size(axis)
    pairs = [(i, i + by) for i in range(count) if 0 <= i + by < count]
    return lax.ppermute(array, axis, pairs)


def angle_table(row_count, col_count, period):
    row_index = lax.broadcasted_iota(jnp.int32, (row_count, col_count), 0)
    col_index = lax.broadcasted_iota(jnp.int32, (row_count, col_count), 1)
    phase = (row_index * col_index % period).astype(jnp.float32) * (2.0 * math.pi / period)
    return (jnp.cos(phase), jnp.sin(phase))


def filter_spectrum(decay_rate, residue, length, outer, inner):
    total = 2 * length
    freq = lax.broadcasted_iota(jnp.int32, (outer, inner), 0) * inner + lax.broadcasted_iota(
        jnp.int32, (outer, inner), 1
    )
    phase = freq.astype(jnp.float32) * (2.0 * math.pi / total)
    half_sin = jnp.sin(0.5 * phase)[None]
    full_sin = jnp.sin(phase)[None]
    parity = (1 - 2 * (freq % 2)).astype(jnp.float32)[None]

    def add_mode(mode, sums):
        real_sum, imag_sum = sums
        rate = lax.dynamic_index_in_dim(decay_rate, mode, 1, keepdims=False)[:, None, None]
        weight = lax.dynamic_index_in_dim(residue, mode, 1, keepdims=False)[:, None, None]
        pole = jnp.exp(-rate)
        real_den = -jnp.expm1(-rate) + 2.0 * pole * half_sin * half_sin
        imag_den = pole * full_sin
        numer = 1.0 - jnp.exp(-rate * length) * parity
        scale = weight * numer / (real_den * real_den + imag_den * imag_den)
        return (real_sum + scale * real_den, imag_sum - scale * imag_den)

    empty = jnp.zeros((decay_rate.shape[0], outer, inner), jnp.float32)
    return lax.fori_loop(0, decay_rate.shape[1], add_mode, (empty, empty))


def causal_conv(signal, decay_rate, residue):
    count, length = signal.shape
    total = 2 * length
    bits = total.bit_length() - 1
    big = 2 ** (bits - bits // 2)
    small = total // big
    lower = signal.reshape(count, big // 2, small)
    cos_first, sin_first = angle_table(big, big // 2, big)
    part_re = jnp.einsum("kn,enj->ekj", cos_first, lower, precision=EXACT)
    part_im = -jnp.einsum("kn,enj->ekj", sin_first, lower, precision=EXACT)
    cos_turn, sin_turn = angle_table(big, small, total)
    turn_re = part_re * cos_turn + part_im * sin_turn
    turn_im = part_im * cos_turn - part_re * sin_turn
    cos_second, sin_second = angle_table(small, small, small)
    spec_re = jnp.einsum("an,ekn->eak", cos_second, turn_re, precision=EXACT) + jnp.einsum(
        "an,ekn->eak", sin_second, turn_im, precision=EXACT
    )
    spec_im = jnp.einsum("an,ekn->eak", cos_second, turn_im, precision=EXACT) - jnp.einsum(
        "an,ekn->eak", sin_second, turn_re, precision=EXACT
    )
    filt_re, filt_im = filter_spectrum(decay_rate, residue, length, small, big)
    prod_re = spec_re * filt_re - spec_im * filt_im
    prod_im = spec_re * filt_im + spec_im * filt_re
    back_re = jnp.einsum("nk,ekb->enb", cos_second, prod_re, precision=EXACT) - jnp.einsum(
        "nk,ekb->enb", sin_second, prod_im, precision=EXACT
    )
    back_im = jnp.einsum("nk,ekb->enb", cos_second, prod_im, precision=EXACT) + jnp.einsum(
        "nk,ekb->enb", sin_second, prod_re, precision=EXACT
    )
    cos_back, sin_back = angle_table(small, big, total)
    twist_re = back_re * cos_back - back_im * sin_back
    twist_im = back_re * sin_back + back_im * cos_back
    cos_last, sin_last = angle_table(big // 2, big, big)
    result = jnp.einsum("mb,enb->emn", cos_last, twist_re, precision=EXACT) - jnp.einsum(
        "mb,enb->emn", sin_last, twist_im, precision=EXACT
    )
    return result.reshape(count, length) / total


def normalize(values, norm_gain, sums, chan_total):
    mean_square = sums / chan_total
    return (values * lax.rsqrt(mean_square + EPSILON)[:, None] * norm_gain[None, :]).astype(
        jnp.bfloat16
    )


def per_device(stream, norm_gain, short_filter, decay_rate, residue):
    row_count, chan_count = stream.shape
    taps = short_filter.shape[0]
    chan_total = chan_count * lax.axis_size("ch")
    values = stream.astype(jnp.float32)
    sums = lax.psum(jnp.sum(values * values, axis=1), "ch")
    normed = normalize(values, norm_gain, sums, chan_total)
    rim = from_behind(normed[row_count - (taps - 1) :], "ctx", 1)
    padded = jnp.concatenate([rim, normed], axis=0).astype(jnp.float32)
    roles = []
    for role in range(3):
        total = jnp.zeros((row_count, chan_count), jnp.float32)
        for tap in range(taps):
            total = (
                total
                + short_filter[tap, role][None, :]
                * padded[taps - 1 - tap : taps - 1 - tap + row_count]
            )
        roles.append(total)
    query_held = roles[0].astype(jnp.bfloat16)
    product = (roles[1] * roles[2]).astype(jnp.bfloat16)
    moved = lax.all_to_all(product, "ctx", split_axis=1, concat_axis=0, tiled=True)
    group_width = moved.shape[1]
    start = lax.axis_index("ctx") * group_width
    my_rates = lax.dynamic_slice_in_dim(decay_rate, start, group_width, 0)
    my_weights = lax.dynamic_slice_in_dim(residue, start, group_width, 0)
    convolved = causal_conv(moved.astype(jnp.float32).T, my_rates, my_weights)
    conv = lax.all_to_all(
        convolved.T.astype(jnp.bfloat16), "ctx", split_axis=0, concat_axis=1, tiled=True
    )
    return (query_held.astype(jnp.float32) * conv.astype(jnp.float32)).astype(jnp.bfloat16)


def solution(mesh):
    in_specs = (P("ctx", "ch"), P("ch"), P(None, None, "ch"), P("ch", None), P("ch", None))
    out_specs = P("ctx", "ch")
    return jax.shard_map(
        per_device, mesh=mesh, in_specs=in_specs, out_specs=out_specs, check_vma=False
    )
```

profile of v0, /device:TPU:32, one launch (start us, length us, event | category | flops | bytes accessed | tf_op | source)
XLA Modules:
  0.0 105.9 jit_solution(15359804682971094967)
XLA Ops:
  0.0 1.0 copy.20
  1.1 14.9 %psum.7 = f32[128]{0:T(128)S(1)} all-reduce(f32[128]{0:T(128)S(1)} %fusion.32), channel_id=1, replica_groups=mesh['ctx'=64,'ch'=8] {'ch'}, use_global_device_ids=true, to_apply=%region_1.0 | all-reduce | flops 128 | bytes 1024 | tf_op jit(solution)/shard_map/psum | solution.py:101
  16.3 3.4 %collective-permute-start = (bf16[2,512]{0,1:T(8,128)(2,1)S(1)}, bf16[2,512]{0,1:T(8,128)(2,1)S(1)}, u32[]{:S(2)}, u32[]{:S(2)}) collective-permute-start(bf16[2,512]{0,1:T(8,128)(2,1)S(1)} %slice.58), channel_id=1, source_target_pairs={{0,8},{8,16},{16,24},{24,32},{32,40},{40,48},{48,56},{56,64},{64,7... | collective-permute-start | bytes 6152 | tf_op jit(solution)/shard_map/ppermute | solution.py:15
  19.7 0.8 constant_dynamic-slice_fusion
  20.5 4.7 %collective-permute-done = bf16[2,512]{0,1:T(8,128)(2,1)S(1)} collective-permute-done((bf16[2,512]{0,1:T(8,128)(2,1)S(1)}, bf16[2,512]{0,1:T(8,128)(2,1)S(1)}, u32[]{:S(2)}, u32[]{:S(2)}) %collective-permute-start) | collective-permute-done | bytes 2080 | tf_op jit(solution)/shard_map/ppermute | solution.py:15
  25.4 1.3 %fusion.42 = bf16[128,64,8]{0,2,1:T(8,128)(2,1)} fusion(f32[512]{0:T(512)S(1)} %bitcast.123, f32[512]{0:T(512)S(1)} %bitcast.124, f32[512]{0:T(512)S(1)} %bitcast.119, f32[130,512]{0,1:T(8,128)S(1)} %maximum_convert_fusion, f32[512]{0:T(512)S(1)} %bitcast.120, f32[512]{0:T(512)S(1)} %bitcast.121, f32[512]{0:T(512)S(1)} %bitcast.122), kind=kLoop, calls=%fused_computation.73 | loop fusion | flops 786432 | bytes 929792 | tf_op jit(solution)/shard_map/all_to_all | solution.py:117
  26.6 17.0 %all-to-all-start = ((bf16[128,64,8]{0,2,1:T(8,128)(2,1)}), bf16[128,64,8]{0,2,1:T(8,128)(2,1)S(1)}, u32[]{:S(2)}, u32[]{:S(2)}) async-start(bf16[128,64,8]{0,2,1:T(8,128)(2,1)} %fusion.42), calls=%async_computation | async-start | bytes 262144 | tf_op jit(solution)/shard_map/all_to_all | solution.py:117
  43.6 19.1 %while.19 = (s32[]{:T(128)}, f32[8,128,128]{2,1,0:T(8,128)S(1)}, f32[8,128,128]{2,1,0:T(8,128)S(1)}, f32[8,16]{0,1:T(8,128)S(1)}, f32[8,16]{0,1:T(8,128)S(1)}, /*index=5*/s32[128]{0:T(128)S(1)}, s32[]{:T(128)}, s32[]{:T(128)}) while((s32[]{:T(128)}, f32[8,128,128]{2,1,0:T(8,128)S(1)}, ...), condition=%wide.region_3.4_spmd.clone.clone.clone.clone, body=%wide.region_2.3_spmd.clone.clone.clone.clone.sunk | while | flops 2539555 | bytes 2491983 | solution.py:47
  43.6 0.5 sine_bitcast_fusion.3
  44.8 0.5 sine_bitcast_fusion.3
  46.0 0.5 sine_bitcast_fusion.3
  46.7 0.5 fusion.160
  47.2 0.5 sine_bitcast_fusion.3
  47.9 0.5 fusion.160
  48.4 0.5 sine_bitcast_fusion.3
  49.0 0.5 fusion.160
  49.5 0.5 sine_bitcast_fusion.3
  50.2 0.5 fusion.160
  50.7 0.5 sine_bitcast_fusion.3
  51.4 0.5 fusion.160
  51.9 0.5 sine_bitcast_fusion.3
  52.6 0.5 fusion.160
  53.1 0.5 sine_bitcast_fusion.3
  53.8 0.5 fusion.160
  54.3 0.5 sine_bitcast_fusion.3
  55.0 0.5 fusion.160
  55.4 0.5 sine_bitcast_fusion.3
  56.1 0.5 fusion.160
  56.6 0.5 sine_bitcast_fusion.3
  57.3 0.5 fusion.160
  57.8 0.5 sine_bitcast_fusion.3
  59.0 0.5 sine_bitcast_fusion.3
  60.2 0.5 sine_bitcast_fusion.3
  61.4 0.5 sine_bitcast_fusion.3
  63.9 0.5 fusion.17
  64.4 0.5 convolution_bitcast_fusion
  64.9 1.2 %fusion.45 = f32[8,128,128]{2,1,0:T(8,128)S(1)} fusion(f32[8,128,128]{1,2,0:T(8,128)S(1)} %fusion.17, f32[8,128,128]{1,2,0:T(8,128)S(1)} %convolution_bitcast_fusion, f32[128,128]{0,1:T(8,128)S(1)} %copy.22, f32[128,128]{0,1:T(8,128)S(1)} %copy.21), kind=kOutput, calls=%fused_computation.76 | convolution fusion | flops 201949184 | bytes 1703936 | tf_op jit(solution)/shard_map/an,ekn->eak/dot_general | solution.py:64
  66.1 1.2 %fusion.46 = f32[8,128,128]{2,1,0:T(8,128)S(1)} fusion(f32[8,128,128]{1,2,0:T(8,128)S(1)} %convolution_bitcast_fusion, f32[8,128,128]{1,2,0:T(8,128)S(1)} %fusion.17, f32[128,128]{0,1:T(8,128)S(1)} %copy.22, f32[128,128]{0,1:T(8,128)S(1)} %copy.21), kind=kOutput, calls=%fused_computation.77 | convolution fusion | flops 201949184 | bytes 1703936 | tf_op jit(solution)/shard_map/an,ekn->eak/dot_general | solution.py:67
  67.3 1.2 %fusion.21 = f32[8,128,128]{1,2,0:T(8,128)S(1)} fusion(f32[8,128,128]{2,1,0:T(8,128)S(1)} %fusion.45, f32[8,128,128]{1,2,0:T(8,128)S(1)} %convolution_bitcast_fusion, f32[8,128,128]{1,2,0:T(8,128)S(1)} %fusion.17, f32[128,128]{0,1:T(8,128)S(1)} %copy.22, f32[128,128]{0,1:T(8,128)S(1)} %copy.21), kind=kOutput, calls=%fused_computation.40 | convolution fusion | flops 202080256 | bytes 2228224 | tf_op jit(solution)/shard_map/an,ekn->eak/dot_general | solution.py:64
  68.5 1.2 %multiply_subtract_fusion = (f32[8,128,128]{1,2,0:T(8,128)S(1)}, f32[8,128,128]{1,2,0:T(8,128)S(1)}) fusion(f32[8,128,128]{1,2,0:T(8,128)S(1)} %copy.28, f32[8,128,128]{1,2,0:T(8,128)S(1)} %fusion.21, f32[8,128,128]{1,2,0:T(8,128)S(1)} %copy.25, f32[8,128,128]{2,1,0:T(8,128)S(1)} %fusion.46, f32[8,128,128]{1,2,0:T(8,128)S(1)} %fusion.17, ...), kind=kOutput, calls=%fused_computation.53 | convolution fusion | flops 202866688 | bytes 4325376 | tf_op jit(solution)/shard_map/an,ekn->eak/dot_general | solution.py:67
  69.7 0.8 fusion.55
  70.5 0.8 fusion.57
  71.3 0.8 fusion.18
  72.2 0.8 fusion.19
  73.0 0.6 fusion.28
  73.6 0.6 fusion.24
  74.4 30.4 %all_to_all.32 = bf16[64,128,8]{1,2,0:T(8,128)(2,1)S(1)} all-to-all(bf16[64,128,8]{1,2,0:T(8,128)(2,1)S(1)} %bitcast.115), channel_id=1, replica_groups=mesh['ctx'=64,'ch'=8] {'ctx'}, dimensions={0} | all-to-all | bytes 262144 | tf_op jit(solution)/shard_map/all_to_all | solution.py:123
  105.1 0.8 copy.33
  (92 shorter events, 7.2 us)
Async XLA Ops:
  1.1 14.9 %copy-start.1 = (f32[512]{0:T(512)S(1)}, f32[512]{0:T(512)}, u32[]{:S(2)}) copy-start(f32[512]{0:T(512)} %param.8) | copy-start | bytes 6148
  16.1 3.5 %copy-start = (f32[3,3,512]{2,1,0:T(4,128)S(1)}, f32[3,3,512]{2,1,0:T(4,128)}, u32[]{:S(2)}) copy-start(f32[3,3,512]{2,1,0:T(4,128)} %param.9) | copy-start | bytes 55300
  16.3 9.0 %collective-permute-start = (bf16[2,512]{0,1:T(8,128)(2,1)S(1)}, bf16[2,512]{0,1:T(8,128)(2,1)S(1)}, u32[]{:S(2)}, u32[]{:S(2)}) collective-permute-start(bf16[2,512]{0,1:T(8,128)(2,1)S(1)} %slice.58), channel_id=1, source_target_pairs={{0,8},{8,16},{16,24},{24,32},{32,40},{40,48},{48,56},{56,64},{64,7... | collective-permute-start | bytes 6152 | tf_op jit(solution)/shard_map/ppermute | solution.py:15
  26.6 37.2 %all-to-all-start = ((bf16[128,64,8]{0,2,1:T(8,128)(2,1)}), bf16[128,64,8]{0,2,1:T(8,128)(2,1)S(1)}, u32[]{:S(2)}, u32[]{:S(2)}) async-start(bf16[128,64,8]{0,2,1:T(8,128)(2,1)} %fusion.42), calls=%async_computation | async-start | bytes 262144 | tf_op jit(solution)/shard_map/all_to_all | solution.py:117
where the time goes:
time: 106 us
  blocking collectives  45.2 us (43%)
  other arithmetic  20.5 us (19%)
  starting transfers between devices  20.4 us (19%)
  matrix products  10.3 us (10%)
  waiting for transfers between devices  4.73 us (4%)
  local copies, waits for them, and re-layouts  3.38 us (3%)
  loops' own time  1.14 us (1%)
    all_to_all x1, blocking collectives, per_device(): lax.all_to_all(convolved.T.astype(jnp.bfloat16), 'ctx', split_axis=0, con...  30.4 us
    all_to_all x1, starting transfers between devices, per_device(): lax.all_to_all(product, 'ctx', split_axis=1, concat_axis=0, tiled=True)  17 us
    psum x1, blocking collectives, per_device(): sums = lax.psum(jnp.sum(values * values, axis=1), 'ch')  14.9 us
    mul x16, other arithmetic, add_mode(): imag_den = pole * full_sin  8.07 us
    sub x16, other arithmetic, add_mode(): return (real_sum + scale * real_den, imag_sum - scale * imag_den)  7.6 us
    ppermute x1, waiting for transfers between devices, from_behind(): return lax.ppermute(array, axis, pairs)  4.72 us
    ppermute x1, starting transfers between devices, from_behind(): return lax.ppermute(array, axis, pairs)  3.4 us
  transfers between devices with their start and end apart: 2, of which 1 were waited for; matrix products, arithmetic and copies ran while one was open for 19% of the time, Pallas kernels for 0%

commit v1 on v0

v1 whole, which is shorter than its diff:
```python
import jax
import jax.numpy as jnp
from jax import lax
from jax.experimental import pallas as pl
from jax.experimental.pallas import tpu as pltpu
from jax.sharding import PartitionSpec as P

EXACT = lax.Precision.HIGHEST
EPSILON = 1e-05
SUB = 8
LANES = 128
RIM = 16
NEAR = 8

F32 = jnp.float32
BF16 = jnp.bfloat16


def call(body, outs, *args, scratch=(), flops=0):
    shapes = [jax.ShapeDtypeStruct(s, d) for s, d in outs]
    moved = sum(a.size * a.dtype.itemsize for a in args)
    return pl.pallas_call(
        body,
        out_shape=shapes,
        in_specs=[pl.BlockSpec(memory_space=pltpu.VMEM)] * len(args),
        out_specs=[pl.BlockSpec(memory_space=pltpu.VMEM)] * len(shapes),
        scratch_shapes=list(scratch),
        compiler_params=pltpu.CompilerParams(vmem_limit_bytes=16 * 2**20),
        cost_estimate=pl.CostEstimate(flops=flops, bytes_accessed=moved, transcendentals=0),
    )(*args)


def square_sums(stream_ref, rim_ref, rate_ref, residue_ref, sums_ref, rate_out, residue_out):
    peers = sums_ref.shape[0]
    ones = jnp.ones((peers, stream_ref.shape[1]), F32)
    contract = (((1,), (1,)), ((), ()))

    def rows(ref):
        values = ref[...].astype(F32)
        return lax.dot_general(ones, values * values, contract, precision=EXACT, preferred_element_type=F32)

    count = stream_ref.shape[0]
    sums_ref[...] = jnp.zeros_like(sums_ref)
    sums_ref[:, :count] = rows(stream_ref)
    sums_ref[:, count : count + RIM] = rows(rim_ref)
    rate_out[...] = rate_ref[...].T
    residue_out[...] = residue_ref[...].T


def block_states(chan_total, sums_ref, stream_ref, rim_ref, gain_ref, taps_ref, rate_ref, query_ref, product_ref, states_ref, normed_ref):
    count, chans = stream_ref.shape
    peers = states_ref.shape[0]
    modes = rate_ref.shape[0]
    ones = jnp.ones((sums_ref.shape[0], chans), F32)

    def normalize(ref, sums):
        mean_square = lax.dot_general(sums, ones, (((0,), (0,)), ((), ())), precision=EXACT, preferred_element_type=F32) / chan_total
        values = ref[...].astype(F32) * lax.rsqrt(mean_square + EPSILON) * gain_ref[...]
        return values.astype(BF16).astype(F32)

    normed_ref[:RIM] = normalize(rim_ref, sums_ref[:, count : count + RIM])
    normed_ref[RIM:] = normalize(stream_ref, sums_ref[:, :count])
    shifted = [normed_ref[RIM - j : RIM - j + count] for j in range(3)]

    def feature(role):
        total = taps_ref[pl.ds(role, 1)] * shifted[0]
        total = total + taps_ref[pl.ds(3 + role, 1)] * shifted[1]
        return total + taps_ref[pl.ds(6 + role, 1)] * shifted[2]

    query_ref[...] = feature(0).astype(BF16)
    product_ref[...] = (feature(1) * feature(2)).astype(BF16).astype(F32)

    lag = (SUB - 1 - lax.broadcasted_iota(jnp.int32, (SUB, LANES), 0)).astype(F32)

    def one_lane(lane, carry):
        at = pl.ds(pl.multiple_of(lane * LANES, LANES), LANES)
        blocks = [product_ref[pl.ds(i * SUB, SUB), at] for i in range(count // SUB)]
        for mode in range(modes):
            rate = rate_ref[pl.ds(mode, 1), at]
            step = jnp.broadcast_to(jnp.exp(-SUB * rate), (SUB, LANES))
            total = blocks[0]
            for block in blocks[1:]:
                total = total * step + block
            total = jnp.sum(total * jnp.exp(-rate * lag), axis=0, keepdims=True)
            for peer in range(peers):
                states_ref[peer, pl.ds(mode, 1), at] = total
        return carry

    lax.fori_loop(0, chans // LANES, one_lane, 0)


def add_mode(totals, term, rate):
    step = jnp.broadcast_to(jnp.exp(-SUB * rate), term.shape)
    out = []
    for total in totals:
        out.append(total + term)
        term = term * step
    return out


def inner_conv(rate_ref, residue_ref, product_ref, local_ref, filter_ref):
    count, chans = product_ref.shape
    modes = rate_ref.shape[0]
    blocks = count // SUB
    row = lax.broadcasted_iota(jnp.int32, (SUB, LANES), 0)
    lead = row.astype(F32)

    def one_lane(lane, carry):
        at = pl.ds(pl.multiple_of(lane * LANES, LANES), LANES)

        zero = jnp.zeros((SUB, LANES), F32)
        totals = [zero] * blocks
        for mode in range(modes):
            rate = rate_ref[pl.ds(mode, 1), at]
            term = residue_ref[pl.ds(mode, 1), at] * jnp.exp(-rate * lead)
            totals = add_mode(totals, term, rate)
        for i in range(blocks):
            filter_ref[pl.ds(i * SUB, SUB), :] = totals[i]

        shifted = [product_ref[pl.ds(i * SUB, SUB), at] for i in range(blocks)]
        totals = [zero] * blocks
        for b in range(SUB):
            for a in range(blocks):
                weight = filter_ref[pl.ds(a * SUB + b, 1), :]
                for j in range(blocks - a):
                    totals[j + a] = totals[j + a] + weight * shifted[j]
            if b < SUB - 1:
                rolled = [pltpu.roll(s, 1, 0) for s in shifted]
                shifted = [jnp.where(row == 0, before, now) for before, now in zip([zero] + rolled[:-1], rolled)]
        for i in range(blocks):
            local_ref[pl.ds(i * SUB, SUB), at] = totals[i]
        return carry

    lax.fori_loop(0, chans // LANES, one_lane, 0)


def near_scan(block, got_ref, rate_ref, before_ref, totals_ref):
    place = lax.axis_index("ctx") % NEAR
    step = jnp.exp(-block * rate_ref[...])
    total = jnp.zeros_like(step)
    before = total
    for j in range(NEAR):
        before = jnp.where(place == j, total, before)
        total = total * step + got_ref[j]
    before_ref[...] = before
    for peer in range(totals_ref.shape[0]):
        totals_ref[peer] = total


def outer_conv(block, far, got_ref, before_ref, rate_ref, residue_ref, local_ref, query_ref, mixed_ref, state_ref):
    count, chans = local_ref.shape
    modes = rate_ref.shape[0]
    blocks = count // SUB
    index = lax.axis_index("ctx")
    place, group = index % NEAR, index // NEAR
    rates = rate_ref[...]
    step = jnp.exp(-(block * NEAR) * rates)
    total = jnp.zeros_like(rates)
    state = total
    for j in range(far):
        state = jnp.where(group == j, total, state)
        total = total * step + got_ref[j]
    state = state * jnp.exp(-rates * (block * place).astype(F32)) + before_ref[...]
    state_ref[...] = state * residue_ref[...]
    lead = (1 + lax.broadcasted_iota(jnp.int32, (SUB, LANES), 0)).astype(F32)

    def one_lane(lane, carry):
        at = pl.ds(pl.multiple_of(lane * LANES, LANES), LANES)

        totals = [local_ref[pl.ds(i * SUB, SUB), at] for i in range(blocks)]
        for mode in range(modes):
            rate = rate_ref[pl.ds(mode, 1), at]
            term = state_ref[pl.ds(mode, 1), at] * jnp.exp(-rate * lead)
            totals = add_mode(totals, term, rate)
        for i in range(0, blocks, 2):
            rows = pl.ds(i * SUB, 2 * SUB)
            conv = jnp.concatenate(totals[i : i + 2], axis=0).astype(BF16).astype(F32)
            mixed_ref[rows, at] = (query_ref[rows, at].astype(F32) * conv).astype(BF16)
        return carry

    lax.fori_loop(0, chans // LANES, one_lane, 0)


def gather(copies, axis, groups=None):
    return lax.all_to_all(copies, axis, 0, 0, tiled=True, axis_index_groups=groups)


def per_device(stream, norm_gain, short_filter, decay_rate, residue):
    count, chans = stream.shape
    modes = decay_rate.shape[1]
    peers = lax.axis_size("ch")
    ctx = lax.axis_size("ctx")
    far = ctx // NEAR
    near_groups = [[g * NEAR + m for m in range(NEAR)] for g in range(far)]
    far_groups = [[g * NEAR + m for g in range(far)] for m in range(NEAR)]

    rim = lax.ppermute(stream[count - RIM :], "ctx", [(i, i + 1) for i in range(ctx - 1)])
    sums, rates, weights = call(
        square_sums,
        [((peers, 2 * LANES), F32), ((modes, chans), F32), ((modes, chans), F32)],
        stream, rim, decay_rate, residue,
    )
    sums = gather(sums, "ch")
    query, product, states = call(
        lambda *refs: block_states(chans * peers, *refs),
        [((count, chans), BF16), ((count, chans), F32), ((NEAR, modes, chans), F32)],
        sums, stream, rim, norm_gain[None, :], short_filter.reshape(9, chans), rates,
        scratch=[pltpu.VMEM((RIM + count, chans), F32)],
    )
    states = gather(states, "ctx", near_groups)
    (local,) = call(
        inner_conv, [((count, chans), F32)], rates, weights, product,
        scratch=[pltpu.VMEM((count, LANES), F32)], flops=10**7,
    )
    before, totals = call(
        lambda *refs: near_scan(count, *refs),
        [((modes, chans), F32), ((far, modes, chans), F32)],
        states, rates,
    )
    totals = gather(totals, "ctx", far_groups)
    (mixed,) = call(
        lambda *refs: outer_conv(count, far, *refs),
        [((count, chans), BF16)],
        totals, before, rates, weights, local, query,
        scratch=[pltpu.VMEM((modes, chans), F32)],
    )
    return mixed


def solution(mesh):
    in_specs = (P("ctx", "ch"), P("ch"), P(None, None, "ch"), P("ch", None), P("ch", None))
    out_specs = P("ctx", "ch")
    return jax.shard_map(
        per_device, mesh=mesh, in_specs=in_specs, out_specs=out_specs, check_vma=False
    )
```

time: 106 us -> 69 us (0.65)
  the two profiles are of different devices: /device:TPU:32 before, /device:TPU:2 now
where the time goes in v1:
time: 69 us; the launch traced here: 68.5 us
  waiting for transfers between devices  29.4 us (43%)
  starting transfers between devices  22.5 us (33%)
  blocking collectives  9.34 us (14%)
  Pallas kernels  4.88 us (7%)
  local copies, waits for them, and re-layouts  2.32 us (3%)
    all_to_all x2, waiting for transfers between devices, gather(): lax.all_to_all(copies, axis, 0, 0, tiled=True, axis_index_groups=groups)  24.2 us
    all_to_all x2, starting transfers between devices, gather(): lax.all_to_all(copies, axis, 0, 0, tiled=True, axis_index_groups=groups)  19 us
    all_to_all x1, blocking collectives, gather(): lax.all_to_all(copies, axis, 0, 0, tiled=True, axis_index_groups=groups)  9.34 us
    ppermute x1, waiting for transfers between devices, per_device(): lax.ppermute(stream[count - RIM:], 'ctx', [(i, i + 1) for i in range(ctx...  5.2 us
    pallas_call x5, Pallas kernels, call(): pl.pallas_call(body, out_shape=shapes, in_specs=[pl.BlockSpec(memory_spac...  4.88 us
    ppermute x1, starting transfers between devices, per_device(): lax.ppermute(stream[count - RIM:], 'ctx', [(i, i + 1) for i in range(ctx...  3.52 us
  transfers between devices with their start and end apart: 3, of which 3 were waited for; matrix products, arithmetic and copies ran while one was open for 0% of the time, Pallas kernels for 2%

profile of v1, /device:TPU:2, one launch (start us, length us, event | category | flops | bytes accessed | tf_op | source)
XLA Modules:
  0.0 68.5 jit_solution(5417561755262152545)
XLA Ops:
  0.0 0.0 copy-start.2
  0.0 0.7 %slice.3 = bf16[16,512]{1,0:T(8,128)(2,1)S(1)} slice(bf16[128,512]{1,0:T(8,128)(2,1)} %refs_1_.1), slice={[112:128], [0:512]} | slice | bytes 32768 | tf_op jit(solution)/shard_map/slice | solution.py:197
  0.7 0.0 copy-start.3
  0.7 3.5 %collective-permute-start = (bf16[16,512]{1,0:T(8,128)(2,1)S(1)}, bf16[16,512]{1,0:T(8,128)(2,1)S(1)}, u32[]{:S(2)}, u32[]{:S(2)}) collective-permute-start(bf16[16,512]{1,0:T(8,128)(2,1)S(1)} %slice.3), channel_id=1, source_target_pairs={{0,8},{8,16},{16,24},{24,32},{32,40},{40,48},{48,56},{56,64},{64,7... | collective-permute-start | bytes 49160 | tf_op jit(solution)/shard_map/ppermute | solution.py:197
  4.3 0.0 copy-done.2
  4.3 0.1 copy.8.rate_ref
  4.4 0.0 copy-done.3
  4.4 0.0 copy-start
  4.4 0.1 copy.9.residue_ref
  4.5 5.2 %collective-permute-done.rim_ref.refs_2_ = bf16[16,512]{1,0:T(8,128)(2,1)S(1)} collective-permute-done((bf16[16,512]{1,0:T(8,128)(2,1)S(1)}, bf16[16,512]{1,0:T(8,128)(2,1)S(1)}, u32[]{:S(2)}, u32[]{:S(2)}) %collective-permute-start) | collective-permute-done | bytes 16416 | tf_op jit(solution)/shard_map/ppermute | solution.py:197
  9.8 0.0 copy-done
  9.8 0.3 shard_map.55
  10.1 0.0 copy-start.4
  10.1 0.6 copy.10
  10.7 3.3 %all-to-all-start = ((f32[8,1,256]{2,1,0:T(1,128)}), f32[8,1,256]{2,1,0:T(1,128)S(1)}, u32[]{:S(2)}, u32[]{:S(2)}) async-start(f32[8,1,256]{2,1,0:T(1,128)} %copy.10), calls=%async_computation | async-start | bytes 16384 | tf_op jit(solution)/shard_map/all_to_all | solution.py:185
  14.1 0.0 copy-done.4
  14.1 5.2 %all-to-all-done = f32[8,1,256]{2,1,0:T(1,128)S(1)} async-done(((f32[8,1,256]{2,1,0:T(1,128)}), f32[8,1,256]{2,1,0:T(1,128)S(1)}, u32[]{:S(2)}, u32[]{:S(2)}) %all-to-all-start) | async-done | bytes 8224 | tf_op jit(solution)/shard_map/all_to_all | solution.py:185
  19.3 0.0 copy-start.1
  19.3 0.7 copy-done.1
  20.0 1.1 %shard_map.56 = (bf16[128,512]{1,0:T(8,128)(2,1)S(1)}, f32[128,512]{1,0:T(8,128)S(1)}, f32[8,16,512]{2,1,0:T(8,128)S(1)}) custom-call(f32[8,256]{1,0:T(8,128)S(1)} %bitcast.5, bf16[128,512]{1,0:T(8,128)(2,1)S(1)} %copy-done, bf16[16,512]{1,0:T(8,128)(2,1)S(1)} %collective-permute-done.rim_ref.refs_2_, f32[1,512]{1,0:T(1,128)S(1)} %bitcast.7, ...), custom_call_target="tpu_custom_call" | custom-call | bytes 208896 | tf_op jit(solution)/shard_map/pallas_call | solution.py:22
  21.1 9.3 %all_to_all.21.refs_0_ = f32[8,16,512]{2,1,0:T(8,128)S(1)} all-to-all(f32[8,16,512]{2,1,0:T(8,128)S(1)} %get-tuple-element.15), channel_id=1, replica_groups={{0,8,16,24,32,40,48,56},{64,72,80,88,96,104,112,120},{128,136,144,152,1..., dimensions={0} | all-to-all | bytes 524288 | tf_op jit(solution)/shard_map/all_to_all | solution.py:185
  30.4 0.8 %shard_map.57 = (f32[16,512]{1,0:T(8,128)S(1)}, f32[8,16,512]{2,1,0:T(8,128)}) custom-call(f32[8,16,512]{2,1,0:T(8,128)S(1)} %all_to_all.21.refs_0_, f32[16,512]{1,0:T(8,128)S(1)} %get-tuple-element.14.refs_5_.refs_1_.rate_ref.refs_2_), custom_call_target="tpu_custom_call" | custom-call | bytes 294912 | tf_op jit(solution)/shard_map/pallas_call | solution.py:22
  31.2 15.6 %all-to-all-start.2 = ((f32[8,16,512]{2,1,0:T(8,128)}), f32[8,16,512]{2,1,0:T(8,128)S(1)}, u32[]{:S(2)}, u32[]{:S(2)}) async-start(f32[8,16,512]{2,1,0:T(8,128)} %get-tuple-element.16), calls=%async_computation.2 | async-start | bytes 524288 | tf_op jit(solution)/shard_map/all_to_all | solution.py:185
  46.8 1.6 %shard_map.58.refs_4_ = f32[128,512]{1,0:T(8,128)S(1)} custom-call(f32[16,512]{1,0:T(8,128)S(1)} %get-tuple-element.14.refs_5_.refs_1_.rate_ref.refs_2_, f32[16,512]{1,0:T(8,128)S(1)} %get-tuple-element.18.residue_ref.refs_3_, f32[128,512]{1,0:T(8,128)S(1)} %get-tuple-element.19.product_ref), custom_call_target="tpu_custom_call" | custom-call | flops 10000000 | bytes 327680 | tf_op jit(solution)/shard_map/pallas_call | solution.py:22
  48.4 19.0 %all-to-all-done.2.refs_0_ = f32[8,16,512]{2,1,0:T(8,128)S(1)} async-done(((f32[8,16,512]{2,1,0:T(8,128)}), f32[8,16,512]{2,1,0:T(8,128)S(1)}, u32[]{:S(2)}, u32[]{:S(2)}) %all-to-all-start.2) | async-done | bytes 262176 | tf_op jit(solution)/shard_map/all_to_all | solution.py:185
  67.4 1.1 %shard_map.59 = bf16[128,512]{1,0:T(8,128)(2,1)} custom-call(f32[8,16,512]{2,1,0:T(8,128)S(1)} %all-to-all-done.2.refs_0_, f32[16,512]{1,0:T(8,128)S(1)} %get-tuple-element.17.refs_1_, f32[16,512]{1,0:T(8,128)S(1)} %get-tuple-element.14.refs_5_.refs_1_.rate_ref.refs_2_, f32[16,512]{1,0:T(8,128)S(1)} %get-tuple-element.18.residue_ref.refs_3_, ...), custom_call_target="tpu_custom_call" | custom-call | bytes 753664 | tf_op jit(solution)/shard_map/pallas_call | solution.py:22
  (2 shorter events, 0.0 us)
Async XLA Ops:
  0.0 4.3 %copy-start.2 = (f32[512,16]{0,1:T(8,128)S(1)}, f32[512,16]{0,1:T(8,128)}, u32[]{:S(2)}) copy-start(f32[512,16]{0,1:T(8,128)} %param.8) | copy-start | bytes 98308
  0.7 3.7 %copy-start.3 = (f32[512,16]{0,1:T(8,128)S(1)}, f32[512,16]{0,1:T(8,128)}, u32[]{:S(2)}) copy-start(f32[512,16]{0,1:T(8,128)} %param.9) | copy-start | bytes 98308
  0.7 9.0 %collective-permute-start = (bf16[16,512]{1,0:T(8,128)(2,1)S(1)}, bf16[16,512]{1,0:T(8,128)(2,1)S(1)}, u32[]{:S(2)}, u32[]{:S(2)}) collective-permute-start(bf16[16,512]{1,0:T(8,128)(2,1)S(1)} %slice.3), channel_id=1, source_target_pairs={{0,8},{8,16},{16,24},{24,32},{32,40},{40,48},{48,56},{56,64},{64,7... | collective-permute-start | bytes 49160 | tf_op jit(solution)/shard_map/ppermute | solution.py:197
  4.4 5.3 %copy-start = (bf16[128,512]{1,0:T(8,128)(2,1)S(1)}, bf16[128,512]{1,0:T(8,128)(2,1)}, u32[]{:S(2)}) copy-start(bf16[128,512]{1,0:T(8,128)(2,1)} %refs_1_.1) | copy-start | bytes 393220
  10.1 4.0 %copy-start.4 = (f32[3,3,512]{2,1,0:T(4,128)S(1)}, f32[3,3,512]{2,1,0:T(4,128)}, u32[]{:S(2)}) copy-start(f32[3,3,512]{2,1,0:T(4,128)} %param.7) | copy-start | bytes 55300
  10.7 8.6 %all-to-all-start = ((f32[8,1,256]{2,1,0:T(1,128)}), f32[8,1,256]{2,1,0:T(1,128)S(1)}, u32[]{:S(2)}, u32[]{:S(2)}) async-start(f32[8,1,256]{2,1,0:T(1,128)} %copy.10), calls=%async_computation | async-start | bytes 16384 | tf_op jit(solution)/shard_map/all_to_all | solution.py:185
  19.3 0.7 copy-start.1
  31.2 36.2 %all-to-all-start.2 = ((f32[8,16,512]{2,1,0:T(8,128)}), f32[8,16,512]{2,1,0:T(8,128)S(1)}, u32[]{:S(2)}, u32[]{:S(2)}) async-start(f32[8,16,512]{2,1,0:T(8,128)} %get-tuple-element.16), calls=%async_computation.2 | async-start | bytes 524288 | tf_op jit(solution)/shard_map/all_to_all | solution.py:185

commit v2 on v1

--- a/solution.py
+++ b/solution.py
@@ -30,9 +30,12 @@
     )(*args)
 
 
-def square_sums(stream_ref, rim_ref, rate_ref, residue_ref, sums_ref, rate_out, residue_out):
+def square_sums(stream_ref, rim_ref, *refs):
+    sums_ref, held = refs[len(refs) // 2], refs[: len(refs) // 2]
+    for ref, out in zip(held, refs[len(refs) // 2 + 1 :]):
+        out[...] = ref[...]
     peers = sums_ref.shape[0]
-    ones = jnp.ones((peers, stream_ref.shape[1]), F32)
+    ones = jnp.ones((SUB, stream_ref.shape[1]), F32)
     contract = (((1,), (1,)), ((), ()))
 
     def rows(ref):
@@ -41,25 +44,29 @@
 
     count = stream_ref.shape[0]
     sums_ref[...] = jnp.zeros_like(sums_ref)
-    sums_ref[:, :count] = rows(stream_ref)
-    sums_ref[:, count : count + RIM] = rows(rim_ref)
-    rate_out[...] = rate_ref[...].T
-    residue_out[...] = residue_ref[...].T
+    own, before = rows(stream_ref), rows(rim_ref)
+    for peer in range(peers):
+        sums_ref[peer, :, :count] = own[:1]
+        sums_ref[peer, :, count : count + RIM] = before[:1]
 
 
 def block_states(chan_total, sums_ref, stream_ref, rim_ref, gain_ref, taps_ref, rate_ref, query_ref, product_ref, states_ref, normed_ref):
     count, chans = stream_ref.shape
     peers = states_ref.shape[0]
     modes = rate_ref.shape[0]
-    ones = jnp.ones((sums_ref.shape[0], chans), F32)
+    ones = jnp.ones((SUB, chans), F32) / SUB
+    sums_all = sums_ref[0]
+    for peer in range(1, sums_ref.shape[0]):
+        sums_all = sums_all + sums_ref[peer]
+    sums_all = jnp.broadcast_to(sums_all, (SUB, sums_all.shape[1]))
 
     def normalize(ref, sums):
         mean_square = lax.dot_general(sums, ones, (((0,), (0,)), ((), ())), precision=EXACT, preferred_element_type=F32) / chan_total
         values = ref[...].astype(F32) * lax.rsqrt(mean_square + EPSILON) * gain_ref[...]
         return values.astype(BF16).astype(F32)
 
-    normed_ref[:RIM] = normalize(rim_ref, sums_ref[:, count : count + RIM])
-    normed_ref[RIM:] = normalize(stream_ref, sums_ref[:, :count])
+    normed_ref[:RIM] = normalize(rim_ref, sums_all[:, count : count + RIM])
+    normed_ref[RIM:] = normalize(stream_ref, sums_all[:, :count])
     shifted = [normed_ref[RIM - j : RIM - j + count] for j in range(3)]
 
     def feature(role):
@@ -134,7 +141,7 @@
     lax.fori_loop(0, chans // LANES, one_lane, 0)
 
 
-def near_scan(block, got_ref, rate_ref, before_ref, totals_ref):
+def near_scan(block, got_ref, rate_ref, residue_ref, product_ref, before_ref, totals_ref, local_ref, filter_ref):
     place = lax.axis_index("ctx") % NEAR
     step = jnp.exp(-block * rate_ref[...])
     total = jnp.zeros_like(step)
@@ -145,6 +152,7 @@
     before_ref[...] = before
     for peer in range(totals_ref.shape[0]):
         totals_ref[peer] = total
+    inner_conv(rate_ref, residue_ref, product_ref, local_ref, filter_ref)
 
 
 def outer_conv(block, far, got_ref, before_ref, rate_ref, residue_ref, local_ref, query_ref, mixed_ref, state_ref):
@@ -195,27 +203,23 @@
     far_groups = [[g * NEAR + m for g in range(far)] for m in range(NEAR)]
 
     rim = lax.ppermute(stream[count - RIM :], "ctx", [(i, i + 1) for i in range(ctx - 1)])
-    sums, rates, weights = call(
-        square_sums,
-        [((peers, 2 * LANES), F32), ((modes, chans), F32), ((modes, chans), F32)],
-        stream, rim, decay_rate, residue,
+    params = [norm_gain[None, :], short_filter.reshape(9, chans), decay_rate.T, residue.T]
+    sums, gain, taps, rates, weights = call(
+        square_sums, [((peers, 1, 2 * LANES), F32)] + [(p.shape, F32) for p in params], stream, rim, *params
     )
     sums = gather(sums, "ch")
     query, product, states = call(
         lambda *refs: block_states(chans * peers, *refs),
         [((count, chans), BF16), ((count, chans), F32), ((NEAR, modes, chans), F32)],
-        sums, stream, rim, norm_gain[None, :], short_filter.reshape(9, chans), rates,
+        sums, stream, rim, gain, taps, rates,
         scratch=[pltpu.VMEM((RIM + count, chans), F32)],
     )
     states = gather(states, "ctx", near_groups)
-    (local,) = call(
-        inner_conv, [((count, chans), F32)], rates, weights, product,
+    before, totals, local = call(
+        lambda *refs: near_scan(count, *refs),
+        [((modes, chans), F32), ((far, modes, chans), F32), ((count, chans), F32)],
+        states, rates, weights, product,
         scratch=[pltpu.VMEM((count, LANES), F32)], flops=10**7,
-    )
-    before, totals = call(
-        lambda *refs: near_scan(count, *refs),
-        [((modes, chans), F32), ((far, modes, chans), F32)],
-        states, rates,
     )
     totals = gather(totals, "ctx", far_groups)
     (mixed,) = call(

time: 69 us -> 69.7 us (1.010)
  blocking collectives: 9.34 us -> 53.8 us
  waiting for transfers between devices: 29.4 us -> 5.46 us
  starting transfers between devices: 22.5 us -> 3.52 us
  Pallas kernels: 4.88 us -> 4.16 us
    all_to_all x1 -> x3, blocking collectives: 9.34 us -> 53.8 us  [gather(): lax.all_to_all(copies, axis, 0, 0, tiled=True, axis_index_groups=groups)]
    all_to_all x2 -> x0, waiting for transfers between devices: 24.2 us -> none  [gather(): lax.all_to_all(copies, axis, 0, 0, tiled=True, axis_index_groups=groups)]
    all_to_all x2 -> x0, starting transfers between devices: 19 us -> none  [gather(): lax.all_to_all(copies, axis, 0, 0, tiled=True, axis_index_groups=groups)]
    pallas_call x5 -> x4, Pallas kernels: 4.88 us -> 4.16 us  [call(): pl.pallas_call(body, out_shape=shapes, in_specs=[pl.BlockSpec(memory_spac...]
    unnamed x13 -> x10, local copies, waits for them, and re-layouts: 0.94 us -> 1.59 us
  transfers between devices with their start and end apart: 3 -> 1, of which waited for: 3 -> 1; matrix products, arithmetic and copies ran while one was open for 0% -> 0% of each run, Pallas kernels for 2% -> 0%
where the time goes in v2:
time: 69.7 us; the launch traced here: 69.3 us
  blocking collectives  53.8 us (77%)
  waiting for transfers between devices  5.46 us (8%)
  Pallas kernels  4.16 us (6%)
  starting transfers between devices  3.52 us (5%)
  local copies, waits for them, and re-layouts  2.33 us (3%)
    all_to_all x3, blocking collectives, gather(): lax.all_to_all(copies, axis, 0, 0, tiled=True, axis_index_groups=groups)  53.8 us
    ppermute x1, waiting for transfers between devices, per_device(): lax.ppermute(stream[count - RIM:], 'ctx', [(i, i + 1) for i in range(ctx...  5.46 us
    pallas_call x4, Pallas kernels, call(): pl.pallas_call(body, out_shape=shapes, in_specs=[pl.BlockSpec(memory_spac...  4.16 us
    ppermute x1, starting transfers between devices, per_device(): lax.ppermute(stream[count - RIM:], 'ctx', [(i, i + 1) for i in range(ctx...  3.52 us
    unnamed x10, local copies, waits for them, and re-layouts  1.59 us
  transfers between devices with their start and end apart: 1, of which 1 were waited for; matrix products, arithmetic and copies ran while one was open for 0% of the time, Pallas kernels for 0%

profile of v2, /device:TPU:2, one launch (start us, length us, event | category | flops | bytes accessed | tf_op | source)
XLA Modules:
  0.0 69.3 jit_solution(4930967059747088345)
XLA Ops:
  0.0 0.0 copy-start.4
  0.0 0.0 copy-start.2
  0.0 0.7 %slice.3 = bf16[16,512]{1,0:T(8,128)(2,1)S(1)} slice(bf16[128,512]{1,0:T(8,128)(2,1)} %refs_1_.1), slice={[112:128], [0:512]} | slice | bytes 32768 | tf_op jit(solution)/shard_map/slice | solution.py:205
  0.7 0.0 copy-start.1
  0.7 3.5 %collective-permute-start = (bf16[16,512]{1,0:T(8,128)(2,1)S(1)}, bf16[16,512]{1,0:T(8,128)(2,1)S(1)}, u32[]{:S(2)}, u32[]{:S(2)}) collective-permute-start(bf16[16,512]{1,0:T(8,128)(2,1)S(1)} %slice.3), channel_id=1, source_target_pairs={{0,8},{8,16},{16,24},{24,32},{32,40},{40,48},{48,56},{56,64},{64,7... | collective-permute-start | bytes 49160 | tf_op jit(solution)/shard_map/ppermute | solution.py:205
  4.3 0.0 copy-done.4
  4.3 5.5 %collective-permute-done.rim_ref.refs_2_ = bf16[16,512]{1,0:T(8,128)(2,1)S(1)} collective-permute-done((bf16[16,512]{1,0:T(8,128)(2,1)S(1)}, bf16[16,512]{1,0:T(8,128)(2,1)S(1)}, u32[]{:S(2)}, u32[]{:S(2)}) %collective-permute-start) | collective-permute-done | bytes 16416 | tf_op jit(solution)/shard_map/ppermute | solution.py:205
  9.8 0.0 copy-start.3
  9.8 0.0 copy-done.2
  9.8 0.0 copy-done.1
  9.8 0.7 copy-done.3
  10.4 0.0 copy-start
  10.4 0.9 %copy-done = bf16[128,512]{1,0:T(8,128)(2,1)S(1)} copy-done((bf16[128,512]{1,0:T(8,128)(2,1)S(1)}, bf16[128,512]{1,0:T(8,128)(2,1)}, u32[]{:S(2)}) %copy-start) | copy-done | bytes 131096
  11.3 0.3 shard_map.55
  11.7 7.7 %all_to_all.15.refs_0_ = f32[8,1,256]{2,1,0:T(1,128)S(1)} all-to-all(f32[8,1,256]{2,1,0:T(1,128)S(1)} %get-tuple-element.16), channel_id=1, replica_groups=mesh['ctx'=64,'ch'=8] {'ch'}, dimensions={0} | all-to-all | bytes 16384 | tf_op jit(solution)/shard_map/all_to_all | solution.py:193
  19.4 1.1 %shard_map.56 = (bf16[128,512]{1,0:T(8,128)(2,1)S(1)}, f32[128,512]{1,0:T(8,128)S(1)}, f32[8,16,512]{2,1,0:T(8,128)S(1)}) custom-call(f32[8,1,256]{2,1,0:T(1,128)S(1)} %all_to_all.15.refs_0_, bf16[128,512]{1,0:T(8,128)(2,1)S(1)} %copy-done, bf16[16,512]{1,0:T(8,128)(2,1)S(1)} %collective-permute-done.rim_ref.refs_2_, ...), custom_call_target="tpu_custom_call" | custom-call | bytes 208896 | tf_op jit(solution)/shard_map/pallas_call | solution.py:22
  20.5 10.0 %all_to_all.16.refs_0_ = f32[8,16,512]{2,1,0:T(8,128)S(1)} all-to-all(f32[8,16,512]{2,1,0:T(8,128)S(1)} %get-tuple-element.20), channel_id=1, replica_groups={{0,8,16,24,32,40,48,56},{64,72,80,88,96,104,112,120},{128,136,144,152,1..., dimensions={0} | all-to-all | bytes 524288 | tf_op jit(solution)/shard_map/all_to_all | solution.py:193
  30.5 1.7 %shard_map.57 = (f32[16,512]{1,0:T(8,128)S(1)}, f32[8,16,512]{2,1,0:T(8,128)S(1)}, f32[128,512]{1,0:T(8,128)S(1)}) custom-call(f32[8,16,512]{2,1,0:T(8,128)S(1)} %all_to_all.16.refs_0_, f32[16,512]{1,0:T(8,128)S(1)} %get-tuple-element.19.refs_5_.refs_1_.refs_2_, f32[16,512]{1,0:T(8,128)S(1)} %get-tuple-element.21.refs_2_.refs_3_, ...), custom_call_target="tpu_custom_call" | custom-call | flops 10000000 | bytes 589824 | tf_op jit(solution)/shard_map/pallas_call | solution.py:22
  32.2 36.0 %all_to_all.17.refs_0_ = f32[8,16,512]{2,1,0:T(8,128)S(1)} all-to-all(f32[8,16,512]{2,1,0:T(8,128)S(1)} %get-tuple-element.23), channel_id=1, replica_groups={{0,64,128,192,256,320,384,448},{8,72,136,200,264,328,392,456},{16,80,14..., dimensions={0} | all-to-all | bytes 524288 | tf_op jit(solution)/shard_map/all_to_all | solution.py:193
  68.2 1.1 %shard_map.58 = bf16[128,512]{1,0:T(8,128)(2,1)} custom-call(f32[8,16,512]{2,1,0:T(8,128)S(1)} %all_to_all.17.refs_0_, f32[16,512]{1,0:T(8,128)S(1)} %get-tuple-element.24.refs_1_, f32[16,512]{1,0:T(8,128)S(1)} %get-tuple-element.19.refs_5_.refs_1_.refs_2_, f32[16,512]{1,0:T(8,128)S(1)} %get-tuple-element.21.refs_2_.refs_3_, ...), custom_call_target="tpu_custom_call" | custom-call | bytes 753664 | tf_op jit(solution)/shard_map/pallas_call | solution.py:22
  (1 shorter events, 0.0 us)
Async XLA Ops:
  0.0 4.3 %copy-start.4 = (f32[3,3,512]{2,1,0:T(4,128)S(1)}, f32[3,3,512]{2,1,0:T(4,128)}, u32[]{:S(2)}) copy-start(f32[3,3,512]{2,1,0:T(4,128)} %param.7) | copy-start | bytes 55300
  0.0 9.8 %copy-start.2 = (f32[512,16]{0,1:T(8,128)S(1)}, f32[512,16]{0,1:T(8,128)}, u32[]{:S(2)}) copy-start(f32[512,16]{0,1:T(8,128)} %param.9) | copy-start | bytes 98308
  0.7 9.0 %copy-start.1 = (f32[512,16]{0,1:T(8,128)S(1)}, f32[512,16]{0,1:T(8,128)}, u32[]{:S(2)}) copy-start(f32[512,16]{0,1:T(8,128)} %param.8) | copy-start | bytes 98308
  0.7 9.0 %collective-permute-start = (bf16[16,512]{1,0:T(8,128)(2,1)S(1)}, bf16[16,512]{1,0:T(8,128)(2,1)S(1)}, u32[]{:S(2)}, u32[]{:S(2)}) collective-permute-start(bf16[16,512]{1,0:T(8,128)(2,1)S(1)} %slice.3), channel_id=1, source_target_pairs={{0,8},{8,16},{16,24},{24,32},{32,40},{40,48},{48,56},{56,64},{64,7... | collective-permute-start | bytes 49160 | tf_op jit(solution)/shard_map/ppermute | solution.py:205
  9.8 0.7 copy-start.3
  10.4 0.9 %copy-start = (bf16[128,512]{1,0:T(8,128)(2,1)S(1)}, bf16[128,512]{1,0:T(8,128)(2,1)}, u32[]{:S(2)}) copy-start(bf16[128,512]{1,0:T(8,128)(2,1)} %refs_1_.1) | copy-start | bytes 393220

commit v3 on v2

v3 whole, which is shorter than its diff:
```python
import jax
import jax.numpy as jnp
from jax import lax
from jax.experimental import pallas as pl
from jax.experimental.pallas import tpu as pltpu
from jax.sharding import PartitionSpec as P

EXACT = lax.Precision.HIGHEST
EPSILON = 1e-05
SUB = 8
LANES = 128
NEAR = 16

F32 = jnp.float32
BF16 = jnp.bfloat16


def call(body, outs, *args, scratch=(), flops=0):
    shapes = [jax.ShapeDtypeStruct(s, d) for s, d in outs]
    moved = sum(a.size * a.dtype.itemsize for a in args)
    return pl.pallas_call(
        body,
        out_shape=shapes,
        in_specs=[pl.BlockSpec(memory_space=pltpu.VMEM)] * len(args),
        out_specs=[pl.BlockSpec(memory_space=pltpu.VMEM)] * len(shapes),
        scratch_shapes=list(scratch),
        compiler_params=pltpu.CompilerParams(vmem_limit_bytes=16 * 2**20),
        cost_estimate=pl.CostEstimate(flops=flops, bytes_accessed=moved, transcendentals=0),
    )(*args)


def pack(ref):
    return jnp.concatenate([ref[:, l * LANES : (l + 1) * LANES] for l in range(ref.shape[1] // LANES)], axis=0)


def square_sums(stream_ref, gain_ref, taps_ref, rate_ref, residue_ref, sums_ref, gain_out, taps_out, rate_out, residue_out, taps_pack, rate_pack, residue_pack):
    chans = stream_ref.shape[1]
    values = stream_ref[...].astype(F32)
    sums = lax.dot_general(
        jnp.ones((SUB, chans), F32), values * values, (((1,), (1,)), ((), ())), precision=EXACT, preferred_element_type=F32
    )
    for peer in range(sums_ref.shape[0]):
        sums_ref[peer] = sums[:1]
    gain_out[...] = gain_ref[...]
    taps_out[...] = taps_ref[...]
    rate_out[...] = rate_ref[...]
    residue_out[...] = residue_ref[...]
    rate_pack[...] = pack(rate_ref)
    residue_pack[...] = pack(residue_ref)
    lanes = chans // LANES
    for k in range(taps_ref.shape[0]):
        for l in range(lanes):
            taps_pack[pl.ds(k * lanes + l, 1), :] = taps_ref[pl.ds(k, 1), pl.ds(l * LANES, LANES)]


def block_states(chan_total, sums_ref, stream_ref, gain_ref, taps_ref, rate_ref, query_ref, product_ref, message_ref, normed_ref, end_ref):
    count, chans = stream_ref.shape
    lanes = chans // LANES
    modes = rate_ref.shape[0]
    sums = sums_ref[0]
    for peer in range(1, sums_ref.shape[0]):
        sums = sums + sums_ref[peer]
    sums = jnp.broadcast_to(sums, (SUB, count))
    mean_square = lax.dot_general(
        sums, jnp.ones((SUB, chans), F32) / SUB, (((0,), (0,)), ((), ())), precision=EXACT, preferred_element_type=F32
    ) / chan_total
    values = stream_ref[...].astype(F32) * lax.rsqrt(mean_square + EPSILON) * gain_ref[...]
    normed_ref[:SUB] = jnp.zeros((SUB, chans), F32)
    normed_ref[SUB:] = values.astype(BF16).astype(F32)
    shifted = [normed_ref[SUB - j : SUB - j + count] for j in range(3)]

    def feature(role):
        total = taps_ref[pl.ds(role, 1)] * shifted[0]
        total = total + taps_ref[pl.ds(3 + role, 1)] * shifted[1]
        return total + taps_ref[pl.ds(6 + role, 1)] * shifted[2]

    query_ref[...] = feature(0).astype(BF16)
    product_ref[...] = (feature(1) * feature(2)).astype(BF16).astype(F32)
    row = lax.broadcasted_iota(jnp.int32, (SUB, chans), 0)
    product_ref[:SUB] = jnp.where(row < 2, 0.0, product_ref[:SUB])

    lag = (SUB - 1 - lax.broadcasted_iota(jnp.int32, (SUB, LANES), 0)).astype(F32)

    def one_lane(lane, carry):
        at = pl.ds(pl.multiple_of(lane * LANES, LANES), LANES)
        blocks = [product_ref[pl.ds(i * SUB, SUB), at] for i in range(count // SUB)]
        for mode in range(modes):
            rate = rate_ref[pl.ds(mode, 1), at]
            step = jnp.broadcast_to(jnp.exp(-SUB * rate), (SUB, LANES))
            total = blocks[0]
            for block in blocks[1:]:
                total = total * step + block
            end_ref[pl.ds(mode, 1), at] = jnp.sum(total * jnp.exp(-rate * lag), axis=0, keepdims=True)
        return carry

    lax.fori_loop(0, lanes, one_lane, 0)
    message_ref[0, : lanes * modes] = pack(end_ref)
    for e, place in enumerate((0, 1, count - 2, count - 1)):
        for l in range(lanes):
            message_ref[0, pl.ds(lanes * (modes + e) + l, 1), :] = normed_ref[pl.ds(SUB + place, 1), pl.ds(l * LANES, LANES)]
    message = message_ref[0]
    for peer in range(1, message_ref.shape[0]):
        message_ref[peer] = message


def first_rows(taps_ref, role, last, head):
    lanes = taps_ref.shape[0] // 9
    taps = [taps_ref[pl.ds((3 * j + role) * lanes, lanes)] for j in range(3)]
    first = taps[0] * head[0] + taps[1] * last[1] + taps[2] * last[0]
    second = taps[0] * head[1] + taps[1] * head[0] + taps[2] * last[1]
    return first, second


def first_products(taps_ref, last, head):
    keys, values = first_rows(taps_ref, 1, last, head), first_rows(taps_ref, 2, last, head)
    return [(k * v).astype(BF16).astype(F32) for k, v in zip(keys, values)]


def spread(rows, modes):
    return jnp.concatenate([jnp.broadcast_to(rows[l : l + 1], (modes, LANES)) for l in range(rows.shape[0])], axis=0)


def pairs(ref, start, lanes):
    return ref[pl.ds(start, lanes), :], ref[pl.ds(start + lanes, lanes), :]


def near_scan(block, lanes, got_ref, rate_ref, taps_ref, before_ref, total_ref, message_ref):
    place = lax.axis_index("ctx") % NEAR
    states = rate_ref.shape[0]
    modes = states // lanes
    rates = rate_ref[...]
    step, late, later = jnp.exp(-block * rates), jnp.exp(-(block - 1) * rates), jnp.exp(-(block - 2) * rates)
    total = got_ref[0, :states]
    before = jnp.where(place == 1, total, jnp.zeros_like(total))
    for j in range(1, NEAR):
        last = pairs(got_ref.at[j - 1], states + 2 * lanes, lanes)
        head = pairs(got_ref.at[j], states, lanes)
        first, second = first_products(taps_ref, last, head)
        total = total * step + got_ref[j, :states] + late * spread(first, modes) + later * spread(second, modes)
        if j < NEAR - 1:
            before = jnp.where(place == j + 1, total, before)
    before_ref[...] = before
    total_ref[...] = total
    send(block, lanes, None, total, got_ref, rates, taps_ref, message_ref)


def send(block, lanes, came_ref, total, got_ref, rates, taps_ref, message_ref):
    states = rates.shape[0]
    modes = states // lanes
    head = pairs(got_ref.at[0], states, lanes)
    if came_ref is None:
        last = [jnp.zeros((lanes, LANES), F32)] * 2
    else:
        last = pairs(came_ref, states, lanes)
        total = total + came_ref[:states] * jnp.exp(-(block * NEAR) * rates)
    first, second = first_products(taps_ref, last, head)
    total = total + jnp.exp(-(block * NEAR - 1) * rates) * spread(first, modes)
    total = total + jnp.exp(-(block * NEAR - 2) * rates) * spread(second, modes)
    message_ref[:states] = total
    message_ref[states:] = got_ref[NEAR - 1, states + 2 * lanes :]


def chain_step(block, lanes, came_ref, total_ref, got_ref, rate_ref, taps_ref, message_ref):
    send(block, lanes, came_ref, total_ref[...], got_ref, rate_ref[...], taps_ref, message_ref)


def add_mode(totals, term, rate):
    step = jnp.broadcast_to(jnp.exp(-SUB * rate), term.shape)
    out = []
    for total in totals:
        out.append(total + term)
        term = term * step
    return out


def inner_conv(rate_ref, residue_ref, product_ref, after_ref, local_ref, filter_ref):
    count, chans = product_ref.shape
    modes = rate_ref.shape[0]
    blocks = count // SUB
    row = lax.broadcasted_iota(jnp.int32, (SUB, LANES), 0)
    lead = row.astype(F32)

    def one_lane(lane, carry):
        at = pl.ds(pl.multiple_of(lane * LANES, LANES), LANES)
        zero = jnp.zeros((SUB, LANES), F32)
        totals = [zero] * blocks
        for mode in range(modes):
            rate = rate_ref[pl.ds(mode, 1), at]
            term = residue_ref[pl.ds(mode, 1), at] * jnp.exp(-rate * lead)
            totals = add_mode(totals, term, rate)
        for i in range(blocks):
            filter_ref[pl.ds(i * SUB, SUB), :] = totals[i]

        shifted = [product_ref[pl.ds(i * SUB, SUB), at] for i in range(blocks)]
        totals = [zero] * blocks
        for b in range(SUB):
            for a in range(blocks):
                weight = filter_ref[pl.ds(a * SUB + b, 1), :]
                for j in range(blocks - a):
                    totals[j + a] = totals[j + a] + weight * shifted[j]
            if b < SUB - 1:
                rolled = [pltpu.roll(s, 1, 0) for s in shifted]
                shifted = [jnp.where(row == 0, before, now) for before, now in zip([zero] + rolled[:-1], rolled)]
        for i in range(blocks):
            local_ref[pl.ds(i * SUB, SUB), at] = totals[i]
        return carry

    lax.fori_loop(0, chans // LANES, one_lane, 0)


def outer_conv(steps, got_ref, *refs):
    came_refs, refs = refs[:steps], refs[steps:]
    before_ref, rate_pack, residue_pack, taps_ref, rate_ref, local_ref, query_ref, mixed_ref, state_ref = refs
    count, chans = local_ref.shape
    lanes = chans // LANES
    modes = rate_ref.shape[0]
    states = lanes * modes
    blocks = count // SUB
    place = lax.axis_index("ctx") % NEAR
    rates = rate_pack[...]
    came = came_refs[0][...]
    for ref in came_refs[1:]:
        came = came + ref[...]
    group_last = (came[states : states + lanes], came[states + lanes :])
    first, second = first_products(taps_ref, group_last, pairs(got_ref.at[0], states, lanes))
    lag = (count * place).astype(F32)
    lead = jnp.exp(-rates * lag)
    state = before_ref[...] + came[:states] * lead
    held = jnp.exp(-rates * jnp.maximum(lag - 1.0, 0.0)) * spread(first, modes)
    held = held + jnp.exp(-rates * jnp.maximum(lag - 2.0, 0.0)) * spread(second, modes)
    state = state + jnp.where(place > 0, held, 0.0)

    own_last = pairs(got_ref.at[jnp.maximum(place - 1, 0)], states + 2 * lanes, lanes)
    own_last = [jnp.where(place > 0, own, group) for own, group in zip(own_last, group_last)]
    own_head = pairs(got_ref.at[place], states, lanes)
    own_query = [q.astype(BF16).astype(F32) for q in first_rows(taps_ref, 0, own_last, own_head)]
    first, second = first_products(taps_ref, own_last, own_head)
    ahead = jnp.exp(rates) * spread(second, modes)
    state = state * jnp.exp(-rates) + spread(first, modes) + ahead
    state = state * residue_pack[...]
    ahead = ahead * residue_pack[...]
    extra = [jnp.sum(ahead[l * modes : (l + 1) * modes], axis=0, keepdims=True) for l in range(lanes)]
    row = lax.broadcasted_iota(jnp.int32, (SUB, LANES), 0)
    lead = row.astype(F32)
    for l in range(lanes):
        state_ref[:modes, pl.ds(l * LANES, LANES)] = state[l * modes : (l + 1) * modes]
        take = jnp.where(row == 0, jnp.broadcast_to(extra[l], row.shape), 0.0)
        query = jnp.where(row == 0, own_query[0][l : l + 1], jnp.where(row == 1, own_query[1][l : l + 1], 0.0))
        state_ref[modes : modes + SUB, pl.ds(l * LANES, LANES)] = take
        state_ref[modes + SUB :, pl.ds(l * LANES, LANES)] = query
    rows = lax.broadcasted_iota(jnp.int32, (2 * SUB, LANES), 0)

    def one_lane(lane, carry):
        at = pl.ds(pl.multiple_of(lane * LANES, LANES), LANES)
        totals = [local_ref[pl.ds(i * SUB, SUB), at] for i in range(blocks)]
        for mode in range(modes):
            rate = rate_ref[pl.ds(mode, 1), at]
            term = state_ref[pl.ds(mode, 1), at] * jnp.exp(-rate * lead)
            totals = add_mode(totals, term, rate)
        totals[0] = totals[0] - state_ref[pl.ds(modes, SUB), at]
        for i in range(0, blocks, 2):
            where = pl.ds(i * SUB, 2 * SUB)
            conv = jnp.concatenate(totals[i : i + 2], axis=0).astype(BF16).astype(F32)
            query = query_ref[where, at].astype(F32)
            if i == 0:
                fixed = state_ref[pl.ds(modes + SUB, SUB), at]
                query = jnp.where(rows < 2, jnp.concatenate([fixed, fixed], axis=0), query)
            mixed_ref[where, at] = (query * conv).astype(BF16)
        return carry

    lax.fori_loop(0, lanes, one_lane, 0)


def gather(copies, axis, groups=None):
    return lax.all_to_all(copies, axis, 0, 0, tiled=True, axis_index_groups=groups)


def per_device(stream, norm_gain, short_filter, decay_rate, residue):
    count, chans = stream.shape
    modes = decay_rate.shape[1]
    lanes = chans // LANES
    states = lanes * modes
    peers = lax.axis_size("ch")
    groups = lax.axis_size("ctx") // NEAR
    members = [[g * NEAR + m for m in range(NEAR)] for g in range(groups)]

    params = [norm_gain[None, :], short_filter.reshape(9, chans), decay_rate.T, residue.T]
    packed = [((9 * lanes, LANES), F32), ((states, LANES), F32), ((states, LANES), F32)]
    sums, gain, taps, rates, weights, taps_pack, rate_pack, residue_pack = call(
        square_sums, [((peers, 1, count), F32)] + [(p.shape, F32) for p in params] + packed, stream, *params
    )
    sums = gather(sums, "ch")
    query, product, message = call(
        lambda *refs: block_states(chans * peers, *refs),
        [((count, chans), BF16), ((count, chans), F32), ((NEAR, states + 4 * lanes, LANES), F32)],
        sums, stream, gain, taps, rates,
        scratch=[pltpu.VMEM((SUB + count, chans), F32), pltpu.VMEM((modes, chans), F32)],
    )
    got = gather(message, "ctx", members)
    carried = ((states + 2 * lanes, LANES), F32)
    before, total, message = call(
        lambda *refs: near_scan(count, lanes, *refs),
        [((states, LANES), F32), ((states, LANES), F32), carried],
        got, rate_pack, taps_pack,
    )
    came = []
    for g in range(1, groups):
        if g > 1:
            (message,) = call(
                lambda *refs: chain_step(count, lanes, *refs), [carried], came[-1], total, got, rate_pack, taps_pack
            )
        came.append(lax.ppermute(message, "ctx", [(a, b) for a, b in zip(members[g - 1], members[g])]))
        if g == 1:
            (local,) = call(
                inner_conv, [((count, chans), F32)], rates, weights, product, before,
                scratch=[pltpu.VMEM((count, LANES), F32)], flops=10**7,
            )
    (mixed,) = call(
        lambda *refs: outer_conv(len(came), *refs),
        [((count, chans), BF16)],
        got, *came, before, rate_pack, residue_pack, taps_pack, rates, local, query,
        scratch=[pltpu.VMEM((modes + 2 * SUB, chans), F32)],
    )
    return mixed


def solution(mesh):
    in_specs = (P("ctx", "ch"), P("ch"), P(None, None, "ch"), P("ch", None), P("ch", None))
    out_specs = P("ctx", "ch")
    return jax.shard_map(
        per_device, mesh=mesh, in_specs=in_specs, out_specs=out_specs, check_vma=False
    )
```

time: 69.7 us -> 61.7 us (0.89)
  the two profiles are of different devices: /device:TPU:2 before, /device:TPU:384 now
where the time goes in v3:
time: 61.7 us; the launch traced here: 61.3 us
  blocking collectives  34.2 us (55%)
  waiting for transfers between devices  16.9 us (27%)
  Pallas kernels  4.46 us (7%)
  local copies, waits for them, and re-layouts  3.09 us (5%)
  starting transfers between devices  2.62 us (4%)
    all_to_all x2, blocking collectives, gather(): lax.all_to_all(copies, axis, 0, 0, tiled=True, axis_index_groups=groups)  34.2 us
    ppermute x3, waiting for transfers between devices, per_device(): lax.ppermute(message, 'ctx', [(a, b) for a, b in zip(members[g - 1], memb...  16.9 us
    pallas_call x7, Pallas kernels, call(): pl.pallas_call(body, out_shape=shapes, in_specs=[pl.BlockSpec(memory_spac...  4.46 us
    ppermute x3, starting transfers between devices, per_device(): lax.ppermute(message, 'ctx', [(a, b) for a, b in zip(members[g - 1], memb...  2.62 us
    unnamed x8, local copies, waits for them, and re-layouts  2.33 us
  transfers between devices with their start and end apart: 3, of which 1 were waited for; matrix products, arithmetic and copies ran while one was open for 0% of the time, Pallas kernels for 3%

profile of v3, /device:TPU:384, one launch (start us, length us, event | category | flops | bytes accessed | tf_op | source)
XLA Modules:
  0.0 61.3 jit_solution(15082765980667285058)
XLA Ops:
  0.0 0.0 copy-start.1
  0.0 0.8 %reshape.3.taps_ref = f32[9,512]{1,0:T(8,128)S(1)} reshape(f32[3,3,512]{2,1,0:T(4,128)} %param.7) | data formatting | bytes 36864 | tf_op jit(solution)/shard_map/reshape | solution.py:287
  0.8 0.0 copy-start.3
  0.8 0.0 copy-done.1
  0.8 0.7 %copy-done.3 = f32[512]{0:T(512)S(1)} copy-done((f32[512]{0:T(512)S(1)}, f32[512]{0:T(512)}, u32[]{:S(2)}) %copy-start.3) | copy-done | bytes 2072
  1.4 0.0 copy-start
  1.4 0.9 %copy-done = bf16[128,512]{1,0:T(8,128)(2,1)S(1)} copy-done((bf16[128,512]{1,0:T(8,128)(2,1)S(1)}, bf16[128,512]{1,0:T(8,128)(2,1)}, u32[]{:S(2)}) %copy-start) | copy-done | bytes 131096
  2.4 0.0 copy-start.2
  2.4 0.8 %copy-done.2 = f32[512,16]{0,1:T(8,128)S(1)} copy-done((f32[512,16]{0,1:T(8,128)S(1)}, f32[512,16]{0,1:T(8,128)}, u32[]{:S(2)}) %copy-start.2) | copy-done | bytes 32792
  3.1 0.3 shard_map.55
  3.4 9.5 %all_to_all.10.refs_0_ = f32[8,1,128]{2,1,0:T(1,128)S(1)} all-to-all(f32[8,1,128]{2,1,0:T(1,128)S(1)} %get-tuple-element.19), channel_id=1, replica_groups=mesh['ctx'=64,'ch'=8] {'ch'}, dimensions={0} | all-to-all | bytes 8192 | tf_op jit(solution)/shard_map/all_to_all | solution.py:275
  13.0 1.1 %shard_map.56 = (bf16[128,512]{1,0:T(8,128)(2,1)S(1)}, f32[128,512]{1,0:T(8,128)S(1)}, f32[16,80,128]{2,1,0:T(8,128)S(1)}) custom-call(f32[8,1,128]{2,1,0:T(1,128)S(1)} %all_to_all.10.refs_0_, bf16[128,512]{1,0:T(8,128)(2,1)S(1)} %copy-done, f32[1,512]{1,0:T(1,128)S(1)} %get-tuple-element.20.refs_2_, f32[9,512]{1,0:T(8,128)S(1)} %get-tuple-element.21.refs_3_, ...), custom_call_target="tpu_custom_call" | custom-call | bytes 188416 | tf_op jit(solution)/shard_map/pallas_call | solution.py:21
  14.0 24.6 %all_to_all.11.refs_0_.refs_2_ = f32[16,80,128]{2,1,0:T(8,128)S(1)} all-to-all(f32[16,80,128]{2,1,0:T(8,128)S(1)} %get-tuple-element.23), channel_id=1, replica_groups={{0,8,16,24,32,40,48,56,64,72,80,88,96,104,112,120},{128,136,144,152,160..., dimensions={0} | all-to-all | bytes 1310720 | tf_op jit(solution)/shard_map/all_to_all | solution.py:275
  38.7 0.3 shard_map.57
  38.9 0.7 %collective-permute-start = (f32[72,128]{1,0:T(8,128)S(1)}, f32[72,128]{1,0:T(8,128)S(1)}, u32[]{:S(2)}, u32[]{:S(2)}) collective-permute-start(f32[72,128]{1,0:T(8,128)S(1)} %get-tuple-element.26), channel_id=1, source_target_pairs={{0,128},{8,136},{16,144},{24,152},{32,160},{40,168},{48,176},{56,1... | collective-permute-start | bytes 110600 | tf_op jit(solution)/shard_map/ppermute | solution.py:312
  39.6 0.0 collective-permute-done.refs_0_.refs_1_
  39.6 0.7 %collective-permute-start.1 = (f32[72,128]{1,0:T(8,128)S(1)}, f32[72,128]{1,0:T(8,128)S(1)}, u32[]{:S(2)}, u32[]{:S(2)}) collective-permute-start(f32[72,128]{1,0:T(8,128)S(1)} %shard_map.58), channel_id=1, source_target_pairs={{128,256},{136,264},{144,272},{152,280},{160,288},{168,296},{176,3... | collective-permute-start | bytes 110600 | tf_op jit(solution)/shard_map/ppermute | solution.py:312
  40.3 0.0 collective-permute-done.1.refs_0_.refs_2_
  40.4 1.3 %collective-permute-start.2 = (f32[72,128]{1,0:T(8,128)S(1)}, f32[72,128]{1,0:T(8,128)S(1)}, u32[]{:S(2)}, u32[]{:S(2)}) collective-permute-start(f32[72,128]{1,0:T(8,128)S(1)} %shard_map.59), channel_id=1, source_target_pairs={{256,384},{264,392},{272,400},{280,408},{288,416},{296,424},{304,4... | collective-permute-start | bytes 110600 | tf_op jit(solution)/shard_map/ppermute | solution.py:312
  41.7 1.6 %shard_map.60.refs_9_ = f32[128,512]{1,0:T(8,128)S(1)} custom-call(f32[16,512]{1,0:T(8,128)S(1)} %get-tuple-element.22.refs_4_.rate_ref.refs_8_, f32[16,512]{1,0:T(8,128)S(1)} %get-tuple-element.30.residue_ref, f32[128,512]{1,0:T(8,128)S(1)} %get-tuple-element.31.product_ref, f32[64,128]{1,0:T(8,128)S(1)} %get-tuple-element.28.after_ref.refs_4_), custom_call_target="tpu_custom_call" | custom-call | flops 10000000 | bytes 360448 | tf_op jit(solution)/shard_map/pallas_call | solution.py:21
  43.3 16.9 %collective-permute-done.2.refs_3_ = f32[72,128]{1,0:T(8,128)S(1)} collective-permute-done((f32[72,128]{1,0:T(8,128)S(1)}, f32[72,128]{1,0:T(8,128)S(1)}, u32[]{:S(2)}, u32[]{:S(2)}) %collective-permute-start.2) | collective-permute-done | bytes 36896 | tf_op jit(solution)/shard_map/ppermute | solution.py:312
  60.2 1.1 %shard_map.61 = bf16[128,512]{1,0:T(8,128)(2,1)} custom-call(f32[16,80,128]{2,1,0:T(8,128)S(1)} %all_to_all.11.refs_0_.refs_2_, f32[72,128]{1,0:T(8,128)S(1)} %collective-permute-done.refs_0_.refs_1_, f32[72,128]{1,0:T(8,128)S(1)} %collective-permute-done.1.refs_0_.refs_2_, f32[72,128]{1,0:T(8,128)S(1)} %collective-permute-done.2.refs_3_, ...), custom_call_target="tpu_custom_call" | custom-call | bytes 1308672 | tf_op jit(solution)/shard_map/pallas_call | solution.py:21
  (2 shorter events, 0.1 us)
Async XLA Ops:
  0.0 0.8 %copy-start.1 = (f32[512,16]{0,1:T(8,128)S(1)}, f32[512,16]{0,1:T(8,128)}, u32[]{:S(2)}) copy-start(f32[512,16]{0,1:T(8,128)} %param.8) | copy-start | bytes 98308
  0.8 0.7 %copy-start.3 = (f32[512]{0:T(512)S(1)}, f32[512]{0:T(512)}, u32[]{:S(2)}) copy-start(f32[512]{0:T(512)} %param.6) | copy-start | bytes 6148
  1.4 0.9 %copy-start = (bf16[128,512]{1,0:T(8,128)(2,1)S(1)}, bf16[128,512]{1,0:T(8,128)(2,1)}, u32[]{:S(2)}) copy-start(bf16[128,512]{1,0:T(8,128)(2,1)} %refs_1_.1) | copy-start | bytes 393220
  2.4 0.8 %copy-start.2 = (f32[512,16]{0,1:T(8,128)S(1)}, f32[512,16]{0,1:T(8,128)}, u32[]{:S(2)}) copy-start(f32[512,16]{0,1:T(8,128)} %param.9) | copy-start | bytes 98308
  38.9 0.7 %collective-permute-start = (f32[72,128]{1,0:T(8,128)S(1)}, f32[72,128]{1,0:T(8,128)S(1)}, u32[]{:S(2)}, u32[]{:S(2)}) collective-permute-start(f32[72,128]{1,0:T(8,128)S(1)} %get-tuple-element.26), channel_id=1, source_target_pairs={{0,128},{8,136},{16,144},{24,152},{32,160},{40,168},{48,176},{56,1... | collective-permute-start | bytes 110600 | tf_op jit(solution)/shard_map/ppermute | solution.py:312
  39.6 0.7 %collective-permute-start.1 = (f32[72,128]{1,0:T(8,128)S(1)}, f32[72,128]{1,0:T(8,128)S(1)}, u32[]{:S(2)}, u32[]{:S(2)}) collective-permute-start(f32[72,128]{1,0:T(8,128)S(1)} %shard_map.58), channel_id=1, source_target_pairs={{128,256},{136,264},{144,272},{152,280},{160,288},{168,296},{176,3... | collective-permute-start | bytes 110600 | tf_op jit(solution)/shard_map/ppermute | solution.py:312
  40.4 19.8 %collective-permute-start.2 = (f32[72,128]{1,0:T(8,128)S(1)}, f32[72,128]{1,0:T(8,128)S(1)}, u32[]{:S(2)}, u32[]{:S(2)}) collective-permute-start(f32[72,128]{1,0:T(8,128)S(1)} %shard_map.59), channel_id=1, source_target_pairs={{256,384},{264,392},{272,400},{280,408},{288,416},{296,424},{304,4... | collective-permute-start | bytes 110600 | tf_op jit(solution)/shard_map/ppermute | solution.py:312

commit v4 on v3

--- a/solution.py
+++ b/solution.py
@@ -9,7 +9,7 @@
 EPSILON = 1e-05
 SUB = 8
 LANES = 128
-NEAR = 16
+NEAR = 4
 
 F32 = jnp.float32
 BF16 = jnp.bfloat16
@@ -124,44 +124,54 @@
     return ref[pl.ds(start, lanes), :], ref[pl.ds(start + lanes, lanes), :]
 
 
-def near_scan(block, lanes, got_ref, rate_ref, taps_ref, before_ref, total_ref, message_ref):
-    place = lax.axis_index("ctx") % NEAR
-    states = rate_ref.shape[0]
-    modes = states // lanes
-    rates = rate_ref[...]
-    step, late, later = jnp.exp(-block * rates), jnp.exp(-(block - 1) * rates), jnp.exp(-(block - 2) * rates)
-    total = got_ref[0, :states]
-    before = jnp.where(place == 1, total, jnp.zeros_like(total))
-    for j in range(1, NEAR):
-        last = pairs(got_ref.at[j - 1], states + 2 * lanes, lanes)
-        head = pairs(got_ref.at[j], states, lanes)
-        first, second = first_products(taps_ref, last, head)
-        total = total * step + got_ref[j, :states] + late * spread(first, modes) + later * spread(second, modes)
-        if j < NEAR - 1:
-            before = jnp.where(place == j + 1, total, before)
-    before_ref[...] = before
-    total_ref[...] = total
-    send(block, lanes, None, total, got_ref, rates, taps_ref, message_ref)
-
-
-def send(block, lanes, came_ref, total, got_ref, rates, taps_ref, message_ref):
+def step_over(block, lanes, rates, taps_ref, state, last, run_ref):
     states = rates.shape[0]
     modes = states // lanes
-    head = pairs(got_ref.at[0], states, lanes)
-    if came_ref is None:
-        last = [jnp.zeros((lanes, LANES), F32)] * 2
-    else:
-        last = pairs(came_ref, states, lanes)
-        total = total + came_ref[:states] * jnp.exp(-(block * NEAR) * rates)
-    first, second = first_products(taps_ref, last, head)
-    total = total + jnp.exp(-(block * NEAR - 1) * rates) * spread(first, modes)
-    total = total + jnp.exp(-(block * NEAR - 2) * rates) * spread(second, modes)
-    message_ref[:states] = total
-    message_ref[states:] = got_ref[NEAR - 1, states + 2 * lanes :]
-
-
-def chain_step(block, lanes, came_ref, total_ref, got_ref, rate_ref, taps_ref, message_ref):
-    send(block, lanes, came_ref, total_ref[...], got_ref, rate_ref[...], taps_ref, message_ref)
+    first, second = first_products(taps_ref, last, pairs(run_ref, states, lanes))
+    end = run_ref[:states] + state * jnp.exp(-block * rates)
+    end = end + jnp.exp(-(block - 1) * rates) * spread(first, modes) + jnp.exp(-(block - 2) * rates) * spread(second, modes)
+    return end, pairs(run_ref, states + 2 * lanes, lanes)
+
+
+def step_into(block, lanes, place, rates, taps_ref, state, last, got_ref, before_ref):
+    states = rates.shape[0]
+    modes = states // lanes
+    first, second = first_products(taps_ref, last, pairs(got_ref.at[0], states, lanes))
+    lag = (block * place).astype(F32)
+    held = jnp.exp(-rates * jnp.maximum(lag - 1.0, 0.0)) * spread(first, modes)
+    held = held + jnp.exp(-rates * jnp.maximum(lag - 2.0, 0.0)) * spread(second, modes)
+    state = before_ref[...] + state * jnp.exp(-rates * lag) + jnp.where(place > 0, held, 0.0)
+    inside = pairs(got_ref.at[jnp.maximum(place - 1, 0)], states + 2 * lanes, lanes)
+    return state, [jnp.where(place > 0, a, b) for a, b in zip(inside, last)]
+
+
+def near_scan(block, lanes, place, got_ref, rate_ref, taps_ref, before_ref, message_ref):
+    states = rate_ref.shape[0]
+    rates = rate_ref[...]
+    total, last = got_ref[0, :states], pairs(got_ref.at[0], states + 2 * lanes, lanes)
+    before = jnp.where(place() == 1, total, jnp.zeros_like(total))
+    for j in range(1, NEAR):
+        total, last = step_over(block, lanes, rates, taps_ref, total, last, got_ref.at[j])
+        if j < NEAR - 1:
+            before = jnp.where(place() == j + 1, total, before)
+    before_ref[...] = before
+    head = got_ref[0, states : states + 2 * lanes]
+    tail = got_ref[NEAR - 1, states + 2 * lanes :]
+    for peer in range(message_ref.shape[0]):
+        message_ref[peer, :states] = total
+        message_ref[peer, states : states + 2 * lanes] = head
+        message_ref[peer, states + 2 * lanes :] = tail
+
+
+def relay(block, lanes, came_ref, own_ref, rate_ref, taps_ref, out_ref):
+    rates = rate_ref[...]
+    states = rates.shape[0]
+    state, last = jnp.zeros_like(rates), [jnp.zeros((lanes, LANES), F32)] * 2
+    for ref in (came_ref, own_ref.at[0]):
+        state, last = step_over(block, lanes, rates, taps_ref, state, last, ref)
+    out_ref[:states] = state
+    out_ref[pl.ds(states, lanes)] = last[0]
+    out_ref[pl.ds(states + lanes, lanes)] = last[1]
 
 
 def add_mode(totals, term, rate):
@@ -208,31 +218,22 @@
     lax.fori_loop(0, chans // LANES, one_lane, 0)
 
 
-def outer_conv(steps, got_ref, *refs):
-    came_refs, refs = refs[:steps], refs[steps:]
-    before_ref, rate_pack, residue_pack, taps_ref, rate_ref, local_ref, query_ref, mixed_ref, state_ref = refs
+def outer_conv(near_ref, near_before, far_ref, far_before, odd_ref, third_ref, fourth_ref, rate_pack, residue_pack, taps_ref, rate_ref, local_ref, query_ref, mixed_ref, state_ref):
     count, chans = local_ref.shape
     lanes = chans // LANES
     modes = rate_ref.shape[0]
     states = lanes * modes
     blocks = count // SUB
-    place = lax.axis_index("ctx") % NEAR
+    place, level, group = places()
     rates = rate_pack[...]
-    came = came_refs[0][...]
-    for ref in came_refs[1:]:
-        came = came + ref[...]
-    group_last = (came[states : states + lanes], came[states + lanes :])
-    first, second = first_products(taps_ref, group_last, pairs(got_ref.at[0], states, lanes))
-    lag = (count * place).astype(F32)
-    lead = jnp.exp(-rates * lag)
-    state = before_ref[...] + came[:states] * lead
-    held = jnp.exp(-rates * jnp.maximum(lag - 1.0, 0.0)) * spread(first, modes)
-    held = held + jnp.exp(-rates * jnp.maximum(lag - 2.0, 0.0)) * spread(second, modes)
-    state = state + jnp.where(place > 0, held, 0.0)
-
-    own_last = pairs(got_ref.at[jnp.maximum(place - 1, 0)], states + 2 * lanes, lanes)
-    own_last = [jnp.where(place > 0, own, group) for own, group in zip(own_last, group_last)]
-    own_head = pairs(got_ref.at[place], states, lanes)
+    came = third_ref[...] + fourth_ref[...]
+    state, last = came[:states], (came[states : states + lanes], came[states + lanes :])
+    after, after_last = step_over(count * NEAR * NEAR, lanes, rates, taps_ref, state, last, odd_ref)
+    odd = group % 2 == 1
+    state, last = jnp.where(odd, after, state), [jnp.where(odd, a, b) for a, b in zip(after_last, last)]
+    state, last = step_into(count * NEAR, lanes, level, rates, taps_ref, state, last, far_ref, far_before)
+    state, own_last = step_into(count, lanes, place, rates, taps_ref, state, last, near_ref, near_before)
+    own_head = pairs(near_ref.at[place], states, lanes)
     own_query = [q.astype(BF16).astype(F32) for q in first_rows(taps_ref, 0, own_last, own_head)]
     first, second = first_products(taps_ref, own_last, own_head)
     ahead = jnp.exp(rates) * spread(second, modes)
@@ -271,6 +272,11 @@
     lax.fori_loop(0, lanes, one_lane, 0)
 
 
+def places():
+    index = lax.axis_index("ctx")
+    return index % NEAR, index // NEAR % NEAR, index // NEAR**2
+
+
 def gather(copies, axis, groups=None):
     return lax.all_to_all(copies, axis, 0, 0, tiled=True, axis_index_groups=groups)
 
@@ -281,8 +287,10 @@
     lanes = chans // LANES
     states = lanes * modes
     peers = lax.axis_size("ch")
-    groups = lax.axis_size("ctx") // NEAR
-    members = [[g * NEAR + m for m in range(NEAR)] for g in range(groups)]
+    ctx = lax.axis_size("ctx")
+    runs = [[r + m for m in range(NEAR)] for r in range(0, ctx, NEAR)]
+    columns = [[g + m + NEAR * r for r in range(NEAR)] for g in range(0, ctx, NEAR**2) for m in range(NEAR)]
+    groups = [[g + m for m in range(NEAR**2)] for g in range(0, ctx, NEAR**2)]
 
     params = [norm_gain[None, :], short_filter.reshape(9, chans), decay_rate.T, residue.T]
     packed = [((9 * lanes, LANES), F32), ((states, LANES), F32), ((states, LANES), F32)]
@@ -296,29 +304,34 @@
         sums, stream, gain, taps, rates,
         scratch=[pltpu.VMEM((SUB + count, chans), F32), pltpu.VMEM((modes, chans), F32)],
     )
-    got = gather(message, "ctx", members)
-    carried = ((states + 2 * lanes, LANES), F32)
-    before, total, message = call(
-        lambda *refs: near_scan(count, lanes, *refs),
-        [((states, LANES), F32), ((states, LANES), F32), carried],
-        got, rate_pack, taps_pack,
-    )
-    came = []
-    for g in range(1, groups):
-        if g > 1:
-            (message,) = call(
-                lambda *refs: chain_step(count, lanes, *refs), [carried], came[-1], total, got, rate_pack, taps_pack
-            )
-        came.append(lax.ppermute(message, "ctx", [(a, b) for a, b in zip(members[g - 1], members[g])]))
-        if g == 1:
-            (local,) = call(
-                inner_conv, [((count, chans), F32)], rates, weights, product, before,
-                scratch=[pltpu.VMEM((count, LANES), F32)], flops=10**7,
-            )
+    shapes = [((states, LANES), F32), ((NEAR, states + 4 * lanes, LANES), F32)]
+    near = gather(message, "ctx", runs)
+    near_before, message = call(
+        lambda *refs: near_scan(count, lanes, lambda: places()[0], *refs), shapes, near, rate_pack, taps_pack
+    )
+    far = gather(message, "ctx", columns)
+    far_before, message = call(
+        lambda *refs: near_scan(count * NEAR, lanes, lambda: places()[1], *refs),
+        [shapes[0], ((1,) + shapes[1][0][1:], F32)],
+        far, rate_pack, taps_pack,
+    )
+    hops = [list(zip(groups[a], groups[b])) for a, b in ((0, 1), (2, 3), (1, 2), (1, 3))]
+    odd = lax.ppermute(message[0], "ctx", hops[0] + hops[1])
+    (local,) = call(
+        inner_conv, [((count, chans), F32)], rates, weights, product, far_before,
+        scratch=[pltpu.VMEM((count, LANES), F32)], flops=10**7,
+    )
+    (relayed,) = call(
+        lambda *refs: relay(count * NEAR**2, lanes, *refs),
+        [((states + 2 * lanes, LANES), F32)],
+        odd, message, rate_pack, taps_pack,
+    )
+    fourth = lax.ppermute(relayed, "ctx", hops[3])
+    third = lax.ppermute(relayed, "ctx", hops[2])
     (mixed,) = call(
-        lambda *refs: outer_conv(len(came), *refs),
+        outer_conv,
         [((count, chans), BF16)],
-        got, *came, before, rate_pack, residue_pack, taps_pack, rates, local, query,
+        near, near_before, far, far_before, odd, third, fourth, rate_pack, residue_pack, taps_pack, rates, local, query,
         scratch=[pltpu.VMEM((modes + 2 * SUB, chans), F32)],
     )
     return mixed

time: 61.7 us -> 60.2 us (0.976)
  the two profiles are of different devices: /device:TPU:384 before, /device:TPU:416 now
where the time goes in v4:
time: 60.2 us; the launch traced here: 59.8 us
  blocking collectives  29.2 us (49%)
  waiting for transfers between devices  19.9 us (33%)
  Pallas kernels  4.32 us (7%)
  starting transfers between devices  3.25 us (5%)
  local copies, waits for them, and re-layouts  3.09 us (5%)
    all_to_all x3, blocking collectives, gather(): lax.all_to_all(copies, axis, 0, 0, tiled=True, axis_index_groups=groups)  29.2 us
    ppermute x1, waiting for transfers between devices, per_device(): fourth = lax.ppermute(relayed, 'ctx', hops[3])  11.4 us
    ppermute x1, waiting for transfers between devices, per_device(): odd = lax.ppermute(message[0], 'ctx', hops[0] + hops[1])  8.5 us
    pallas_call x7, Pallas kernels, call(): pl.pallas_call(body, out_shape=shapes, in_specs=[pl.BlockSpec(memory_spac...  4.32 us
    unnamed x8, local copies, waits for them, and re-layouts  2.33 us
    ppermute x1, starting transfers between devices, per_device(): odd = lax.ppermute(message[0], 'ctx', hops[0] + hops[1])  1.29 us
    ppermute x1, starting transfers between devices, per_device(): fourth = lax.ppermute(relayed, 'ctx', hops[3])  1.29 us
  transfers between devices with their start and end apart: 3, of which 2 were waited for; matrix products, arithmetic and copies ran while one was open for 0% of the time, Pallas kernels for 3%

profile of v4, /device:TPU:416, one launch (start us, length us, event | category | flops | bytes accessed | tf_op | source)
XLA Modules:
  0.0 59.8 jit_solution(10524777279409154115)
XLA Ops:
  0.0 0.0 copy-start.1
  0.0 0.8 %reshape.3.taps_ref = f32[9,512]{1,0:T(8,128)S(1)} reshape(f32[3,3,512]{2,1,0:T(4,128)} %param.7) | data formatting | bytes 36864 | tf_op jit(solution)/shard_map/reshape | solution.py:295
  0.8 0.0 copy-start.3
  0.8 0.0 copy-done.1
  0.8 0.7 %copy-done.3 = f32[512]{0:T(512)S(1)} copy-done((f32[512]{0:T(512)S(1)}, f32[512]{0:T(512)}, u32[]{:S(2)}) %copy-start.3) | copy-done | bytes 2072
  1.4 0.0 copy-start
  1.4 0.9 %copy-done = bf16[128,512]{1,0:T(8,128)(2,1)S(1)} copy-done((bf16[128,512]{1,0:T(8,128)(2,1)S(1)}, bf16[128,512]{1,0:T(8,128)(2,1)}, u32[]{:S(2)}) %copy-start) | copy-done | bytes 131096
  2.4 0.0 copy-start.2
  2.4 0.8 %copy-done.2 = f32[512,16]{0,1:T(8,128)S(1)} copy-done((f32[512,16]{0,1:T(8,128)S(1)}, f32[512,16]{0,1:T(8,128)}, u32[]{:S(2)}) %copy-start.2) | copy-done | bytes 32792
  3.1 0.3 shard_map.55
  3.4 9.5 %all_to_all.15.refs_0_ = f32[8,1,128]{2,1,0:T(1,128)S(1)} all-to-all(f32[8,1,128]{2,1,0:T(1,128)S(1)} %get-tuple-element.20), channel_id=1, replica_groups=mesh['ctx'=64,'ch'=8] {'ch'}, dimensions={0} | all-to-all | bytes 8192 | tf_op jit(solution)/shard_map/all_to_all | solution.py:281
  13.0 1.1 %shard_map.56 = (bf16[128,512]{1,0:T(8,128)(2,1)S(1)}, f32[128,512]{1,0:T(8,128)S(1)}, f32[4,80,128]{2,1,0:T(8,128)S(1)}) custom-call(f32[8,1,128]{2,1,0:T(1,128)S(1)} %all_to_all.15.refs_0_, bf16[128,512]{1,0:T(8,128)(2,1)S(1)} %copy-done, f32[1,512]{1,0:T(1,128)S(1)} %get-tuple-element.21.refs_2_, f32[9,512]{1,0:T(8,128)S(1)} %get-tuple-element.22.refs_3_, ...), custom_call_target="tpu_custom_call" | custom-call | bytes 188416 | tf_op jit(solution)/shard_map/pallas_call | solution.py:21
  14.0 10.2 %all_to_all.16.refs_0_.near_ref = f32[4,80,128]{2,1,0:T(8,128)S(1)} all-to-all(f32[4,80,128]{2,1,0:T(8,128)S(1)} %get-tuple-element.24), channel_id=1, replica_groups={{0,8,16,24},{32,40,48,56},{64,72,80,88},{96,104,112,120},{128,136,144,1..., dimensions={0} | all-to-all | bytes 327680 | tf_op jit(solution)/shard_map/all_to_all | solution.py:281
  24.3 0.1 shard_map.57
  24.3 9.4 %all_to_all.17.refs_0_.far_ref = f32[4,80,128]{2,1,0:T(8,128)S(1)} all-to-all(f32[4,80,128]{2,1,0:T(8,128)S(1)} %get-tuple-element.28), channel_id=1, replica_groups={{0,32,64,96},{8,40,72,104},{16,48,80,112},{24,56,88,120},{128,160,192,2..., dimensions={0} | all-to-all | bytes 327680 | tf_op jit(solution)/shard_map/all_to_all | solution.py:281
  33.8 0.1 shard_map.58
  33.8 1.3 %collective-permute-start = (f32[80,128]{1,0:T(8,128)S(1)}, f32[80,128]{1,0:T(8,128)S(1)}, u32[]{:S(2)}, u32[]{:S(2)}) collective-permute-start(f32[80,128]{1,0:T(8,128)S(1)} %bitcast.4), channel_id=1, source_target_pairs={{0,128},{8,136},{16,144},{24,152},{32,160},{40,168},{48,176},{56,1... | collective-permute-start | bytes 122888 | tf_op jit(solution)/shard_map/ppermute | solution.py:319
  35.1 8.5 %collective-permute-done.refs_0_.odd_ref = f32[80,128]{1,0:T(8,128)S(1)} collective-permute-done((f32[80,128]{1,0:T(8,128)S(1)}, f32[80,128]{1,0:T(8,128)S(1)}, u32[]{:S(2)}, u32[]{:S(2)}) %collective-permute-start) | collective-permute-done | bytes 40992 | tf_op jit(solution)/shard_map/ppermute | solution.py:319
  43.7 1.3 %collective-permute-start.2 = (f32[72,128]{1,0:T(8,128)S(1)}, f32[72,128]{1,0:T(8,128)S(1)}, u32[]{:S(2)}, u32[]{:S(2)}) collective-permute-start(f32[72,128]{1,0:T(8,128)S(1)} %shard_map.59), channel_id=1, source_target_pairs={{128,384},{136,392},{144,400},{152,408},{160,416},{168,424},{176,4... | collective-permute-start | bytes 110600 | tf_op jit(solution)/shard_map/ppermute | solution.py:329
  45.0 0.7 %collective-permute-start.1 = (f32[72,128]{1,0:T(8,128)S(1)}, f32[72,128]{1,0:T(8,128)S(1)}, u32[]{:S(2)}, u32[]{:S(2)}) collective-permute-start(f32[72,128]{1,0:T(8,128)S(1)} %shard_map.59), channel_id=1, source_target_pairs={{128,256},{136,264},{144,272},{152,280},{160,288},{168,296},{176,3... | collective-permute-start | bytes 110600 | tf_op jit(solution)/shard_map/ppermute | solution.py:330
  45.6 1.6 %shard_map.60.local_ref = f32[128,512]{1,0:T(8,128)S(1)} custom-call(f32[16,512]{1,0:T(8,128)S(1)} %get-tuple-element.23.refs_4_.rate_ref, f32[16,512]{1,0:T(8,128)S(1)} %get-tuple-element.32.residue_ref, f32[128,512]{1,0:T(8,128)S(1)} %get-tuple-element.33.product_ref, f32[64,128]{1,0:T(8,128)S(1)} %get-tuple-element.29.after_ref.far_before), custom_call_target="tpu_custom_call" | custom-call | flops 10000000 | bytes 360448 | tf_op jit(solution)/shard_map/pallas_call | solution.py:21
  47.3 11.4 %collective-permute-done.2.fourth_ref = f32[72,128]{1,0:T(8,128)S(1)} collective-permute-done((f32[72,128]{1,0:T(8,128)S(1)}, f32[72,128]{1,0:T(8,128)S(1)}, u32[]{:S(2)}, u32[]{:S(2)}) %collective-permute-start.2) | collective-permute-done | bytes 36896 | tf_op jit(solution)/shard_map/ppermute | solution.py:329
  58.6 0.0 collective-permute-done.1.third_ref
  58.6 1.2 %shard_map.61 = bf16[128,512]{1,0:T(8,128)(2,1)} custom-call(f32[4,80,128]{2,1,0:T(8,128)S(1)} %all_to_all.16.refs_0_.near_ref, f32[64,128]{1,0:T(8,128)S(1)} %get-tuple-element.27.near_before, f32[4,80,128]{2,1,0:T(8,128)S(1)} %all_to_all.17.refs_0_.far_ref, f32[64,128]{1,0:T(8,128)S(1)} %get-tuple-element.29.after_ref.far_before, ...), custom_call_target="tpu_custom_call" | custom-call | bytes 1017856 | tf_op jit(solution)/shard_map/pallas_call | solution.py:21
  (1 shorter events, 0.0 us)
Async XLA Ops:
  0.0 0.8 %copy-start.1 = (f32[512,16]{0,1:T(8,128)S(1)}, f32[512,16]{0,1:T(8,128)}, u32[]{:S(2)}) copy-start(f32[512,16]{0,1:T(8,128)} %param.8) | copy-start | bytes 98308
  0.8 0.7 %copy-start.3 = (f32[512]{0:T(512)S(1)}, f32[512]{0:T(512)}, u32[]{:S(2)}) copy-start(f32[512]{0:T(512)} %param.6) | copy-start | bytes 6148
  1.4 0.9 %copy-start = (bf16[128,512]{1,0:T(8,128)(2,1)S(1)}, bf16[128,512]{1,0:T(8,128)(2,1)}, u32[]{:S(2)}) copy-start(bf16[128,512]{1,0:T(8,128)(2,1)} %refs_1_.1) | copy-start | bytes 393220
  2.4 0.8 %copy-start.2 = (f32[512,16]{0,1:T(8,128)S(1)}, f32[512,16]{0,1:T(8,128)}, u32[]{:S(2)}) copy-start(f32[512,16]{0,1:T(8,128)} %param.9) | copy-start | bytes 98308
  33.8 9.8 %collective-permute-start = (f32[80,128]{1,0:T(8,128)S(1)}, f32[80,128]{1,0:T(8,128)S(1)}, u32[]{:S(2)}, u32[]{:S(2)}) collective-permute-start(f32[80,128]{1,0:T(8,128)S(1)} %bitcast.4), channel_id=1, source_target_pairs={{0,128},{8,136},{16,144},{24,152},{32,160},{40,168},{48,176},{56,1... | collective-permute-start | bytes 122888 | tf_op jit(solution)/shard_map/ppermute | solution.py:319
  43.7 15.0 %collective-permute-start.2 = (f32[72,128]{1,0:T(8,128)S(1)}, f32[72,128]{1,0:T(8,128)S(1)}, u32[]{:S(2)}, u32[]{:S(2)}) collective-permute-start(f32[72,128]{1,0:T(8,128)S(1)} %shard_map.59), channel_id=1, source_target_pairs={{128,384},{136,392},{144,400},{152,408},{160,416},{168,424},{176,4... | collective-permute-start | bytes 110600 | tf_op jit(solution)/shard_map/ppermute | solution.py:329
  45.0 13.7 %collective-permute-start.1 = (f32[72,128]{1,0:T(8,128)S(1)}, f32[72,128]{1,0:T(8,128)S(1)}, u32[]{:S(2)}, u32[]{:S(2)}) collective-permute-start(f32[72,128]{1,0:T(8,128)S(1)} %shard_map.59), channel_id=1, source_target_pairs={{128,256},{136,264},{144,272},{152,280},{160,288},{168,296},{176,3... | collective-permute-start | bytes 110600 | tf_op jit(solution)/shard_map/ppermute | solution.py:330

commit v5 on v4

--- a/solution.py
+++ b/solution.py
@@ -15,16 +15,16 @@
 BF16 = jnp.bfloat16
 
 
-def call(body, outs, *args, scratch=(), flops=0):
+def call(body, outs, *args, scratch=(), flops=0, space=pltpu.VMEM, grant=16):
     shapes = [jax.ShapeDtypeStruct(s, d) for s, d in outs]
     moved = sum(a.size * a.dtype.itemsize for a in args)
     return pl.pallas_call(
         body,
         out_shape=shapes,
-        in_specs=[pl.BlockSpec(memory_space=pltpu.VMEM)] * len(args),
+        in_specs=[pl.BlockSpec(memory_space=space)] * len(args),
         out_specs=[pl.BlockSpec(memory_space=pltpu.VMEM)] * len(shapes),
         scratch_shapes=list(scratch),
-        compiler_params=pltpu.CompilerParams(vmem_limit_bytes=16 * 2**20),
+        compiler_params=pltpu.CompilerParams(vmem_limit_bytes=grant * 2**20),
         cost_estimate=pl.CostEstimate(flops=flops, bytes_accessed=moved, transcendentals=0),
     )(*args)
 
@@ -33,7 +33,16 @@
     return jnp.concatenate([ref[:, l * LANES : (l + 1) * LANES] for l in range(ref.shape[1] // LANES)], axis=0)
 
 
-def square_sums(stream_ref, gain_ref, taps_ref, rate_ref, residue_ref, sums_ref, gain_out, taps_out, rate_out, residue_out, taps_pack, rate_pack, residue_pack):
+def square_sums(*refs):
+    count = 5
+    held, refs = refs[:count], refs[count:]
+    (stream_ref, gain_ref, taps_ref, rate_ref, residue_ref), refs = refs[:count], refs[count:]
+    sums_ref, taps_pack, rate_pack, residue_pack, sem = refs
+    copies = [pltpu.make_async_copy(held[i], out, sem.at[i]) for i, out in enumerate((stream_ref, gain_ref, taps_ref, rate_ref, residue_ref))]
+    for copy in copies:
+        copy.start()
+    for copy in copies:
+        copy.wait()
     chans = stream_ref.shape[1]
     values = stream_ref[...].astype(F32)
     sums = lax.dot_general(
@@ -41,16 +50,13 @@
     )
     for peer in range(sums_ref.shape[0]):
         sums_ref[peer] = sums[:1]
-    gain_out[...] = gain_ref[...]
-    taps_out[...] = taps_ref[...]
-    rate_out[...] = rate_ref[...]
-    residue_out[...] = residue_ref[...]
     rate_pack[...] = pack(rate_ref)
     residue_pack[...] = pack(residue_ref)
     lanes = chans // LANES
-    for k in range(taps_ref.shape[0]):
-        for l in range(lanes):
-            taps_pack[pl.ds(k * lanes + l, 1), :] = taps_ref[pl.ds(k, 1), pl.ds(l * LANES, LANES)]
+    for tap in range(3):
+        for role in range(3):
+            for l in range(lanes):
+                taps_pack[pl.ds((tap * 3 + role) * lanes + l, 1), :] = taps_ref[tap, pl.ds(role, 1), pl.ds(l * LANES, LANES)]
 
 
 def block_states(chan_total, sums_ref, stream_ref, gain_ref, taps_ref, rate_ref, query_ref, product_ref, message_ref, normed_ref, end_ref):
@@ -70,9 +76,9 @@
     shifted = [normed_ref[SUB - j : SUB - j + count] for j in range(3)]
 
     def feature(role):
-        total = taps_ref[pl.ds(role, 1)] * shifted[0]
-        total = total + taps_ref[pl.ds(3 + role, 1)] * shifted[1]
-        return total + taps_ref[pl.ds(6 + role, 1)] * shifted[2]
+        total = taps_ref[0, pl.ds(role, 1)] * shifted[0]
+        total = total + taps_ref[1, pl.ds(role, 1)] * shifted[1]
+        return total + taps_ref[2, pl.ds(role, 1)] * shifted[2]
 
     query_ref[...] = feature(0).astype(BF16)
     product_ref[...] = (feature(1) * feature(2)).astype(BF16).astype(F32)
@@ -121,7 +127,7 @@
 
 
 def pairs(ref, start, lanes):
-    return ref[pl.ds(start, lanes), :], ref[pl.ds(start + lanes, lanes), :]
+    return ref[start : start + lanes], ref[start + lanes : start + 2 * lanes]
 
 
 def step_over(block, lanes, rates, taps_ref, state, last, run_ref):
@@ -166,12 +172,16 @@
 def relay(block, lanes, came_ref, own_ref, rate_ref, taps_ref, out_ref):
     rates = rate_ref[...]
     states = rates.shape[0]
+    low = places()[2] == 0
+    own, came = own_ref[0], came_ref[...]
     state, last = jnp.zeros_like(rates), [jnp.zeros((lanes, LANES), F32)] * 2
-    for ref in (came_ref, own_ref.at[0]):
-        state, last = step_over(block, lanes, rates, taps_ref, state, last, ref)
+    for run in (jnp.where(low, own, came), jnp.where(low, came, own)):
+        state, last = step_over(block, lanes, rates, taps_ref, state, last, run)
     out_ref[:states] = state
     out_ref[pl.ds(states, lanes)] = last[0]
     out_ref[pl.ds(states + lanes, lanes)] = last[1]
+    rest = states + 2 * lanes
+    out_ref[rest:] = jnp.zeros((out_ref.shape[0] - rest, LANES), F32)
 
 
 def add_mode(totals, term, rate):
@@ -218,7 +228,7 @@
     lax.fori_loop(0, chans // LANES, one_lane, 0)
 
 
-def outer_conv(near_ref, near_before, far_ref, far_before, odd_ref, third_ref, fourth_ref, rate_pack, residue_pack, taps_ref, rate_ref, local_ref, query_ref, mixed_ref, state_ref):
+def outer_conv(near_ref, near_before, far_ref, far_before, swap_ref, two_ref, third_ref, rate_pack, residue_pack, taps_ref, rate_ref, local_ref, query_ref, mixed_ref, state_ref):
     count, chans = local_ref.shape
     lanes = chans // LANES
     modes = rate_ref.shape[0]
@@ -226,9 +236,10 @@
     blocks = count // SUB
     place, level, group = places()
     rates = rate_pack[...]
-    came = third_ref[...] + fourth_ref[...]
-    state, last = came[:states], (came[states : states + lanes], came[states + lanes :])
-    after, after_last = step_over(count * NEAR * NEAR, lanes, rates, taps_ref, state, last, odd_ref)
+    came = two_ref[...]
+    state, last = came[:states], (came[states : states + lanes], came[states + lanes : states + 2 * lanes])
+    run = jnp.where(group == 1, swap_ref[...], third_ref[...])
+    after, after_last = step_over(count * NEAR * NEAR, lanes, rates, taps_ref, state, last, run)
     odd = group % 2 == 1
     state, last = jnp.where(odd, after, state), [jnp.where(odd, a, b) for a, b in zip(after_last, last)]
     state, last = step_into(count * NEAR, lanes, level, rates, taps_ref, state, last, far_ref, far_before)
@@ -292,10 +303,15 @@
     columns = [[g + m + NEAR * r for r in range(NEAR)] for g in range(0, ctx, NEAR**2) for m in range(NEAR)]
     groups = [[g + m for m in range(NEAR**2)] for g in range(0, ctx, NEAR**2)]
 
-    params = [norm_gain[None, :], short_filter.reshape(9, chans), decay_rate.T, residue.T]
-    packed = [((9 * lanes, LANES), F32), ((states, LANES), F32), ((states, LANES), F32)]
-    sums, gain, taps, rates, weights, taps_pack, rate_pack, residue_pack = call(
-        square_sums, [((peers, 1, count), F32)] + [(p.shape, F32) for p in params] + packed, stream, *params
+    held = [stream, norm_gain[None, :], short_filter, decay_rate.T, residue.T]
+    held = [pltpu.with_memory_space_constraint(h, pltpu.HBM) for h in held]
+    stream, gain, taps, rates, weights, sums, taps_pack, rate_pack, residue_pack = call(
+        square_sums,
+        [(h.shape, h.dtype) for h in held]
+        + [((peers, 1, count), F32), ((9 * lanes, LANES), F32), ((states, LANES), F32), ((states, LANES), F32)],
+        *held,
+        scratch=[pltpu.SemaphoreType.DMA((len(held),))],
+        space=pltpu.HBM,
     )
     sums = gather(sums, "ch")
     query, product, message = call(
@@ -315,23 +331,24 @@
         [shapes[0], ((1,) + shapes[1][0][1:], F32)],
         far, rate_pack, taps_pack,
     )
-    hops = [list(zip(groups[a], groups[b])) for a, b in ((0, 1), (2, 3), (1, 2), (1, 3))]
-    odd = lax.ppermute(message[0], "ctx", hops[0] + hops[1])
+    hops = lambda *ends: [pair for a, b in ends for pair in zip(groups[a], groups[b])]
+    swap = lax.ppermute(message[0], "ctx", hops((0, 1), (1, 0)))
+    (two,) = call(
+        lambda *refs: relay(count * NEAR**2, lanes, *refs),
+        [((states + 6 * lanes, LANES), F32)],
+        swap, message, rate_pack, taps_pack,
+    )
+    third, two = lax.optimization_barrier((message[0], two))
+    third = lax.ppermute(third, "ctx", hops((2, 3)))
+    two = lax.ppermute(two, "ctx", hops((0, 3), (1, 2)))
     (local,) = call(
         inner_conv, [((count, chans), F32)], rates, weights, product, far_before,
         scratch=[pltpu.VMEM((count, LANES), F32)], flops=10**7,
     )
-    (relayed,) = call(
-        lambda *refs: relay(count * NEAR**2, lanes, *refs),
-        [((states + 2 * lanes, LANES), F32)],
-        odd, message, rate_pack, taps_pack,
-    )
-    fourth = lax.ppermute(relayed, "ctx", hops[3])
-    third = lax.ppermute(relayed, "ctx", hops[2])
     (mixed,) = call(
         outer_conv,
         [((count, chans), BF16)],
-        near, near_before, far, far_before, odd, third, fourth, rate_pack, residue_pack, taps_pack, rates, local, query,
+        near, near_before, far, far_before, swap, two, third, rate_pack, residue_pack, taps_pack, rates, local, query,
         scratch=[pltpu.VMEM((modes + 2 * SUB, chans), F32)],
     )
     return mixed

time: 60.2 us -> 51.3 us (0.85)
  the two profiles are of different devices: /device:TPU:416 before, /device:TPU:2 now
where the time goes in v5:
time: 51.3 us; the launch traced here: 51 us
  blocking collectives  31.3 us (61%)
  starting transfers between devices  11.1 us (22%)
  Pallas kernels  5.29 us (10%)
  waiting for transfers between devices  3.38 us (7%)
    all_to_all x3, blocking collectives, gather(): lax.all_to_all(copies, axis, 0, 0, tiled=True, axis_index_groups=groups)  31.3 us
    ppermute x1, starting transfers between devices, per_device(): swap = lax.ppermute(message[0], 'ctx', hops((0, 1), (1, 0)))  9.09 us
    pallas_call x7, Pallas kernels, call(): pl.pallas_call(body, out_shape=shapes, in_specs=[pl.BlockSpec(memory_spac...  5.29 us
    ppermute x1, waiting for transfers between devices, per_device(): swap = lax.ppermute(message[0], 'ctx', hops((0, 1), (1, 0)))  3.29 us
    ppermute x1, starting transfers between devices, per_device(): two = lax.ppermute(two, 'ctx', hops((0, 3), (1, 2)))  1.29 us
  transfers between devices with their start and end apart: 3, of which 2 were waited for; matrix products, arithmetic and copies ran while one was open for 0% of the time, Pallas kernels for 3%

profile of v5, /device:TPU:2, one launch (start us, length us, event | category | flops | bytes accessed | tf_op | source)
XLA Modules:
  0.0 51.0 jit_solution(14662963337506891536)
XLA Ops:
  0.0 1.3 %shard_map.55 = (bf16[128,512]{1,0:T(8,128)(2,1)S(1)}, f32[1,512]{1,0:T(1,128)S(1)}, f32[3,3,512]{2,1,0:T(4,128)S(1)}, f32[16,512]{1,0:T(8,128)S(1)}, f32[16,512...) custom-call(bf16[128,512]{1,0:T(8,128)(2,1)} %refs_0_.1, ...), custom_call_target="tpu_custom_call" | custom-call | bytes 217088 | tf_op jit(solution)/shard_map/pallas_call | solution.py:21
  1.3 9.5 %all_to_all.15.refs_0_ = f32[8,1,128]{2,1,0:T(1,128)S(1)} all-to-all(f32[8,1,128]{2,1,0:T(1,128)S(1)} %get-tuple-element.23), channel_id=1, replica_groups=mesh['ctx'=64,'ch'=8] {'ch'}, dimensions={0} | all-to-all | bytes 8192 | tf_op jit(solution)/shard_map/all_to_all | solution.py:292
  10.8 1.0 %shard_map.56 = (bf16[128,512]{1,0:T(8,128)(2,1)S(1)}, f32[128,512]{1,0:T(8,128)S(1)}, f32[4,80,128]{2,1,0:T(8,128)S(1)}) custom-call(f32[8,1,128]{2,1,0:T(1,128)S(1)} %all_to_all.15.refs_0_, bf16[128,512]{1,0:T(8,128)(2,1)S(1)} %get-tuple-element.24.refs_1_, f32[1,512]{1,0:T(1,128)S(1)} %get-tuple-element.25.refs_2_, ...), custom_call_target="tpu_custom_call" | custom-call | bytes 188416 | tf_op jit(solution)/shard_map/pallas_call | solution.py:21
  11.9 11.0 %all_to_all.16.refs_0_.near_ref = f32[4,80,128]{2,1,0:T(8,128)S(1)} all-to-all(f32[4,80,128]{2,1,0:T(8,128)S(1)} %get-tuple-element.28), channel_id=1, replica_groups={{0,8,16,24},{32,40,48,56},{64,72,80,88},{96,104,112,120},{128,136,144,1..., dimensions={0} | all-to-all | bytes 327680 | tf_op jit(solution)/shard_map/all_to_all | solution.py:292
  22.9 0.1 shard_map.57
  23.0 10.7 %all_to_all.17.refs_0_.far_ref = f32[4,80,128]{2,1,0:T(8,128)S(1)} all-to-all(f32[4,80,128]{2,1,0:T(8,128)S(1)} %get-tuple-element.32), channel_id=1, replica_groups={{0,32,64,96},{8,40,72,104},{16,48,80,112},{24,56,88,120},{128,160,192,2..., dimensions={0} | all-to-all | bytes 327680 | tf_op jit(solution)/shard_map/all_to_all | solution.py:292
  33.7 0.1 shard_map.58
  33.7 9.1 %collective-permute-start = (f32[80,128]{1,0:T(8,128)S(1)}, f32[80,128]{1,0:T(8,128)S(1)}, u32[]{:S(2)}, u32[]{:S(2)}) collective-permute-start(f32[80,128]{1,0:T(8,128)S(1)} %bitcast.4), channel_id=1, source_target_pairs={{0,128},{8,136},{16,144},{24,152},{32,160},{40,168},{48,176},{56,1... | collective-permute-start | bytes 122888 | tf_op jit(solution)/shard_map/ppermute | solution.py:335
  42.8 3.3 %collective-permute-done.refs_0_.swap_ref = f32[80,128]{1,0:T(8,128)S(1)} collective-permute-done((f32[80,128]{1,0:T(8,128)S(1)}, f32[80,128]{1,0:T(8,128)S(1)}, u32[]{:S(2)}, u32[]{:S(2)}) %collective-permute-start) | collective-permute-done | bytes 40992 | tf_op jit(solution)/shard_map/ppermute | solution.py:335
  46.2 1.3 %collective-permute-start.1 = (f32[88,128]{1,0:T(8,128)S(1)}, f32[88,128]{1,0:T(8,128)S(1)}, u32[]{:S(2)}, u32[]{:S(2)}) collective-permute-start(f32[88,128]{1,0:T(8,128)S(1)} %shard_map.59), channel_id=1, source_target_pairs={{0,384},{8,392},{16,400},{24,408},{32,416},{40,424},{48,432},{56,4... | collective-permute-start | bytes 135176 | tf_op jit(solution)/shard_map/ppermute | solution.py:343
  47.5 0.7 %collective-permute-start.2 = (f32[80,128]{1,0:T(8,128)S(1)}, f32[80,128]{1,0:T(8,128)S(1)}, u32[]{:S(2)}, u32[]{:S(2)}) collective-permute-start(f32[80,128]{1,0:T(8,128)S(1)} %bitcast.5), channel_id=1, source_target_pairs={{256,384},{264,392},{272,400},{280,408},{288,416},{296,424},{304,4... | collective-permute-start | bytes 122888 | tf_op jit(solution)/shard_map/ppermute | solution.py:342
  48.1 1.6 %shard_map.60.local_ref = f32[128,512]{1,0:T(8,128)S(1)} custom-call(f32[16,512]{1,0:T(8,128)S(1)} %get-tuple-element.27.refs_4_.rate_ref, f32[16,512]{1,0:T(8,128)S(1)} %get-tuple-element.38.residue_ref, f32[128,512]{1,0:T(8,128)S(1)} %get-tuple-element.39.product_ref, f32[64,128]{1,0:T(8,128)S(1)} %get-tuple-element.33.after_ref.far_before), custom_call_target="tpu_custom_call" | custom-call | flops 10000000 | bytes 360448 | tf_op jit(solution)/shard_map/pallas_call | solution.py:21
  49.8 0.0 collective-permute-done.2.third_ref
  49.8 0.1 collective-permute-done.1.two_ref
  49.9 1.2 %shard_map.61 = bf16[128,512]{1,0:T(8,128)(2,1)} custom-call(f32[4,80,128]{2,1,0:T(8,128)S(1)} %all_to_all.16.refs_0_.near_ref, f32[64,128]{1,0:T(8,128)S(1)} %get-tuple-element.31.near_before, f32[4,80,128]{2,1,0:T(8,128)S(1)} %all_to_all.17.refs_0_.far_ref, f32[64,128]{1,0:T(8,128)S(1)} %get-tuple-element.33.after_ref.far_before, ...), custom_call_target="tpu_custom_call" | custom-call | bytes 1030144 | tf_op jit(solution)/shard_map/pallas_call | solution.py:21
  (1 shorter events, 0.0 us)
Async XLA Ops:
  33.7 12.4 %collective-permute-start = (f32[80,128]{1,0:T(8,128)S(1)}, f32[80,128]{1,0:T(8,128)S(1)}, u32[]{:S(2)}, u32[]{:S(2)}) collective-permute-start(f32[80,128]{1,0:T(8,128)S(1)} %bitcast.4), channel_id=1, source_target_pairs={{0,128},{8,136},{16,144},{24,152},{32,160},{40,168},{48,176},{56,1... | collective-permute-start | bytes 122888 | tf_op jit(solution)/shard_map/ppermute | solution.py:335
  46.2 3.7 %collective-permute-start.1 = (f32[88,128]{1,0:T(8,128)S(1)}, f32[88,128]{1,0:T(8,128)S(1)}, u32[]{:S(2)}, u32[]{:S(2)}) collective-permute-start(f32[88,128]{1,0:T(8,128)S(1)} %shard_map.59), channel_id=1, source_target_pairs={{0,384},{8,392},{16,400},{24,408},{32,416},{40,424},{48,432},{56,4... | collective-permute-start | bytes 135176 | tf_op jit(solution)/shard_map/ppermute | solution.py:343
  47.5 2.3 %collective-permute-start.2 = (f32[80,128]{1,0:T(8,128)S(1)}, f32[80,128]{1,0:T(8,128)S(1)}, u32[]{:S(2)}, u32[]{:S(2)}) collective-permute-start(f32[80,128]{1,0:T(8,128)S(1)} %bitcast.5), channel_id=1, source_target_pairs={{256,384},{264,392},{272,400},{280,408},{288,416},{296,424},{304,4... | collective-permute-start | bytes 122888 | tf_op jit(solution)/shard_map/ppermute | solution.py:342

commit v6 on v5

--- a/solution.py
+++ b/solution.py
@@ -9,22 +9,25 @@
 EPSILON = 1e-05
 SUB = 8
 LANES = 128
-NEAR = 4
+NEAR = 16
 
 F32 = jnp.float32
 BF16 = jnp.bfloat16
 
 
-def call(body, outs, *args, scratch=(), flops=0, space=pltpu.VMEM, grant=16):
+def call(body, outs, *args, scratch=(), flops=0, space=pltpu.VMEM, in_hbm=(), out_hbm=(), aliases=None):
     shapes = [jax.ShapeDtypeStruct(s, d) for s, d in outs]
+    spaces = [pltpu.HBM if i in in_hbm else space for i in range(len(args))]
+    out_spaces = [pltpu.HBM if i in out_hbm else pltpu.VMEM for i in range(len(outs))]
     moved = sum(a.size * a.dtype.itemsize for a in args)
     return pl.pallas_call(
         body,
         out_shape=shapes,
-        in_specs=[pl.BlockSpec(memory_space=space)] * len(args),
-        out_specs=[pl.BlockSpec(memory_space=pltpu.VMEM)] * len(shapes),
+        in_specs=[pl.BlockSpec(memory_space=m) for m in spaces],
+        out_specs=[pl.BlockSpec(memory_space=m) for m in out_spaces],
         scratch_shapes=list(scratch),
-        compiler_params=pltpu.CompilerParams(vmem_limit_bytes=grant * 2**20),
+        input_output_aliases=aliases or {},
+        compiler_params=pltpu.CompilerParams(vmem_limit_bytes=16 * 2**20),
         cost_estimate=pl.CostEstimate(flops=flops, bytes_accessed=moved, transcendentals=0),
     )(*args)
 
@@ -59,7 +62,7 @@
                 taps_pack[pl.ds((tap * 3 + role) * lanes + l, 1), :] = taps_ref[tap, pl.ds(role, 1), pl.ds(l * LANES, LANES)]
 
 
-def block_states(chan_total, sums_ref, stream_ref, gain_ref, taps_ref, rate_ref, query_ref, product_ref, message_ref, normed_ref, end_ref):
+def block_states(chan_total, sums_ref, stream_ref, gain_ref, taps_ref, rate_ref, query_ref, product_ref, message_ref, normed_ref, end_ref, whole_ref):
     count, chans = stream_ref.shape
     lanes = chans // LANES
     modes = rate_ref.shape[0]
@@ -100,12 +103,12 @@
         return carry
 
     lax.fori_loop(0, lanes, one_lane, 0)
-    message_ref[0, : lanes * modes] = pack(end_ref)
+    whole_ref[: lanes * modes] = pack(end_ref)
     for e, place in enumerate((0, 1, count - 2, count - 1)):
         for l in range(lanes):
-            message_ref[0, pl.ds(lanes * (modes + e) + l, 1), :] = normed_ref[pl.ds(SUB + place, 1), pl.ds(l * LANES, LANES)]
-    message = message_ref[0]
-    for peer in range(1, message_ref.shape[0]):
+            whole_ref[pl.ds(lanes * (modes + e) + l, 1), :] = normed_ref[pl.ds(SUB + place, 1), pl.ds(l * LANES, LANES)]
+    message = whole_ref[...].astype(BF16)
+    for peer in range(message_ref.shape[0]):
         message_ref[peer] = message
 
 
@@ -130,50 +133,51 @@
     return ref[start : start + lanes], ref[start + lanes : start + 2 * lanes]
 
 
-def step_over(block, lanes, rates, taps_ref, state, last, run_ref):
+def step_over(block, lanes, rates, taps_ref, state, last, run):
     states = rates.shape[0]
     modes = states // lanes
-    first, second = first_products(taps_ref, last, pairs(run_ref, states, lanes))
-    end = run_ref[:states] + state * jnp.exp(-block * rates)
+    first, second = first_products(taps_ref, last, pairs(run, states, lanes))
+    end = run[:states] + state * jnp.exp(-block * rates)
     end = end + jnp.exp(-(block - 1) * rates) * spread(first, modes) + jnp.exp(-(block - 2) * rates) * spread(second, modes)
-    return end, pairs(run_ref, states + 2 * lanes, lanes)
+    return end, pairs(run, states + 2 * lanes, lanes)
 
 
 def step_into(block, lanes, place, rates, taps_ref, state, last, got_ref, before_ref):
     states = rates.shape[0]
     modes = states // lanes
-    first, second = first_products(taps_ref, last, pairs(got_ref.at[0], states, lanes))
+    first, second = first_products(taps_ref, last, pairs(got_ref[0].astype(F32), states, lanes))
     lag = (block * place).astype(F32)
     held = jnp.exp(-rates * jnp.maximum(lag - 1.0, 0.0)) * spread(first, modes)
     held = held + jnp.exp(-rates * jnp.maximum(lag - 2.0, 0.0)) * spread(second, modes)
     state = before_ref[...] + state * jnp.exp(-rates * lag) + jnp.where(place > 0, held, 0.0)
-    inside = pairs(got_ref.at[jnp.maximum(place - 1, 0)], states + 2 * lanes, lanes)
+    inside = pairs(got_ref[jnp.maximum(place - 1, 0)].astype(F32), states + 2 * lanes, lanes)
     return state, [jnp.where(place > 0, a, b) for a, b in zip(inside, last)]
 
 
-def near_scan(block, lanes, place, got_ref, rate_ref, taps_ref, before_ref, message_ref):
+def near_scan(block, lanes, got_ref, rate_ref, taps_ref, before_ref, message_ref):
+    place, _ = places()
     states = rate_ref.shape[0]
     rates = rate_ref[...]
-    total, last = got_ref[0, :states], pairs(got_ref.at[0], states + 2 * lanes, lanes)
-    before = jnp.where(place() == 1, total, jnp.zeros_like(total))
+    run = got_ref[0].astype(F32)
+    head = run[states : states + 2 * lanes]
+    total, last = run[:states], pairs(run, states + 2 * lanes, lanes)
+    before = jnp.where(place == 1, total, jnp.zeros_like(total))
     for j in range(1, NEAR):
-        total, last = step_over(block, lanes, rates, taps_ref, total, last, got_ref.at[j])
+        total, last = step_over(block, lanes, rates, taps_ref, total, last, got_ref[j].astype(F32))
         if j < NEAR - 1:
-            before = jnp.where(place() == j + 1, total, before)
+            before = jnp.where(place == j + 1, total, before)
     before_ref[...] = before
-    head = got_ref[0, states : states + 2 * lanes]
-    tail = got_ref[NEAR - 1, states + 2 * lanes :]
-    for peer in range(message_ref.shape[0]):
-        message_ref[peer, :states] = total
-        message_ref[peer, states : states + 2 * lanes] = head
-        message_ref[peer, states + 2 * lanes :] = tail
-
-
-def relay(block, lanes, came_ref, own_ref, rate_ref, taps_ref, out_ref):
+    message_ref[:states] = total
+    message_ref[states : states + 2 * lanes] = head
+    message_ref[states + 2 * lanes : states + 3 * lanes] = last[0]
+    message_ref[states + 3 * lanes :] = last[1]
+
+
+def relay(block, lanes, came_ref, own_ref, rate_ref, taps_ref, after_ref, out_ref):
     rates = rate_ref[...]
     states = rates.shape[0]
-    low = places()[2] == 0
-    own, came = own_ref[0], came_ref[...]
+    low = places()[1] == 0
+    own, came = own_ref[...], came_ref[...]
     state, last = jnp.zeros_like(rates), [jnp.zeros((lanes, LANES), F32)] * 2
     for run in (jnp.where(low, own, came), jnp.where(low, came, own)):
         state, last = step_over(block, lanes, rates, taps_ref, state, last, run)
@@ -193,7 +197,7 @@
     return out
 
 
-def inner_conv(rate_ref, residue_ref, product_ref, after_ref, local_ref, filter_ref):
+def inner_conv(rate_ref, residue_ref, product_ref, local_ref, filter_ref):
     count, chans = product_ref.shape
     modes = rate_ref.shape[0]
     blocks = count // SUB
@@ -228,23 +232,16 @@
     lax.fori_loop(0, chans // LANES, one_lane, 0)
 
 
-def outer_conv(near_ref, near_before, far_ref, far_before, swap_ref, two_ref, third_ref, rate_pack, residue_pack, taps_ref, rate_ref, local_ref, query_ref, mixed_ref, state_ref):
+def finish(state, last, got_ref, before_ref, rate_pack, residue_pack, taps_ref, rate_ref, query_ref, local_ref, mixed_ref, state_ref):
     count, chans = local_ref.shape
     lanes = chans // LANES
     modes = rate_ref.shape[0]
     states = lanes * modes
     blocks = count // SUB
-    place, level, group = places()
+    place, _ = places()
     rates = rate_pack[...]
-    came = two_ref[...]
-    state, last = came[:states], (came[states : states + lanes], came[states + lanes : states + 2 * lanes])
-    run = jnp.where(group == 1, swap_ref[...], third_ref[...])
-    after, after_last = step_over(count * NEAR * NEAR, lanes, rates, taps_ref, state, last, run)
-    odd = group % 2 == 1
-    state, last = jnp.where(odd, after, state), [jnp.where(odd, a, b) for a, b in zip(after_last, last)]
-    state, last = step_into(count * NEAR, lanes, level, rates, taps_ref, state, last, far_ref, far_before)
-    state, own_last = step_into(count, lanes, place, rates, taps_ref, state, last, near_ref, near_before)
-    own_head = pairs(near_ref.at[place], states, lanes)
+    state, own_last = step_into(count, lanes, place, rates, taps_ref, state, last, got_ref, before_ref)
+    own_head = pairs(got_ref[place].astype(F32), states, lanes)
     own_query = [q.astype(BF16).astype(F32) for q in first_rows(taps_ref, 0, own_last, own_head)]
     first, second = first_products(taps_ref, own_last, own_head)
     ahead = jnp.exp(rates) * spread(second, modes)
@@ -283,9 +280,52 @@
     lax.fori_loop(0, lanes, one_lane, 0)
 
 
+def early(got_ref, before_ref, rate_pack, residue_pack, taps_ref, rate_ref, query_ref, residue_ref, product_ref, local_ref, out_ref, filter_ref, state_ref, mixed_ref, sem):
+    _, group = places()
+
+    @pl.when(group < 2)
+    def _():
+        inner_conv(rate_ref, residue_ref, product_ref, local_ref, filter_ref)
+
+    @pl.when(group == 0)
+    def _():
+        nothing = jnp.zeros(rate_pack.shape, F32)
+        last = [jnp.zeros((taps_ref.shape[0] // 9, LANES), F32)] * 2
+        finish(nothing, last, got_ref, before_ref, rate_pack, residue_pack, taps_ref, rate_ref, query_ref, local_ref, mixed_ref, state_ref)
+        copy = pltpu.make_async_copy(mixed_ref, out_ref, sem)
+        copy.start()
+        copy.wait()
+
+
+def later(rate_ref, residue_ref, product_ref, after_ref, held_ref, local_ref, filter_ref):
+    @pl.when(places()[1] >= 2)
+    def _():
+        inner_conv(rate_ref, residue_ref, product_ref, local_ref, filter_ref)
+
+
+def final(got_ref, before_ref, rate_pack, residue_pack, taps_ref, rate_ref, query_ref, local_ref, swap_ref, two_ref, third_ref, held_ref, out_ref, state_ref, mixed_ref, sem):
+    _, group = places()
+    block = local_ref.shape[0] * NEAR
+    states = rate_pack.shape[0]
+    lanes = taps_ref.shape[0] // 9
+
+    @pl.when(group > 0)
+    def _():
+        came = two_ref[...]
+        state, last = came[:states], (came[states : states + lanes], came[states + lanes : states + 2 * lanes])
+        run = jnp.where(group == 1, swap_ref[...], third_ref[...])
+        after, after_last = step_over(block, lanes, rate_pack[...], taps_ref, state, last, run)
+        odd = group % 2 == 1
+        state, last = jnp.where(odd, after, state), [jnp.where(odd, a, b) for a, b in zip(after_last, last)]
+        finish(state, last, got_ref, before_ref, rate_pack, residue_pack, taps_ref, rate_ref, query_ref, local_ref, mixed_ref, state_ref)
+        copy = pltpu.make_async_copy(mixed_ref, out_ref, sem)
+        copy.start()
+        copy.wait()
+
+
 def places():
     index = lax.axis_index("ctx")
-    return index % NEAR, index // NEAR % NEAR, index // NEAR**2
+    return index % NEAR, index // NEAR
 
 
 def gather(copies, axis, groups=None):
@@ -299,9 +339,7 @@
     states = lanes * modes
     peers = lax.axis_size("ch")
     ctx = lax.axis_size("ctx")
-    runs = [[r + m for m in range(NEAR)] for r in range(0, ctx, NEAR)]
-    columns = [[g + m + NEAR * r for r in range(NEAR)] for g in range(0, ctx, NEAR**2) for m in range(NEAR)]
-    groups = [[g + m for m in range(NEAR**2)] for g in range(0, ctx, NEAR**2)]
+    groups = [[g + m for m in range(NEAR)] for g in range(0, ctx, NEAR)]
 
     held = [stream, norm_gain[None, :], short_filter, decay_rate.T, residue.T]
     held = [pltpu.with_memory_space_constraint(h, pltpu.HBM) for h in held]
@@ -316,40 +354,43 @@
     sums = gather(sums, "ch")
     query, product, message = call(
         lambda *refs: block_states(chans * peers, *refs),
-        [((count, chans), BF16), ((count, chans), F32), ((NEAR, states + 4 * lanes, LANES), F32)],
+        [((count, chans), BF16), ((count, chans), F32), ((NEAR, states + 4 * lanes, LANES), BF16)],
         sums, stream, gain, taps, rates,
-        scratch=[pltpu.VMEM((SUB + count, chans), F32), pltpu.VMEM((modes, chans), F32)],
-    )
-    shapes = [((states, LANES), F32), ((NEAR, states + 4 * lanes, LANES), F32)]
-    near = gather(message, "ctx", runs)
+        scratch=[pltpu.VMEM((SUB + count, chans), F32), pltpu.VMEM((modes, chans), F32), pltpu.VMEM((states + 4 * lanes, LANES), F32)],
+    )
+    near = gather(message, "ctx", groups)
     near_before, message = call(
-        lambda *refs: near_scan(count, lanes, lambda: places()[0], *refs), shapes, near, rate_pack, taps_pack
-    )
-    far = gather(message, "ctx", columns)
-    far_before, message = call(
-        lambda *refs: near_scan(count * NEAR, lanes, lambda: places()[1], *refs),
-        [shapes[0], ((1,) + shapes[1][0][1:], F32)],
-        far, rate_pack, taps_pack,
+        lambda *refs: near_scan(count, lanes, *refs),
+        [((states, LANES), F32), ((states + 4 * lanes, LANES), F32)],
+        near, rate_pack, taps_pack,
     )
     hops = lambda *ends: [pair for a, b in ends for pair in zip(groups[a], groups[b])]
-    swap = lax.ppermute(message[0], "ctx", hops((0, 1), (1, 0)))
+    swap = lax.ppermute(message, "ctx", hops((0, 1), (1, 0)))
+    common = [near, near_before, rate_pack, residue_pack, taps_pack, rates, query]
+    work = [pltpu.VMEM((modes + 2 * SUB, chans), F32), pltpu.VMEM((count, chans), BF16), pltpu.SemaphoreType.DMA]
+    local, mixed = call(
+        early,
+        [((count, chans), F32), ((count, chans), BF16)],
+        *common, weights, product,
+        scratch=[pltpu.VMEM((count, LANES), F32)] + work, flops=10**7, out_hbm=(1,),
+    )
     (two,) = call(
-        lambda *refs: relay(count * NEAR**2, lanes, *refs),
+        lambda *refs: relay(count * NEAR, lanes, *refs),
         [((states + 6 * lanes, LANES), F32)],
-        swap, message, rate_pack, taps_pack,
-    )
-    third, two = lax.optimization_barrier((message[0], two))
+        swap, message, rate_pack, taps_pack, local,
+    )
+    third, relayed = lax.optimization_barrier((message, two))
     third = lax.ppermute(third, "ctx", hops((2, 3)))
-    two = lax.ppermute(two, "ctx", hops((0, 3), (1, 2)))
+    two = lax.ppermute(relayed, "ctx", hops((0, 3), (1, 2)))
     (local,) = call(
-        inner_conv, [((count, chans), F32)], rates, weights, product, far_before,
-        scratch=[pltpu.VMEM((count, LANES), F32)], flops=10**7,
+        later, [((count, chans), F32)], rates, weights, product, relayed, local,
+        scratch=[pltpu.VMEM((count, LANES), F32)], flops=10**7, aliases={4: 0},
     )
     (mixed,) = call(
-        outer_conv,
+        final,
         [((count, chans), BF16)],
-        near, near_before, far, far_before, swap, two, third, rate_pack, residue_pack, taps_pack, rates, local, query,
-        scratch=[pltpu.VMEM((modes + 2 * SUB, chans), F32)],
+        *common, local, swap, two, third, mixed,
+        scratch=work, in_hbm=(11,), out_hbm=(0,), aliases={11: 0},
     )
     return mixed
 

time: 51.3 us -> 48 us (0.936)
  the two profiles are of different devices: /device:TPU:2 before, /device:TPU:8 now
where the time goes in v6:
time: 48 us; the launch traced here: 47.8 us
  blocking collectives  28.6 us (60%)
  starting transfers between devices  11 us (23%)
  Pallas kernels  5.48 us (11%)
  waiting for transfers between devices  2.55 us (5%)
    all_to_all x2, blocking collectives, gather(): lax.all_to_all(copies, axis, 0, 0, tiled=True, axis_index_groups=groups)  28.6 us
    ppermute x1, starting transfers between devices, per_device(): swap = lax.ppermute(message, 'ctx', hops((0, 1), (1, 0)))  9.09 us
    pallas_call x7, Pallas kernels, call(): pl.pallas_call(body, out_shape=shapes, in_specs=[pl.BlockSpec(memory_spac...  5.48 us
    ppermute x1, waiting for transfers between devices, per_device(): two = lax.ppermute(relayed, 'ctx', hops((0, 3), (1, 2)))  2.03 us
    ppermute x1, starting transfers between devices, per_device(): two = lax.ppermute(relayed, 'ctx', hops((0, 3), (1, 2)))  1.29 us
  transfers between devices with their start and end apart: 3, of which 2 were waited for; matrix products, arithmetic and copies ran while one was open for 0% of the time, Pallas kernels for 6%

profile of v6, /device:TPU:8, one launch (start us, length us, event | category | flops | bytes accessed | tf_op | source)
XLA Modules:
  0.0 47.8 jit_solution(5396089349672818340)
XLA Ops:
  0.0 1.3 %shard_map.55 = (bf16[128,512]{1,0:T(8,128)(2,1)S(1)}, f32[1,512]{1,0:T(1,128)S(1)}, f32[3,3,512]{2,1,0:T(4,128)S(1)}, f32[16,512]{1,0:T(8,128)S(1)}, f32[16,512...) custom-call(bf16[128,512]{1,0:T(8,128)(2,1)} %refs_0_.1, ...), custom_call_target="tpu_custom_call" | custom-call | bytes 217088 | tf_op jit(solution)/shard_map/pallas_call | solution.py:23
  1.3 12.0 %all_to_all.10.refs_0_ = f32[8,1,128]{2,1,0:T(1,128)S(1)} all-to-all(f32[8,1,128]{2,1,0:T(1,128)S(1)} %get-tuple-element.23), channel_id=1, replica_groups=mesh['ctx'=64,'ch'=8] {'ch'}, dimensions={0} | all-to-all | bytes 8192 | tf_op jit(solution)/shard_map/all_to_all | solution.py:332
  13.3 1.1 %shard_map.56 = (bf16[128,512]{1,0:T(8,128)(2,1)S(1)}, f32[128,512]{1,0:T(8,128)S(1)}, bf16[16,80,128]{2,1,0:T(8,128)(2,1)S(1)}) custom-call(f32[8,1,128]{2,1,0:T(1,128)S(1)} %all_to_all.10.refs_0_, bf16[128,512]{1,0:T(8,128)(2,1)S(1)} %get-tuple-element.24.refs_1_, f32[1,512]{1,0:T(1,128)S(1)} %get-tuple-element.25.refs_2_, ...), custom_call_target="tpu_custom_call" | custom-call | bytes 188416 | tf_op jit(solution)/shard_map/pallas_call | solution.py:23
  14.4 16.6 %all_to_all.11.refs_0_.got_ref = bf16[16,80,128]{2,1,0:T(8,128)(2,1)S(1)} all-to-all(bf16[16,80,128]{2,1,0:T(8,128)(2,1)S(1)} %get-tuple-element.28), channel_id=1, replica_groups={{0,8,16,24,32,40,48,56,64,72,80,88,96,104,112,120},{128,136,144,152,160..., dimensions={0} | all-to-all | bytes 655360 | tf_op jit(solution)/shard_map/all_to_all | solution.py:332
  31.0 0.3 shard_map.57
  31.3 9.1 %collective-permute-start = (f32[80,128]{1,0:T(8,128)S(1)}, f32[80,128]{1,0:T(8,128)S(1)}, u32[]{:S(2)}, u32[]{:S(2)}) collective-permute-start(f32[80,128]{1,0:T(8,128)S(1)} %get-tuple-element.39.refs_1_), channel_id=1, source_target_pairs={{0,128},{8,136},{16,144},{24,152},{32,160},{40,168},{48,176},{56,1... | collective-permute-start | bytes 122888 | tf_op jit(solution)/shard_map/ppermute | solution.py:368
  40.4 2.8 %shard_map.58 = (f32[128,512]{1,0:T(8,128)S(1)}, bf16[128,512]{1,0:T(8,128)(2,1)}) custom-call(bf16[16,80,128]{2,1,0:T(8,128)(2,1)S(1)} %all_to_all.11.refs_0_.got_ref, f32[64,128]{1,0:T(8,128)S(1)} %get-tuple-element.31.before_ref, f32[64,128]{1,0:T(8,128)S(1)} %get-tuple-element.29.refs_1_.rate_pack.refs_2_, f32[64,128]{1,0:T(8,128)S(1)} %get-tuple-element.32.residue_pack, ...), custom_call_target="tpu_custom_call" | custom-call | flops 10000000 | bytes 903168 | tf_op jit(solution)/shard_map/pallas_call | solution.py:23
  43.1 0.5 %collective-permute-done.refs_0_.swap_ref = f32[80,128]{1,0:T(8,128)S(1)} collective-permute-done((f32[80,128]{1,0:T(8,128)S(1)}, f32[80,128]{1,0:T(8,128)S(1)}, u32[]{:S(2)}, u32[]{:S(2)}) %collective-permute-start) | collective-permute-done | bytes 40992 | tf_op jit(solution)/shard_map/ppermute | solution.py:368
  43.7 1.3 %collective-permute-start.1 = (f32[88,128]{1,0:T(8,128)S(1)}, f32[88,128]{1,0:T(8,128)S(1)}, u32[]{:S(2)}, u32[]{:S(2)}) collective-permute-start(f32[88,128]{1,0:T(8,128)S(1)} %shard_map.59.after_ref), channel_id=1, source_target_pairs={{0,384},{8,392},{16,400},{24,408},{32,416},{40,424},{48,432},{56,4... | collective-permute-start | bytes 135176 | tf_op jit(solution)/shard_map/ppermute | solution.py:384
  45.0 0.7 %collective-permute-start.2 = (f32[80,128]{1,0:T(8,128)S(1)}, f32[80,128]{1,0:T(8,128)S(1)}, u32[]{:S(2)}, u32[]{:S(2)}) collective-permute-start(f32[80,128]{1,0:T(8,128)S(1)} %get-tuple-element.39.refs_1_), channel_id=1, source_target_pairs={{256,384},{264,392},{272,400},{280,408},{288,416},{296,424},{304,4... | collective-permute-start | bytes 122888 | tf_op jit(solution)/shard_map/ppermute | solution.py:383
  45.7 0.0 collective-permute-done.2.third_ref
  45.7 2.0 %collective-permute-done.1.two_ref = f32[88,128]{1,0:T(8,128)S(1)} collective-permute-done((f32[88,128]{1,0:T(8,128)S(1)}, f32[88,128]{1,0:T(8,128)S(1)}, u32[]{:S(2)}, u32[]{:S(2)}) %collective-permute-start.1) | collective-permute-done | bytes 45088 | tf_op jit(solution)/shard_map/ppermute | solution.py:384
  (3 shorter events, 0.1 us)
Async XLA Ops:
  31.3 12.4 %collective-permute-start = (f32[80,128]{1,0:T(8,128)S(1)}, f32[80,128]{1,0:T(8,128)S(1)}, u32[]{:S(2)}, u32[]{:S(2)}) collective-permute-start(f32[80,128]{1,0:T(8,128)S(1)} %get-tuple-element.39.refs_1_), channel_id=1, source_target_pairs={{0,128},{8,136},{16,144},{24,152},{32,160},{40,168},{48,176},{56,1... | collective-permute-start | bytes 122888 | tf_op jit(solution)/shard_map/ppermute | solution.py:368
  43.7 4.0 %collective-permute-start.1 = (f32[88,128]{1,0:T(8,128)S(1)}, f32[88,128]{1,0:T(8,128)S(1)}, u32[]{:S(2)}, u32[]{:S(2)}) collective-permute-start(f32[88,128]{1,0:T(8,128)S(1)} %shard_map.59.after_ref), channel_id=1, source_target_pairs={{0,384},{8,392},{16,400},{24,408},{32,416},{40,424},{48,432},{56,4... | collective-permute-start | bytes 135176 | tf_op jit(solution)/shard_map/ppermute | solution.py:384
  45.0 0.7 %collective-permute-start.2 = (f32[80,128]{1,0:T(8,128)S(1)}, f32[80,128]{1,0:T(8,128)S(1)}, u32[]{:S(2)}, u32[]{:S(2)}) collective-permute-start(f32[80,128]{1,0:T(8,128)S(1)} %get-tuple-element.39.refs_1_), channel_id=1, source_target_pairs={{256,384},{264,392},{272,400},{280,408},{288,416},{296,424},{304,4... | collective-permute-start | bytes 122888 | tf_op jit(solution)/shard_map/ppermute | solution.py:383

commit v7 on v6

--- a/solution.py
+++ b/solution.py
@@ -36,6 +36,14 @@
     return jnp.concatenate([ref[:, l * LANES : (l + 1) * LANES] for l in range(ref.shape[1] // LANES)], axis=0)
 
 
+def exact_parts(values, count):
+    parts = []
+    for _ in range(count):
+        parts.append(values.astype(BF16))
+        values = values - parts[-1].astype(F32)
+    return parts
+
+
 def square_sums(*refs):
     count = 5
     held, refs = refs[:count], refs[count:]
@@ -48,9 +56,9 @@
         copy.wait()
     chans = stream_ref.shape[1]
     values = stream_ref[...].astype(F32)
-    sums = lax.dot_general(
-        jnp.ones((SUB, chans), F32), values * values, (((1,), (1,)), ((), ())), precision=EXACT, preferred_element_type=F32
-    )
+    sums = jnp.zeros((SUB, values.shape[0]), F32)
+    for part in exact_parts(values * values, 2):
+        sums = sums + lax.dot_general(jnp.ones((SUB, chans), BF16), part, (((1,), (1,)), ((), ())), preferred_element_type=F32)
     for peer in range(sums_ref.shape[0]):
         sums_ref[peer] = sums[:1]
     rate_pack[...] = pack(rate_ref)
@@ -69,11 +77,13 @@
     sums = sums_ref[0]
     for peer in range(1, sums_ref.shape[0]):
         sums = sums + sums_ref[peer]
-    sums = jnp.broadcast_to(sums, (SUB, count))
-    mean_square = lax.dot_general(
-        sums, jnp.ones((SUB, chans), F32) / SUB, (((0,), (0,)), ((), ())), precision=EXACT, preferred_element_type=F32
-    ) / chan_total
-    values = stream_ref[...].astype(F32) * lax.rsqrt(mean_square + EPSILON) * gain_ref[...]
+    scale = lax.rsqrt(sums / chan_total + EPSILON)
+    parts = exact_parts(jnp.broadcast_to(scale, (2 * SUB, count)), 3)
+    ones = jnp.full((2 * SUB, chans), 1.0 / (2 * SUB), BF16)
+    scale = jnp.zeros((count, chans), F32)
+    for part in parts:
+        scale = scale + lax.dot_general(part, ones, (((0,), (0,)), ((), ())), preferred_element_type=F32)
+    values = stream_ref[...].astype(F32) * scale * gain_ref[...]
     normed_ref[:SUB] = jnp.zeros((SUB, chans), F32)
     normed_ref[SUB:] = values.astype(BF16).astype(F32)
     shifted = [normed_ref[SUB - j : SUB - j + count] for j in range(3)]
@@ -167,25 +177,19 @@
         if j < NEAR - 1:
             before = jnp.where(place == j + 1, total, before)
     before_ref[...] = before
-    message_ref[:states] = total
-    message_ref[states : states + 2 * lanes] = head
-    message_ref[states + 2 * lanes : states + 3 * lanes] = last[0]
-    message_ref[states + 3 * lanes :] = last[1]
+    message_ref[...] = jnp.concatenate([total, head, *last], axis=0).astype(BF16)
 
 
 def relay(block, lanes, came_ref, own_ref, rate_ref, taps_ref, after_ref, out_ref):
     rates = rate_ref[...]
     states = rates.shape[0]
     low = places()[1] == 0
-    own, came = own_ref[...], came_ref[...]
+    own, came = own_ref[...].astype(F32), came_ref[...].astype(F32)
     state, last = jnp.zeros_like(rates), [jnp.zeros((lanes, LANES), F32)] * 2
     for run in (jnp.where(low, own, came), jnp.where(low, came, own)):
         state, last = step_over(block, lanes, rates, taps_ref, state, last, run)
-    out_ref[:states] = state
-    out_ref[pl.ds(states, lanes)] = last[0]
-    out_ref[pl.ds(states + lanes, lanes)] = last[1]
-    rest = states + 2 * lanes
-    out_ref[rest:] = jnp.zeros((out_ref.shape[0] - rest, LANES), F32)
+    rest = jnp.zeros((out_ref.shape[0] - states - 2 * lanes, LANES), F32)
+    out_ref[...] = jnp.concatenate([state, *last, rest], axis=0).astype(BF16)
 
 
 def add_mode(totals, term, rate):
@@ -311,9 +315,9 @@
 
     @pl.when(group > 0)
     def _():
-        came = two_ref[...]
+        came = two_ref[...].astype(F32)
         state, last = came[:states], (came[states : states + lanes], came[states + lanes : states + 2 * lanes])
-        run = jnp.where(group == 1, swap_ref[...], third_ref[...])
+        run = jnp.where(group == 1, swap_ref[...].astype(F32), third_ref[...].astype(F32))
         after, after_last = step_over(block, lanes, rate_pack[...], taps_ref, state, last, run)
         odd = group % 2 == 1
         state, last = jnp.where(odd, after, state), [jnp.where(odd, a, b) for a, b in zip(after_last, last)]
@@ -361,7 +365,7 @@
     near = gather(message, "ctx", groups)
     near_before, message = call(
         lambda *refs: near_scan(count, lanes, *refs),
-        [((states, LANES), F32), ((states + 4 * lanes, LANES), F32)],
+        [((states, LANES), F32), ((states + 4 * lanes, LANES), BF16)],
         near, rate_pack, taps_pack,
     )
     hops = lambda *ends: [pair for a, b in ends for pair in zip(groups[a], groups[b])]
@@ -376,7 +380,7 @@
     )
     (two,) = call(
         lambda *refs: relay(count * NEAR, lanes, *refs),
-        [((states + 6 * lanes, LANES), F32)],
+        [((states + 8 * lanes, LANES), BF16)],
         swap, message, rate_pack, taps_pack, local,
     )
     third, relayed = lax.optimization_barrier((message, two))

time: 48 us -> 46.1 us (0.960)
  waiting for transfers between devices: 2.55 us -> 0.79 us
    ppermute x1, waiting for transfers between devices: 2.03 us -> 0.79 us  [per_device(): two = lax.ppermute(relayed, 'ctx', hops((0, 3), (1, 2)))]
    ppermute x1, waiting for transfers between devices: 0.51 us -> 0.01 us  [per_device(): swap = lax.ppermute(message, 'ctx', hops((0, 1), (1, 0)))]
  transfers between devices with their start and end apart: 3 -> 3, of which waited for: 2 -> 1; matrix products, arithmetic and copies ran while one was open for 0% -> 0% of each run, Pallas kernels for 6% -> 6%
where the time goes in v7:
time: 46.1 us; the launch traced here: 45.8 us
  blocking collectives  28.6 us (62%)
  starting transfers between devices  11 us (24%)
  Pallas kernels  5.3 us (11%)
  waiting for transfers between devices  0.79 us (2%)
    all_to_all x2, blocking collectives, gather(): lax.all_to_all(copies, axis, 0, 0, tiled=True, axis_index_groups=groups)  28.6 us
    ppermute x1, starting transfers between devices, per_device(): swap = lax.ppermute(message, 'ctx', hops((0, 1), (1, 0)))  9.09 us
    pallas_call x7, Pallas kernels, call(): pl.pallas_call(body, out_shape=shapes, in_specs=[pl.BlockSpec(memory_spac...  5.3 us
    ppermute x1, starting transfers between devices, per_device(): two = lax.ppermute(relayed, 'ctx', hops((0, 3), (1, 2)))  1.29 us
  transfers between devices with their start and end apart: 3, of which 1 were waited for; matrix products, arithmetic and copies ran while one was open for 0% of the time, Pallas kernels for 6%

profile of v7, /device:TPU:8, one launch (start us, length us, event | category | flops | bytes accessed | tf_op | source)
XLA Modules:
  0.0 45.8 jit_solution(14467573458185510561)
XLA Ops:
  0.0 1.2 %shard_map.55 = (bf16[128,512]{1,0:T(8,128)(2,1)S(1)}, f32[1,512]{1,0:T(1,128)S(1)}, f32[3,3,512]{2,1,0:T(4,128)S(1)}, f32[16,512]{1,0:T(8,128)S(1)}, f32[16,512...) custom-call(bf16[128,512]{1,0:T(8,128)(2,1)} %refs_0_.1, ...), custom_call_target="tpu_custom_call" | custom-call | bytes 217088 | tf_op jit(solution)/shard_map/pallas_call | solution.py:23
  1.2 12.0 %all_to_all.10.refs_0_ = f32[8,1,128]{2,1,0:T(1,128)S(1)} all-to-all(f32[8,1,128]{2,1,0:T(1,128)S(1)} %get-tuple-element.23), channel_id=1, replica_groups=mesh['ctx'=64,'ch'=8] {'ch'}, dimensions={0} | all-to-all | bytes 8192 | tf_op jit(solution)/shard_map/all_to_all | solution.py:336
  13.2 1.0 %shard_map.56 = (bf16[128,512]{1,0:T(8,128)(2,1)S(1)}, f32[128,512]{1,0:T(8,128)S(1)}, bf16[16,80,128]{2,1,0:T(8,128)(2,1)S(1)}) custom-call(f32[8,1,128]{2,1,0:T(1,128)S(1)} %all_to_all.10.refs_0_, bf16[128,512]{1,0:T(8,128)(2,1)S(1)} %get-tuple-element.24.refs_1_, f32[1,512]{1,0:T(1,128)S(1)} %get-tuple-element.25.refs_2_, ...), custom_call_target="tpu_custom_call" | custom-call | bytes 188416 | tf_op jit(solution)/shard_map/pallas_call | solution.py:23
  14.2 16.6 %all_to_all.11.refs_0_.got_ref = bf16[16,80,128]{2,1,0:T(8,128)(2,1)S(1)} all-to-all(bf16[16,80,128]{2,1,0:T(8,128)(2,1)S(1)} %get-tuple-element.28), channel_id=1, replica_groups={{0,8,16,24,32,40,48,56,64,72,80,88,96,104,112,120},{128,136,144,152,160..., dimensions={0} | all-to-all | bytes 655360 | tf_op jit(solution)/shard_map/all_to_all | solution.py:336
  30.8 0.3 shard_map.57
  31.1 9.1 %collective-permute-start = (bf16[80,128]{1,0:T(8,128)(2,1)S(1)}, bf16[80,128]{1,0:T(8,128)(2,1)S(1)}, u32[]{:S(2)}, u32[]{:S(2)}) collective-permute-start(bf16[80,128]{1,0:T(8,128)(2,1)S(1)} %get-tuple-element.39.refs_1_), channel_id=1, source_target_pairs={{0,128},{8,136},{16,144},{24,152},{32,160},{40,168},{48,176},{56,1... | collective-permute-start | bytes 61448 | tf_op jit(solution)/shard_map/ppermute | solution.py:372
  40.2 2.8 %shard_map.58 = (f32[128,512]{1,0:T(8,128)S(1)}, bf16[128,512]{1,0:T(8,128)(2,1)}) custom-call(bf16[16,80,128]{2,1,0:T(8,128)(2,1)S(1)} %all_to_all.11.refs_0_.got_ref, f32[64,128]{1,0:T(8,128)S(1)} %get-tuple-element.31.before_ref, f32[64,128]{1,0:T(8,128)S(1)} %get-tuple-element.29.refs_1_.rate_pack.refs_2_, f32[64,128]{1,0:T(8,128)S(1)} %get-tuple-element.32.residue_pack, ...), custom_call_target="tpu_custom_call" | custom-call | flops 10000000 | bytes 903168 | tf_op jit(solution)/shard_map/pallas_call | solution.py:23
  43.0 0.0 collective-permute-done.refs_0_.swap_ref
  43.0 0.1 shard_map.59.after_ref
  43.0 1.3 %collective-permute-start.1 = (bf16[96,128]{1,0:T(8,128)(2,1)S(1)}, bf16[96,128]{1,0:T(8,128)(2,1)S(1)}, u32[]{:S(2)}, u32[]{:S(2)}) collective-permute-start(bf16[96,128]{1,0:T(8,128)(2,1)S(1)} %shard_map.59.after_ref), channel_id=1, source_target_pairs={{0,384},{8,392},{16,400},{24,408},{32,416},{40,424},{48,432},{56,4... | collective-permute-start | bytes 73736 | tf_op jit(solution)/shard_map/ppermute | solution.py:388
  44.3 0.7 %collective-permute-start.2 = (bf16[80,128]{1,0:T(8,128)(2,1)S(1)}, bf16[80,128]{1,0:T(8,128)(2,1)S(1)}, u32[]{:S(2)}, u32[]{:S(2)}) collective-permute-start(bf16[80,128]{1,0:T(8,128)(2,1)S(1)} %get-tuple-element.39.refs_1_), channel_id=1, source_target_pairs={{256,384},{264,392},{272,400},{280,408},{288,416},{296,424},{304,4... | collective-permute-start | bytes 61448 | tf_op jit(solution)/shard_map/ppermute | solution.py:387
  45.0 0.0 collective-permute-done.2.third_ref
  45.0 0.8 %collective-permute-done.1.two_ref = bf16[96,128]{1,0:T(8,128)(2,1)S(1)} collective-permute-done((bf16[96,128]{1,0:T(8,128)(2,1)S(1)}, bf16[96,128]{1,0:T(8,128)(2,1)S(1)}, u32[]{:S(2)}, u32[]{:S(2)}) %collective-permute-start.1) | collective-permute-done | bytes 24608 | tf_op jit(solution)/shard_map/ppermute | solution.py:388
  (2 shorter events, 0.0 us)
Async XLA Ops:
  31.1 11.9 %collective-permute-start = (bf16[80,128]{1,0:T(8,128)(2,1)S(1)}, bf16[80,128]{1,0:T(8,128)(2,1)S(1)}, u32[]{:S(2)}, u32[]{:S(2)}) collective-permute-start(bf16[80,128]{1,0:T(8,128)(2,1)S(1)} %get-tuple-element.39.refs_1_), channel_id=1, source_target_pairs={{0,128},{8,136},{16,144},{24,152},{32,160},{40,168},{48,176},{56,1... | collective-permute-start | bytes 61448 | tf_op jit(solution)/shard_map/ppermute | solution.py:372
  43.0 2.8 %collective-permute-start.1 = (bf16[96,128]{1,0:T(8,128)(2,1)S(1)}, bf16[96,128]{1,0:T(8,128)(2,1)S(1)}, u32[]{:S(2)}, u32[]{:S(2)}) collective-permute-start(bf16[96,128]{1,0:T(8,128)(2,1)S(1)} %shard_map.59.after_ref), channel_id=1, source_target_pairs={{0,384},{8,392},{16,400},{24,408},{32,416},{40,424},{48,432},{56,4... | collective-permute-start | bytes 73736 | tf_op jit(solution)/shard_map/ppermute | solution.py:388
  44.3 0.7 %collective-permute-start.2 = (bf16[80,128]{1,0:T(8,128)(2,1)S(1)}, bf16[80,128]{1,0:T(8,128)(2,1)S(1)}, u32[]{:S(2)}, u32[]{:S(2)}) collective-permute-start(bf16[80,128]{1,0:T(8,128)(2,1)S(1)} %get-tuple-element.39.refs_1_), channel_id=1, source_target_pairs={{256,384},{264,392},{272,400},{280,408},{288,416},{296,424},{304,4... | collective-permute-start | bytes 61448 | tf_op jit(solution)/shard_map/ppermute | solution.py:387

commit v8 on v7

--- a/solution.py
+++ b/solution.py
@@ -36,87 +36,95 @@
     return jnp.concatenate([ref[:, l * LANES : (l + 1) * LANES] for l in range(ref.shape[1] // LANES)], axis=0)
 
 
-def exact_parts(values, count):
-    parts = []
-    for _ in range(count):
-        parts.append(values.astype(BF16))
-        values = values - parts[-1].astype(F32)
-    return parts
-
-
 def square_sums(*refs):
     count = 5
-    held, refs = refs[:count], refs[count:]
-    (stream_ref, gain_ref, taps_ref, rate_ref, residue_ref), refs = refs[:count], refs[count:]
+    held, outs, refs = refs[:count], refs[count : 2 * count], refs[2 * count :]
     sums_ref, taps_pack, rate_pack, residue_pack, sem = refs
-    copies = [pltpu.make_async_copy(held[i], out, sem.at[i]) for i, out in enumerate((stream_ref, gain_ref, taps_ref, rate_ref, residue_ref))]
+    copies = [pltpu.make_async_copy(source, target, sem.at[i]) for i, (source, target) in enumerate(zip(held, outs))]
     for copy in copies:
         copy.start()
-    for copy in copies:
+    copies[0].wait()
+    stream_ref, _, taps_ref, rate_ref, residue_ref = outs
+    lanes = stream_ref.shape[1] // LANES
+    total = 0.0
+    for l in range(lanes):
+        values = stream_ref[:, l * LANES : (l + 1) * LANES].astype(F32)
+        total = total + values * values
+    sums = jnp.sum(total.T, axis=0, keepdims=True)
+    for peer in range(sums_ref.shape[0]):
+        sums_ref[peer] = sums
+    for copy in copies[1:]:
         copy.wait()
-    chans = stream_ref.shape[1]
-    values = stream_ref[...].astype(F32)
-    sums = jnp.zeros((SUB, values.shape[0]), F32)
-    for part in exact_parts(values * values, 2):
-        sums = sums + lax.dot_general(jnp.ones((SUB, chans), BF16), part, (((1,), (1,)), ((), ())), preferred_element_type=F32)
-    for peer in range(sums_ref.shape[0]):
-        sums_ref[peer] = sums[:1]
     rate_pack[...] = pack(rate_ref)
     residue_pack[...] = pack(residue_ref)
-    lanes = chans // LANES
     for tap in range(3):
         for role in range(3):
             for l in range(lanes):
                 taps_pack[pl.ds((tap * 3 + role) * lanes + l, 1), :] = taps_ref[tap, pl.ds(role, 1), pl.ds(l * LANES, LANES)]
 
 
-def block_states(chan_total, sums_ref, stream_ref, gain_ref, taps_ref, rate_ref, query_ref, product_ref, message_ref, normed_ref, end_ref, whole_ref):
+def block_states(chan_total, sums_ref, stream_ref, gain_ref, taps_ref, rate_ref, query_ref, product_ref, message_ref, edge_ref, end_ref, whole_ref):
     count, chans = stream_ref.shape
     lanes = chans // LANES
     modes = rate_ref.shape[0]
+    blocks = count // SUB
     sums = sums_ref[0]
     for peer in range(1, sums_ref.shape[0]):
         sums = sums + sums_ref[peer]
-    scale = lax.rsqrt(sums / chan_total + EPSILON)
-    parts = exact_parts(jnp.broadcast_to(scale, (2 * SUB, count)), 3)
-    ones = jnp.full((2 * SUB, chans), 1.0 / (2 * SUB), BF16)
-    scale = jnp.zeros((count, chans), F32)
-    for part in parts:
-        scale = scale + lax.dot_general(part, ones, (((0,), (0,)), ((), ())), preferred_element_type=F32)
-    values = stream_ref[...].astype(F32) * scale * gain_ref[...]
-    normed_ref[:SUB] = jnp.zeros((SUB, chans), F32)
-    normed_ref[SUB:] = values.astype(BF16).astype(F32)
-    shifted = [normed_ref[SUB - j : SUB - j + count] for j in range(3)]
-
-    def feature(role):
-        total = taps_ref[0, pl.ds(role, 1)] * shifted[0]
-        total = total + taps_ref[1, pl.ds(role, 1)] * shifted[1]
-        return total + taps_ref[2, pl.ds(role, 1)] * shifted[2]
-
-    query_ref[...] = feature(0).astype(BF16)
-    product_ref[...] = (feature(1) * feature(2)).astype(BF16).astype(F32)
-    row = lax.broadcasted_iota(jnp.int32, (SUB, chans), 0)
-    product_ref[:SUB] = jnp.where(row < 2, 0.0, product_ref[:SUB])
-
-    lag = (SUB - 1 - lax.broadcasted_iota(jnp.int32, (SUB, LANES), 0)).astype(F32)
+    rest = lax.rsqrt(sums / chan_total + EPSILON)
+    rows = lax.broadcasted_iota(jnp.int32, (2 * SUB, count), 0)
+    parts = jnp.zeros((2 * SUB, count), F32)
+    for i in range(3):
+        part = rest.astype(BF16).astype(F32)
+        parts = jnp.where(rows == i, part, parts)
+        rest = rest - part
+    scale = lax.dot_general(
+        parts.astype(BF16), jnp.ones((2 * SUB, LANES), BF16), (((0,), (0,)), ((), ())), preferred_element_type=F32
+    )
+    row = lax.broadcasted_iota(jnp.int32, (SUB, LANES), 0)
+    lag = (SUB - 1 - row).astype(F32)
 
     def one_lane(lane, carry):
         at = pl.ds(pl.multiple_of(lane * LANES, LANES), LANES)
-        blocks = [product_ref[pl.ds(i * SUB, SUB), at] for i in range(count // SUB)]
+        gain = jnp.broadcast_to(gain_ref[:, at], (SUB, LANES))
+        taps = [[jnp.broadcast_to(taps_ref[j, pl.ds(role, 1), at], (SUB, LANES)) for j in range(3)] for role in range(3)]
+        before = [jnp.zeros((SUB, LANES), F32)] * 2
+        products, queries = [], []
+        for i in range(blocks):
+            if i % 2 == 0:
+                pair = stream_ref[pl.ds(i * SUB, 2 * SUB), at].astype(F32)
+            normed = pair[i % 2 * SUB : (i % 2 + 1) * SUB] * scale[i * SUB : (i + 1) * SUB] * gain
+            normed = normed.astype(BF16).astype(F32)
+            if i == 0:
+                edge_ref[:2, at] = normed[:2]
+            if i == blocks - 1:
+                edge_ref[2:4, at] = normed[SUB - 2 :]
+            rolled = [pltpu.roll(normed, j, 0) for j in (1, 2)]
+            shifted = [normed] + [jnp.where(row < j, b, r) for j, b, r in zip((1, 2), before, rolled)]
+            before = rolled
+            query, key, value = [sum(t * n for t, n in zip(taps[role], shifted)) for role in range(3)]
+            product = (key * value).astype(BF16).astype(F32)
+            if i == 0:
+                product = jnp.where(row < 2, 0.0, product)
+            product_ref[pl.ds(i * SUB, SUB), at] = product
+            products.append(product)
+            queries.append(query)
+            if i % 2 == 1:
+                query_ref[pl.ds((i - 1) * SUB, 2 * SUB), at] = jnp.concatenate(queries[-2:], axis=0).astype(BF16)
         for mode in range(modes):
             rate = rate_ref[pl.ds(mode, 1), at]
             step = jnp.broadcast_to(jnp.exp(-SUB * rate), (SUB, LANES))
-            total = blocks[0]
-            for block in blocks[1:]:
-                total = total * step + block
+            total = products[0]
+            for product in products[1:]:
+                total = total * step + product
             end_ref[pl.ds(mode, 1), at] = jnp.sum(total * jnp.exp(-rate * lag), axis=0, keepdims=True)
         return carry
 
     lax.fori_loop(0, lanes, one_lane, 0)
     whole_ref[: lanes * modes] = pack(end_ref)
-    for e, place in enumerate((0, 1, count - 2, count - 1)):
+    for e in range(4):
         for l in range(lanes):
-            whole_ref[pl.ds(lanes * (modes + e) + l, 1), :] = normed_ref[pl.ds(SUB + place, 1), pl.ds(l * LANES, LANES)]
+            whole_ref[pl.ds(lanes * (modes + e) + l, 1), :] = edge_ref[pl.ds(e, 1), pl.ds(l * LANES, LANES)]
     message = whole_ref[...].astype(BF16)
     for peer in range(message_ref.shape[0]):
         message_ref[peer] = message
@@ -284,47 +292,49 @@
     lax.fori_loop(0, lanes, one_lane, 0)
 
 
-def early(got_ref, before_ref, rate_pack, residue_pack, taps_ref, rate_ref, query_ref, residue_ref, product_ref, local_ref, out_ref, filter_ref, state_ref, mixed_ref, sem):
-    _, group = places()
+def leave(mixed_ref, out_ref, sem):
+    copy = pltpu.make_async_copy(mixed_ref, out_ref, sem)
+    copy.start()
+    copy.wait()
+
+
+def early_inner(rate_ref, residue_ref, product_ref, after_ref, local_ref, filter_ref):
+    @pl.when(places()[1] < 2)
+    def _():
+        inner_conv(rate_ref, residue_ref, product_ref, local_ref, filter_ref)
+
+
+def early_output(got_ref, before_ref, rate_pack, residue_pack, taps_ref, rate_ref, query_ref, residue_ref, product_ref, swap_ref, after_ref, held_ref, local_ref, out_ref, filter_ref, state_ref, mixed_ref, sem):
+    group = places()[1]
+
+    @pl.when(group >= 2)
+    def _():
+        inner_conv(rate_ref, residue_ref, product_ref, local_ref, filter_ref)
 
     @pl.when(group < 2)
     def _():
-        inner_conv(rate_ref, residue_ref, product_ref, local_ref, filter_ref)
-
-    @pl.when(group == 0)
-    def _():
-        nothing = jnp.zeros(rate_pack.shape, F32)
-        last = [jnp.zeros((taps_ref.shape[0] // 9, LANES), F32)] * 2
-        finish(nothing, last, got_ref, before_ref, rate_pack, residue_pack, taps_ref, rate_ref, query_ref, local_ref, mixed_ref, state_ref)
-        copy = pltpu.make_async_copy(mixed_ref, out_ref, sem)
-        copy.start()
-        copy.wait()
-
-
-def later(rate_ref, residue_ref, product_ref, after_ref, held_ref, local_ref, filter_ref):
-    @pl.when(places()[1] >= 2)
-    def _():
-        inner_conv(rate_ref, residue_ref, product_ref, local_ref, filter_ref)
-
-
-def final(got_ref, before_ref, rate_pack, residue_pack, taps_ref, rate_ref, query_ref, local_ref, swap_ref, two_ref, third_ref, held_ref, out_ref, state_ref, mixed_ref, sem):
-    _, group = places()
-    block = local_ref.shape[0] * NEAR
+        rates = rate_pack[...]
+        state, last = jnp.zeros_like(rates), [jnp.zeros((taps_ref.shape[0] // 9, LANES), F32)] * 2
+        after, after_last = step_over(local_ref.shape[0] * NEAR, len(last[0]), rates, taps_ref, state, last, swap_ref[...].astype(F32))
+        state, last = jnp.where(group == 1, after, state), [jnp.where(group == 1, a, b) for a, b in zip(after_last, last)]
+        finish(state, last, got_ref, before_ref, rate_pack, residue_pack, taps_ref, rate_ref, query_ref, local_ref, mixed_ref, state_ref)
+        leave(mixed_ref, out_ref, sem)
+
+
+def last_output(got_ref, before_ref, rate_pack, residue_pack, taps_ref, rate_ref, query_ref, local_ref, two_ref, third_ref, held_ref, out_ref, state_ref, mixed_ref, sem):
+    group = places()[1]
     states = rate_pack.shape[0]
     lanes = taps_ref.shape[0] // 9
 
-    @pl.when(group > 0)
+    @pl.when(group >= 2)
     def _():
         came = two_ref[...].astype(F32)
         state, last = came[:states], (came[states : states + lanes], came[states + lanes : states + 2 * lanes])
-        run = jnp.where(group == 1, swap_ref[...].astype(F32), third_ref[...].astype(F32))
-        after, after_last = step_over(block, lanes, rate_pack[...], taps_ref, state, last, run)
-        odd = group % 2 == 1
+        after, after_last = step_over(local_ref.shape[0] * NEAR, lanes, rate_pack[...], taps_ref, state, last, third_ref[...].astype(F32))
+        odd = group == 3
         state, last = jnp.where(odd, after, state), [jnp.where(odd, a, b) for a, b in zip(after_last, last)]
         finish(state, last, got_ref, before_ref, rate_pack, residue_pack, taps_ref, rate_ref, query_ref, local_ref, mixed_ref, state_ref)
-        copy = pltpu.make_async_copy(mixed_ref, out_ref, sem)
-        copy.start()
-        copy.wait()
+        leave(mixed_ref, out_ref, sem)
 
 
 def places():
@@ -360,7 +370,7 @@
         lambda *refs: block_states(chans * peers, *refs),
         [((count, chans), BF16), ((count, chans), F32), ((NEAR, states + 4 * lanes, LANES), BF16)],
         sums, stream, gain, taps, rates,
-        scratch=[pltpu.VMEM((SUB + count, chans), F32), pltpu.VMEM((modes, chans), F32), pltpu.VMEM((states + 4 * lanes, LANES), F32)],
+        scratch=[pltpu.VMEM((SUB, chans), F32), pltpu.VMEM((modes, chans), F32), pltpu.VMEM((states + 4 * lanes, LANES), F32)],
     )
     near = gather(message, "ctx", groups)
     near_before, message = call(
@@ -368,33 +378,31 @@
         [((states, LANES), F32), ((states + 4 * lanes, LANES), BF16)],
         near, rate_pack, taps_pack,
     )
-    hops = lambda *ends: [pair for a, b in ends for pair in zip(groups[a], groups[b])]
-    swap = lax.ppermute(message, "ctx", hops((0, 1), (1, 0)))
+    outs = [((count, chans), F32), ((count, chans), BF16)]
     common = [near, near_before, rate_pack, residue_pack, taps_pack, rates, query]
+    room = [pltpu.VMEM((count, LANES), F32)]
     work = [pltpu.VMEM((modes + 2 * SUB, chans), F32), pltpu.VMEM((count, chans), BF16), pltpu.SemaphoreType.DMA]
-    local, mixed = call(
-        early,
-        [((count, chans), F32), ((count, chans), BF16)],
-        *common, weights, product,
-        scratch=[pltpu.VMEM((count, LANES), F32)] + work, flops=10**7, out_hbm=(1,),
-    )
+    hops = lambda *ends: [pair for a, b in ends for pair in zip(a, b)]
+    first, second, third, fourth = groups
+    width = NEAR // 4
+    turned = [fourth[NEAR - width * (i // width + 1) + i % width] for i in range(NEAR)]
+    swap = lax.ppermute(message, "ctx", hops((first, second), (second, first)))
+    (local,) = call(early_inner, outs[:1], rates, weights, product, near_before, scratch=room, flops=10**7)
     (two,) = call(
         lambda *refs: relay(count * NEAR, lanes, *refs),
         [((states + 8 * lanes, LANES), BF16)],
         swap, message, rate_pack, taps_pack, local,
     )
-    third, relayed = lax.optimization_barrier((message, two))
-    third = lax.ppermute(third, "ctx", hops((2, 3)))
-    two = lax.ppermute(relayed, "ctx", hops((0, 3), (1, 2)))
-    (local,) = call(
-        later, [((count, chans), F32)], rates, weights, product, relayed, local,
-        scratch=[pltpu.VMEM((count, LANES), F32)], flops=10**7, aliases={4: 0},
+    message, relayed = lax.optimization_barrier((message, two))
+    three = lax.ppermute(message, "ctx", hops((third, fourth)))
+    two = lax.ppermute(relayed, "ctx", hops((first, turned), (second, third)))
+    local, mixed = call(
+        early_output, outs, *common, weights, product, swap, relayed, local,
+        scratch=room + work, flops=10**7, out_hbm=(1,), aliases={11: 0},
     )
     (mixed,) = call(
-        final,
-        [((count, chans), BF16)],
-        *common, local, swap, two, third, mixed,
-        scratch=work, in_hbm=(11,), out_hbm=(0,), aliases={11: 0},
+        last_output, outs[1:], *common, local, two, three, mixed,
+        scratch=work, in_hbm=(10,), out_hbm=(0,), aliases={10: 0},
     )
     return mixed
 

time: 46.1 us -> 45.4 us (0.985)
  the two profiles are of different devices: /device:TPU:8 before, /device:TPU:2 now
where the time goes in v8:
time: 45.4 us; the launch traced here: 45.2 us
  blocking collectives  28.6 us (63%)
  starting transfers between devices  11 us (24%)
  Pallas kernels  5.15 us (11%)
    all_to_all x2, blocking collectives, gather(): lax.all_to_all(copies, axis, 0, 0, tiled=True, axis_index_groups=groups)  28.6 us
    ppermute x1, starting transfers between devices, per_device(): swap = lax.ppermute(message, 'ctx', hops((first, second), (second, first)))  9.09 us
    pallas_call x7, Pallas kernels, call(): pl.pallas_call(body, out_shape=shapes, in_specs=[pl.BlockSpec(memory_spac...  5.15 us
    ppermute x1, starting transfers between devices, per_device(): two = lax.ppermute(relayed, 'ctx', hops((first, turned), (second, third)))  1.29 us
  transfers between devices with their start and end apart: 3, of which 1 were waited for; matrix products, arithmetic and copies ran while one was open for 0% of the time, Pallas kernels for 6%

profile of v8, /device:TPU:2, one launch (start us, length us, event | category | flops | bytes accessed | tf_op | source)
XLA Modules:
  0.0 45.2 jit_solution(9580699781613482005)
XLA Ops:
  0.0 1.1 %shard_map.55 = (bf16[128,512]{1,0:T(8,128)(2,1)S(1)}, f32[1,512]{1,0:T(1,128)S(1)}, f32[3,3,512]{2,1,0:T(4,128)S(1)}, f32[16,512]{1,0:T(8,128)S(1)}, f32[16,512...) custom-call(bf16[128,512]{1,0:T(8,128)(2,1)} %refs_0_.1, ...), custom_call_target="tpu_custom_call" | custom-call | bytes 217088 | tf_op jit(solution)/shard_map/pallas_call | solution.py:23
  1.1 9.5 %all_to_all.10.refs_0_ = f32[8,1,128]{2,1,0:T(1,128)S(1)} all-to-all(f32[8,1,128]{2,1,0:T(1,128)S(1)} %get-tuple-element.23), channel_id=1, replica_groups=mesh['ctx'=64,'ch'=8] {'ch'}, dimensions={0} | all-to-all | bytes 8192 | tf_op jit(solution)/shard_map/all_to_all | solution.py:346
  10.6 0.9 %shard_map.56 = (bf16[128,512]{1,0:T(8,128)(2,1)S(1)}, f32[128,512]{1,0:T(8,128)S(1)}, bf16[16,80,128]{2,1,0:T(8,128)(2,1)S(1)}) custom-call(f32[8,1,128]{2,1,0:T(1,128)S(1)} %all_to_all.10.refs_0_, bf16[128,512]{1,0:T(8,128)(2,1)S(1)} %get-tuple-element.24.refs_1_, f32[1,512]{1,0:T(1,128)S(1)} %get-tuple-element.25.refs_2_, ...), custom_call_target="tpu_custom_call" | custom-call | bytes 188416 | tf_op jit(solution)/shard_map/pallas_call | solution.py:23
  11.5 19.1 %all_to_all.11.refs_0_.got_ref = bf16[16,80,128]{2,1,0:T(8,128)(2,1)S(1)} all-to-all(bf16[16,80,128]{2,1,0:T(8,128)(2,1)S(1)} %get-tuple-element.28), channel_id=1, replica_groups={{0,8,16,24,32,40,48,56,64,72,80,88,96,104,112,120},{128,136,144,152,160..., dimensions={0} | all-to-all | bytes 655360 | tf_op jit(solution)/shard_map/all_to_all | solution.py:346
  30.6 0.3 shard_map.57
  30.8 9.1 %collective-permute-start = (bf16[80,128]{1,0:T(8,128)(2,1)S(1)}, bf16[80,128]{1,0:T(8,128)(2,1)S(1)}, u32[]{:S(2)}, u32[]{:S(2)}) collective-permute-start(bf16[80,128]{1,0:T(8,128)(2,1)S(1)} %get-tuple-element.39.refs_1_), channel_id=1, source_target_pairs={{0,128},{8,136},{16,144},{24,152},{32,160},{40,168},{48,176},{56,1... | collective-permute-start | bytes 61448 | tf_op jit(solution)/shard_map/ppermute | solution.py:389
  39.9 1.6 %shard_map.58.refs_4_.held_ref = f32[128,512]{1,0:T(8,128)S(1)} custom-call(f32[16,512]{1,0:T(8,128)S(1)} %get-tuple-element.27.refs_4_.rate_ref, f32[16,512]{1,0:T(8,128)S(1)} %get-tuple-element.34.residue_ref, f32[128,512]{1,0:T(8,128)S(1)} %get-tuple-element.35.product_ref, f32[64,128]{1,0:T(8,128)S(1)} %get-tuple-element.31.after_ref.before_ref), custom_call_target="tpu_custom_call" | custom-call | flops 10000000 | bytes 360448 | tf_op jit(solution)/shard_map/pallas_call | solution.py:23
  41.6 0.3 collective-permute-done.refs_0_.swap_ref
  41.9 0.1 shard_map.59.after_ref
  42.0 1.3 %collective-permute-start.1 = (bf16[96,128]{1,0:T(8,128)(2,1)S(1)}, bf16[96,128]{1,0:T(8,128)(2,1)S(1)}, u32[]{:S(2)}, u32[]{:S(2)}) collective-permute-start(bf16[96,128]{1,0:T(8,128)(2,1)S(1)} %shard_map.59.after_ref), channel_id=1, source_target_pairs={{0,480},{8,488},{16,496},{24,504},{32,448},{40,456},{48,464},{56,4... | collective-permute-start | bytes 73736 | tf_op jit(solution)/shard_map/ppermute | solution.py:398
  43.3 0.7 %collective-permute-start.2 = (bf16[80,128]{1,0:T(8,128)(2,1)S(1)}, bf16[80,128]{1,0:T(8,128)(2,1)S(1)}, u32[]{:S(2)}, u32[]{:S(2)}) collective-permute-start(bf16[80,128]{1,0:T(8,128)(2,1)S(1)} %get-tuple-element.39.refs_1_), channel_id=1, source_target_pairs={{256,384},{264,392},{272,400},{280,408},{288,416},{296,424},{304,4... | collective-permute-start | bytes 61448 | tf_op jit(solution)/shard_map/ppermute | solution.py:397
  43.9 1.2 %shard_map.60 = (f32[128,512]{1,0:T(8,128)S(1)}, bf16[128,512]{1,0:T(8,128)(2,1)}) custom-call(bf16[16,80,128]{2,1,0:T(8,128)(2,1)S(1)} %all_to_all.11.refs_0_.got_ref, f32[64,128]{1,0:T(8,128)S(1)} %get-tuple-element.31.after_ref.before_ref, f32[64,128]{1,0:T(8,128)S(1)} %get-tuple-element.29.refs_1_.refs_2_.rate_pack, ...), custom_call_target="tpu_custom_call", output_to_operand_aliasing={{0}: (11, {})} | custom-call | flops 10000000 | bytes 1210368 | tf_op jit(solution)/shard_map/pallas_call | solution.py:23
  45.1 0.0 collective-permute-done.2.third_ref
  45.1 0.0 collective-permute-done.1.two_ref
  (1 shorter events, 0.0 us)
Async XLA Ops:
  30.8 11.1 %collective-permute-start = (bf16[80,128]{1,0:T(8,128)(2,1)S(1)}, bf16[80,128]{1,0:T(8,128)(2,1)S(1)}, u32[]{:S(2)}, u32[]{:S(2)}) collective-permute-start(bf16[80,128]{1,0:T(8,128)(2,1)S(1)} %get-tuple-element.39.refs_1_), channel_id=1, source_target_pairs={{0,128},{8,136},{16,144},{24,152},{32,160},{40,168},{48,176},{56,1... | collective-permute-start | bytes 61448 | tf_op jit(solution)/shard_map/ppermute | solution.py:389
  42.0 3.2 %collective-permute-start.1 = (bf16[96,128]{1,0:T(8,128)(2,1)S(1)}, bf16[96,128]{1,0:T(8,128)(2,1)S(1)}, u32[]{:S(2)}, u32[]{:S(2)}) collective-permute-start(bf16[96,128]{1,0:T(8,128)(2,1)S(1)} %shard_map.59.after_ref), channel_id=1, source_target_pairs={{0,480},{8,488},{16,496},{24,504},{32,448},{40,456},{48,464},{56,4... | collective-permute-start | bytes 73736 | tf_op jit(solution)/shard_map/ppermute | solution.py:398
  43.3 1.9 %collective-permute-start.2 = (bf16[80,128]{1,0:T(8,128)(2,1)S(1)}, bf16[80,128]{1,0:T(8,128)(2,1)S(1)}, u32[]{:S(2)}, u32[]{:S(2)}) collective-permute-start(bf16[80,128]{1,0:T(8,128)(2,1)S(1)} %get-tuple-element.39.refs_1_), channel_id=1, source_target_pairs={{256,384},{264,392},{272,400},{280,408},{288,416},{296,424},{304,4... | collective-permute-start | bytes 61448 | tf_op jit(solution)/shard_map/ppermute | solution.py:397

commit v9 on v8

--- a/solution.py
+++ b/solution.py
@@ -9,7 +9,8 @@
 EPSILON = 1e-05
 SUB = 8
 LANES = 128
-NEAR = 16
+WIDE = 16
+NEAR = 8
 
 F32 = jnp.float32
 BF16 = jnp.bfloat16
@@ -18,7 +19,7 @@
 def call(body, outs, *args, scratch=(), flops=0, space=pltpu.VMEM, in_hbm=(), out_hbm=(), aliases=None):
     shapes = [jax.ShapeDtypeStruct(s, d) for s, d in outs]
     spaces = [pltpu.HBM if i in in_hbm else space for i in range(len(args))]
-    out_spaces = [pltpu.HBM if i in out_hbm else pltpu.VMEM for i in range(len(outs))]
+    out_spaces = [pl.ANY if i in out_hbm else pltpu.VMEM for i in range(len(outs))]
     moved = sum(a.size * a.dtype.itemsize for a in args)
     return pl.pallas_call(
         body,
@@ -63,7 +64,7 @@
                 taps_pack[pl.ds((tap * 3 + role) * lanes + l, 1), :] = taps_ref[tap, pl.ds(role, 1), pl.ds(l * LANES, LANES)]
 
 
-def block_states(chan_total, sums_ref, stream_ref, gain_ref, taps_ref, rate_ref, query_ref, product_ref, message_ref, edge_ref, end_ref, whole_ref):
+def block_states(chan_total, sums_ref, stream_ref, gain_ref, taps_ref, rate_ref, query_ref, product_ref, wide_ref, near_ref, edge_ref, end_ref, whole_ref):
     count, chans = stream_ref.shape
     lanes = chans // LANES
     modes = rate_ref.shape[0]
@@ -126,8 +127,9 @@
         for l in range(lanes):
             whole_ref[pl.ds(lanes * (modes + e) + l, 1), :] = edge_ref[pl.ds(e, 1), pl.ds(l * LANES, LANES)]
     message = whole_ref[...].astype(BF16)
-    for peer in range(message_ref.shape[0]):
-        message_ref[peer] = message
+    for ref in (wide_ref, near_ref):
+        for peer in range(ref.shape[0]):
+            ref[peer] = message
 
 
 def first_rows(taps_ref, role, last, head):
@@ -160,44 +162,93 @@
     return end, pairs(run, states + 2 * lanes, lanes)
 
 
-def step_into(block, lanes, place, rates, taps_ref, state, last, got_ref, before_ref):
+def step_into(block, lanes, place, rates, taps_ref, state, last, edge_ref, before_ref):
     states = rates.shape[0]
     modes = states // lanes
-    first, second = first_products(taps_ref, last, pairs(got_ref[0].astype(F32), states, lanes))
+    first, second = first_products(taps_ref, last, pairs(edge_ref, 0, lanes))
     lag = (block * place).astype(F32)
     held = jnp.exp(-rates * jnp.maximum(lag - 1.0, 0.0)) * spread(first, modes)
     held = held + jnp.exp(-rates * jnp.maximum(lag - 2.0, 0.0)) * spread(second, modes)
     state = before_ref[...] + state * jnp.exp(-rates * lag) + jnp.where(place > 0, held, 0.0)
-    inside = pairs(got_ref[jnp.maximum(place - 1, 0)].astype(F32), states + 2 * lanes, lanes)
+    inside = pairs(edge_ref, 2 * lanes, lanes)
     return state, [jnp.where(place > 0, a, b) for a, b in zip(inside, last)]
 
 
-def near_scan(block, lanes, got_ref, rate_ref, taps_ref, before_ref, message_ref):
-    place, _ = places()
+def near_scan(block, lanes, got_ref, rate_ref, taps_ref, before_ref, edge_ref):
+    size = got_ref.shape[0]
+    place = lax.axis_index("ctx") % size
     states = rate_ref.shape[0]
     rates = rate_ref[...]
     run = got_ref[0].astype(F32)
     head = run[states : states + 2 * lanes]
     total, last = run[:states], pairs(run, states + 2 * lanes, lanes)
     before = jnp.where(place == 1, total, jnp.zeros_like(total))
-    for j in range(1, NEAR):
+    for j in range(1, size):
         total, last = step_over(block, lanes, rates, taps_ref, total, last, got_ref[j].astype(F32))
-        if j < NEAR - 1:
+        if j < size - 1:
             before = jnp.where(place == j + 1, total, before)
     before_ref[...] = before
-    message_ref[...] = jnp.concatenate([total, head, *last], axis=0).astype(BF16)
-
-
-def relay(block, lanes, came_ref, own_ref, rate_ref, taps_ref, after_ref, out_ref):
+    edge_ref[: 2 * lanes] = head
+    edge_ref[2 * lanes : 4 * lanes] = got_ref[jnp.maximum(place - 1, 0)].astype(F32)[states + 2 * lanes :]
+    edge_ref[4 * lanes :] = got_ref[place].astype(F32)[states : states + 2 * lanes]
+    return jnp.concatenate([total, head, *last], axis=0)
+
+
+def write(message, *refs):
+    for ref in refs:
+        rest = ref.shape[0] - message.shape[0]
+        whole = jnp.concatenate([message, jnp.zeros((rest, LANES), F32)], axis=0) if rest else message
+        ref[...] = whole.astype(BF16)
+
+
+def first_scan(block, lanes, got_ref, rate_ref, taps_ref, before_ref, edge_ref, message_ref):
+    @pl.when(lax.axis_index("ctx") // WIDE == 0)
+    def _():
+        write(near_scan(block, lanes, got_ref, rate_ref, taps_ref, before_ref, edge_ref), message_ref)
+
+
+def second_scan(block, lanes, got_ref, came_ref, rate_ref, taps_ref, before_ref, edge_ref, *message_refs):
+    @pl.when(lax.axis_index("ctx") // WIDE == 1)
+    def _():
+        rates = rate_ref[...]
+        own = near_scan(block, lanes, got_ref, rate_ref, taps_ref, before_ref, edge_ref)
+        state, last = jnp.zeros_like(rates), [jnp.zeros((lanes, LANES), F32)] * 2
+        for run in (came_ref[...].astype(F32), own):
+            state, last = step_over(block * WIDE, lanes, rates, taps_ref, state, last, run)
+        write(jnp.concatenate([state, *last], axis=0), *message_refs)
+
+
+def third_scan(block, lanes, got_ref, rate_ref, taps_ref, before_ref, edge_ref, *message_refs):
+    @pl.when(lax.axis_index("ctx") // WIDE == 2)
+    def _():
+        write(near_scan(block, lanes, got_ref, rate_ref, taps_ref, before_ref, edge_ref), *message_refs)
+
+
+def fourth_scan(block, lanes, got_ref, third_before, third_edge, third_message, rate_ref, taps_ref, before_ref, edge_ref, message_ref):
+    group = lax.axis_index("ctx") // WIDE
+
+    @pl.when(group == 2)
+    def _():
+        before_ref[...] = third_before[...]
+        edge_ref[...] = third_edge[...]
+        message_ref[...] = third_message[...]
+
+    @pl.when(group == 3)
+    def _():
+        write(near_scan(block, lanes, got_ref, rate_ref, taps_ref, before_ref, edge_ref), message_ref)
+
+
+def merge(block, lanes, across_ref, cross_ref, next_ref, rate_ref, taps_ref, ahead_ref):
+    run = lax.axis_index("ctx") // NEAR
+    states = rate_ref.shape[0]
     rates = rate_ref[...]
-    states = rates.shape[0]
-    low = places()[1] == 0
-    own, came = own_ref[...].astype(F32), came_ref[...].astype(F32)
-    state, last = jnp.zeros_like(rates), [jnp.zeros((lanes, LANES), F32)] * 2
-    for run in (jnp.where(low, own, came), jnp.where(low, came, own)):
-        state, last = step_over(block, lanes, rates, taps_ref, state, last, run)
-    rest = jnp.zeros((out_ref.shape[0] - states - 2 * lanes, LANES), F32)
-    out_ref[...] = jnp.concatenate([state, *last, rest], axis=0).astype(BF16)
+    across, cross, following = [r[: states + 4 * lanes].astype(F32) for r in (across_ref, cross_ref, next_ref)]
+    start = jnp.where(run == 5, following, jnp.where(run == 6, across, cross))
+    state, last = start[:states], pairs(start, states + 2 * lanes, lanes)
+    for needed, message in ((run > 5, jnp.where(run == 6, cross, across)), (run > 6, following)):
+        after, after_last = step_over(block * NEAR, lanes, rates, taps_ref, state, last, message)
+        state, last = jnp.where(needed, after, state), [jnp.where(needed, a, b) for a, b in zip(after_last, last)]
+    ahead_ref[...] = jnp.concatenate([state, start[states : states + 2 * lanes], *last], axis=0)
 
 
 def add_mode(totals, term, rate):
@@ -244,16 +295,15 @@
     lax.fori_loop(0, chans // LANES, one_lane, 0)
 
 
-def finish(state, last, got_ref, before_ref, rate_pack, residue_pack, taps_ref, rate_ref, query_ref, local_ref, mixed_ref, state_ref):
+def finish(place, state, last, edge_ref, before_ref, rate_pack, residue_pack, taps_ref, rate_ref, query_ref, local_ref, mixed_ref, state_ref):
     count, chans = local_ref.shape
     lanes = chans // LANES
     modes = rate_ref.shape[0]
     states = lanes * modes
     blocks = count // SUB
-    place, _ = places()
     rates = rate_pack[...]
-    state, own_last = step_into(count, lanes, place, rates, taps_ref, state, last, got_ref, before_ref)
-    own_head = pairs(got_ref[place].astype(F32), states, lanes)
+    state, own_last = step_into(count, lanes, place, rates, taps_ref, state, last, edge_ref, before_ref)
+    own_head = pairs(edge_ref, 4 * lanes, lanes)
     own_query = [q.astype(BF16).astype(F32) for q in first_rows(taps_ref, 0, own_last, own_head)]
     first, second = first_products(taps_ref, own_last, own_head)
     ahead = jnp.exp(rates) * spread(second, modes)
@@ -292,54 +342,24 @@
     lax.fori_loop(0, lanes, one_lane, 0)
 
 
-def leave(mixed_ref, out_ref, sem):
-    copy = pltpu.make_async_copy(mixed_ref, out_ref, sem)
-    copy.start()
-    copy.wait()
-
-
-def early_inner(rate_ref, residue_ref, product_ref, after_ref, local_ref, filter_ref):
-    @pl.when(places()[1] < 2)
-    def _():
-        inner_conv(rate_ref, residue_ref, product_ref, local_ref, filter_ref)
-
-
-def early_output(got_ref, before_ref, rate_pack, residue_pack, taps_ref, rate_ref, query_ref, residue_ref, product_ref, swap_ref, after_ref, held_ref, local_ref, out_ref, filter_ref, state_ref, mixed_ref, sem):
-    group = places()[1]
-
-    @pl.when(group >= 2)
-    def _():
-        inner_conv(rate_ref, residue_ref, product_ref, local_ref, filter_ref)
-
-    @pl.when(group < 2)
-    def _():
-        rates = rate_pack[...]
-        state, last = jnp.zeros_like(rates), [jnp.zeros((taps_ref.shape[0] // 9, LANES), F32)] * 2
-        after, after_last = step_over(local_ref.shape[0] * NEAR, len(last[0]), rates, taps_ref, state, last, swap_ref[...].astype(F32))
-        state, last = jnp.where(group == 1, after, state), [jnp.where(group == 1, a, b) for a, b in zip(after_last, last)]
-        finish(state, last, got_ref, before_ref, rate_pack, residue_pack, taps_ref, rate_ref, query_ref, local_ref, mixed_ref, state_ref)
-        leave(mixed_ref, out_ref, sem)
-
-
-def last_output(got_ref, before_ref, rate_pack, residue_pack, taps_ref, rate_ref, query_ref, local_ref, two_ref, third_ref, held_ref, out_ref, state_ref, mixed_ref, sem):
-    group = places()[1]
+def output(first_before, first_edge, second_before, second_edge, upper_before, upper_edge, rate_pack, residue_pack, taps_ref, rate_ref, query_ref, local_ref, low_ref, third_ref, fourth_ref, ahead_ref, mixed_ref, state_ref):
+    index = lax.axis_index("ctx")
+    group, run = index // WIDE, index // NEAR
     states = rate_pack.shape[0]
     lanes = taps_ref.shape[0] // 9
-
-    @pl.when(group >= 2)
-    def _():
-        came = two_ref[...].astype(F32)
-        state, last = came[:states], (came[states : states + lanes], came[states + lanes : states + 2 * lanes])
-        after, after_last = step_over(local_ref.shape[0] * NEAR, lanes, rate_pack[...], taps_ref, state, last, third_ref[...].astype(F32))
-        odd = group == 3
-        state, last = jnp.where(odd, after, state), [jnp.where(odd, a, b) for a, b in zip(after_last, last)]
-        finish(state, last, got_ref, before_ref, rate_pack, residue_pack, taps_ref, rate_ref, query_ref, local_ref, mixed_ref, state_ref)
-        leave(mixed_ref, out_ref, sem)
-
-
-def places():
-    index = lax.axis_index("ctx")
-    return index % NEAR, index // NEAR
+    count = local_ref.shape[0]
+    came = third_ref[...].astype(F32) + fourth_ref[: states + 4 * lanes].astype(F32)
+    state, last = came[:states], (came[states : states + lanes], came[states + lanes : states + 2 * lanes])
+    length = jnp.where(group == 1, WIDE, NEAR * jnp.maximum(run - 4, 1)) * count
+    message = jnp.where(group == 1, low_ref[...].astype(F32), ahead_ref[...])
+    needed = (group == 1) | (run > 4)
+    after, after_last = step_over(length.astype(F32), lanes, rate_pack[...], taps_ref, state, last, message)
+    state, last = jnp.where(needed, after, state), [jnp.where(needed, a, b) for a, b in zip(after_last, last)]
+    place = jnp.where(group < 2, index % WIDE, index % NEAR)
+    pick = lambda a, b, c: jnp.where(group == 0, a[...], jnp.where(group == 1, b[...], c[...]))
+    before = pick(first_before, second_before, upper_before)
+    edges = pick(first_edge, second_edge, upper_edge)
+    finish(place, state, last, edges, before, rate_pack, residue_pack, taps_ref, rate_ref, query_ref, local_ref, mixed_ref, state_ref)
 
 
 def gather(copies, axis, groups=None):
@@ -353,8 +373,9 @@
     states = lanes * modes
     peers = lax.axis_size("ch")
     ctx = lax.axis_size("ctx")
-    groups = [[g + m for m in range(NEAR)] for g in range(0, ctx, NEAR)]
-
+    groups = [[g + m for m in range(WIDE)] for g in range(0, ctx, WIDE)]
+    runs = [[g + m for m in range(NEAR)] for g in range(0, ctx, NEAR)]
+    index, stream = lax.optimization_barrier((lax.axis_index("ctx"), stream))
     held = [stream, norm_gain[None, :], short_filter, decay_rate.T, residue.T]
     held = [pltpu.with_memory_space_constraint(h, pltpu.HBM) for h in held]
     stream, gain, taps, rates, weights, sums, taps_pack, rate_pack, residue_pack = call(
@@ -365,44 +386,62 @@
         scratch=[pltpu.SemaphoreType.DMA((len(held),))],
         space=pltpu.HBM,
     )
-    sums = gather(sums, "ch")
-    query, product, message = call(
+    sums = lax.cond(index < ctx, lambda c: gather(c, "ch"), lambda c: c, sums)
+    query, product, wide, near = call(
         lambda *refs: block_states(chans * peers, *refs),
-        [((count, chans), BF16), ((count, chans), F32), ((NEAR, states + 4 * lanes, LANES), BF16)],
+        [((count, chans), BF16), ((count, chans), F32), ((WIDE, states + 4 * lanes, LANES), BF16), ((NEAR, states + 4 * lanes, LANES), BF16)],
         sums, stream, gain, taps, rates,
         scratch=[pltpu.VMEM((SUB, chans), F32), pltpu.VMEM((modes, chans), F32), pltpu.VMEM((states + 4 * lanes, LANES), F32)],
     )
-    near = gather(message, "ctx", groups)
-    near_before, message = call(
-        lambda *refs: near_scan(count, lanes, *refs),
-        [((states, LANES), F32), ((states + 4 * lanes, LANES), BF16)],
-        near, rate_pack, taps_pack,
-    )
-    outs = [((count, chans), F32), ((count, chans), BF16)]
-    common = [near, near_before, rate_pack, residue_pack, taps_pack, rates, query]
-    room = [pltpu.VMEM((count, LANES), F32)]
-    work = [pltpu.VMEM((modes + 2 * SUB, chans), F32), pltpu.VMEM((count, chans), BF16), pltpu.SemaphoreType.DMA]
+    index, wide, near = lax.optimization_barrier((index, wide, near))
+    group = lax.shift_right_logical(index, WIDE.bit_length() - 1)
+    small, large = ((states + 4 * lanes, LANES), BF16), ((states + 8 * lanes, LANES), BF16)
+    kept = [((states, LANES), F32), ((6 * lanes, LANES), F32)]
+    nothing = lambda *shapes: tuple(call(lambda *refs: None, shapes, out_hbm=range(len(shapes))))
     hops = lambda *ends: [pair for a, b in ends for pair in zip(a, b)]
     first, second, third, fourth = groups
-    width = NEAR // 4
-    turned = [fourth[NEAR - width * (i // width + 1) + i % width] for i in range(NEAR)]
-    swap = lax.ppermute(message, "ctx", hops((first, second), (second, first)))
-    (local,) = call(early_inner, outs[:1], rates, weights, product, near_before, scratch=room, flops=10**7)
-    (two,) = call(
-        lambda *refs: relay(count * NEAR, lanes, *refs),
-        [((states + 8 * lanes, LANES), BF16)],
-        swap, message, rate_pack, taps_pack, local,
-    )
-    message, relayed = lax.optimization_barrier((message, two))
-    three = lax.ppermute(message, "ctx", hops((third, fourth)))
-    two = lax.ppermute(relayed, "ctx", hops((first, turned), (second, third)))
-    local, mixed = call(
-        early_output, outs, *common, weights, product, swap, relayed, local,
-        scratch=room + work, flops=10**7, out_hbm=(1,), aliases={11: 0},
+    scan = lambda body, outs, *args: call(
+        lambda *refs: body(count, lanes, *refs), [*kept, *outs], *args, rate_pack, taps_pack
+    )
+
+    def gather_in(number, copies, members):
+        return lax.cond(
+            group == number, lambda c: gather(c, "ctx", members), lambda c: nothing((c.shape, c.dtype))[0], copies
+        )
+
+    def inner():
+        return call(
+            inner_conv, [((count, chans), F32)], rates, weights, product, scratch=[pltpu.VMEM((count, LANES), F32)], flops=10**7
+        )[0]
+
+    *first_kept, message = scan(first_scan, [small], gather_in(0, wide, groups))
+    low = lax.ppermute(message, "ctx", hops((first, second)))
+    *second_kept, to_third, to_fourth = scan(second_scan, [small, large], gather_in(1, wide, groups), low)
+    width = WIDE // 4
+    turned = [fourth[WIDE - width * (i // width + 1) + i % width] for i in range(WIDE)]
+    to_fourth = lax.ppermute(to_fourth, "ctx", hops((second, turned)))
+    to_third = lax.ppermute(to_third, "ctx", hops((second, third)))
+
+    def upper(copies):
+        *own, message, first_message = scan(third_scan, [small, large], gather_in(2, copies, runs))
+        across = lax.ppermute(first_message, "ctx", hops((runs[4], runs[6]), (runs[5], runs[7])))
+        cross = lax.ppermute(first_message, "ctx", hops((runs[4], runs[7]), (runs[5], runs[6])))
+        *own, message = scan(fourth_scan, [small], gather_in(3, copies, runs), *own, message)
+        following = lax.ppermute(message, "ctx", hops((runs[4], runs[5]), (runs[6], runs[7])))
+        (ahead,) = call(
+            lambda *refs: merge(count, lanes, *refs), [(small[0], F32)], across, cross, following, rate_pack, taps_pack
+        )
+        return inner(), *own, ahead
+
+    local, *upper_kept, ahead = lax.cond(
+        group >= 2, upper, lambda c: (inner(), *nothing(*kept, (small[0], F32))), near
     )
     (mixed,) = call(
-        last_output, outs[1:], *common, local, two, three, mixed,
-        scratch=work, in_hbm=(10,), out_hbm=(0,), aliases={10: 0},
+        output,
+        [((count, chans), BF16)],
+        *first_kept, *second_kept, *upper_kept, rate_pack, residue_pack, taps_pack, rates, query,
+        local, low, to_third, to_fourth, ahead,
+        scratch=[pltpu.VMEM((modes + 2 * SUB, chans), F32)],
     )
     return mixed
 

time: 45.4 us -> 39.7 us (0.87)
  the two profiles are of different devices: /device:TPU:2 before, /device:TPU:416 now
where the time goes in v9:
time: 39.7 us; the launch traced here: 39.4 us
  blocking collectives  20.5 us (52%)
  starting transfers between devices  8.58 us (22%)
  Pallas kernels  5.04 us (13%)
  waiting for transfers between devices  5.04 us (13%)
    all_to_all x2, blocking collectives, gather(): lax.all_to_all(copies, axis, 0, 0, tiled=True, axis_index_groups=groups)  20.5 us
    pallas_call x12, Pallas kernels, call(): pl.pallas_call(body, out_shape=shapes, in_specs=[pl.BlockSpec(memory_spac...  5.04 us
    ppermute x1, waiting for transfers between devices, per_device(): to_fourth = lax.ppermute(to_fourth, 'ctx', hops((second, turned)))  5.03 us
    ppermute x1, starting transfers between devices, upper(): lax.ppermute(message, 'ctx', hops((runs[4], runs[5]), (runs[6], runs[7])))  3.38 us
    ppermute x1, starting transfers between devices, per_device(): to_fourth = lax.ppermute(to_fourth, 'ctx', hops((second, turned)))  1.29 us
    ppermute x1, starting transfers between devices, upper(): lax.ppermute(first_message, 'ctx', hops((runs[4], runs[6]), (runs[5], run...  1.29 us
    ppermute x1, starting transfers between devices, upper(): lax.ppermute(first_message, 'ctx', hops((runs[4], runs[7]), (runs[5], run...  1.29 us
  transfers between devices with their start and end apart: 6, of which 1 were waited for; matrix products, arithmetic and copies ran while one was open for 0% of the time, Pallas kernels for 5%

profile of v9, /device:TPU:416, one launch (start us, length us, event | category | flops | bytes accessed | tf_op | source)
XLA Modules:
  0.0 39.4 jit_solution(14155258172687538383)
XLA Ops:
  0.0 1.1 %shard_map.55 = (bf16[128,512]{1,0:T(8,128)(2,1)S(1)}, f32[1,512]{1,0:T(1,128)S(1)}, f32[3,3,512]{2,1,0:T(4,128)S(1)}, f32[16,512]{1,0:T(8,128)S(1)}, f32[16,512...) custom-call(bf16[128,512]{1,0:T(8,128)(2,1)} %refs_0_, ...), custom_call_target="tpu_custom_call" | custom-call | bytes 217088 | tf_op jit(solution)/shard_map/pallas_call | solution.py:24
  1.1 9.6 %conditional.6 = (f32[8,1,128]{2,1,0:T(1,128)S(1)}) conditional(s32[]{:T(128)} %convert_element_type.18, f32[8,1,128]{2,1,0:T(1,128)S(1)} %get-tuple-element.97, f32[8,1,128]{2,1,0:T(1,128)S(1)} %get-tuple-element.97), branch_computations={%region_0.0_spmd, %region_1.0_spmd} | conditional | bytes 16392 | solution.py:389
  1.1 9.5 %all_to_all.20 = f32[8,1,128]{2,1,0:T(1,128)S(1)} all-to-all(f32[8,1,128]{2,1,0:T(1,128)S(1)} %copy.24), channel_id=1, replica_groups=mesh['ctx'=64,'ch'=8] {'ch'}, dimensions={0} | all-to-all | bytes 8192 | tf_op jit(solution)/shard_map/cond/branch_1_fun/all_to_all | solution.py:366
  10.6 0.9 %shard_map.56 = (bf16[128,512]{1,0:T(8,128)(2,1)S(1)}, f32[128,512]{1,0:T(8,128)S(1)}, bf16[16,80,128]{2,1,0:T(8,128)(2,1)S(1)}, bf16[8,80,128]{2,1,0:T(8,128)(2,1)S(1)}) custom-call(f32[8,1,128]{2,1,0:T(1,128)S(1)} %get-tuple-element.134.refs_0_, bf16[128,512]{1,0:T(8,128)(2,1)S(1)} %get-tuple-element.98.refs_1_, f32[1,512]{1,0:T(1,128)S(1)} %get-tuple-element.99.refs_2_, ...), custom_call_target="tpu_custom_call" | custom-call | bytes 188416 | tf_op jit(solution)/shard_map/pallas_call | solution.py:24
  11.6 0.7 %collective-permute-start.3 = (bf16[80,128]{1,0:T(8,128)(2,1)S(1)}, bf16[80,128]{1,0:T(8,128)(2,1)S(1)}, u32[]{:S(2)}, u32[]{:S(2)}) collective-permute-start(bf16[80,128]{1,0:T(8,128)(2,1)S(1)} %get-tuple-element.110), channel_id=1, source_target_pairs={{0,128},{8,136},{16,144},{24,152},{32,160},{40,168},{48,176},{56,1... | collective-permute-start | bytes 61448 | tf_op jit(solution)/shard_map/ppermute | solution.py:418
  12.3 0.0 collective-permute-done.3.refs_1_.low_ref
  12.4 1.3 %collective-permute-start.5 = (bf16[96,128]{1,0:T(8,128)(2,1)S(1)}, bf16[96,128]{1,0:T(8,128)(2,1)S(1)}, u32[]{:S(2)}, u32[]{:S(2)}) collective-permute-start(bf16[96,128]{1,0:T(8,128)(2,1)S(1)} %get-tuple-element.122), channel_id=1, source_target_pairs={{128,480},{136,488},{144,496},{152,504},{160,448},{168,456},{176,4... | collective-permute-start | bytes 73736 | tf_op jit(solution)/shard_map/ppermute | solution.py:422
  13.7 0.7 %collective-permute-start.4 = (bf16[80,128]{1,0:T(8,128)(2,1)S(1)}, bf16[80,128]{1,0:T(8,128)(2,1)S(1)}, u32[]{:S(2)}, u32[]{:S(2)}) collective-permute-start(bf16[80,128]{1,0:T(8,128)(2,1)S(1)} %get-tuple-element.121), channel_id=1, source_target_pairs={{128,256},{136,264},{144,272},{152,280},{160,288},{168,296},{176,3... | collective-permute-start | bytes 61448 | tf_op jit(solution)/shard_map/ppermute | solution.py:423
  14.3 18.9 %conditional.9 = (f32[128,512]{1,0:T(8,128)S(1)}, f32[64,128]{1,0:T(8,128)S(1)}, f32[24,128]{1,0:T(8,128)S(1)}, f32[80,128]{1,0:T(8,128)S(1)}) conditional(s32[]{:T(128)} %convert_element_type.21, (f32[16,512]{1,0:T(8,128)S(1)}, f32[16,512]{1,0:T(8,128)S(1)}, f32[128,512]{1,0:T(8,128)S(1)}) %tuple.49, (f32[16,512]{1,0:T(8,128)S(1)}, ...), branch_computations={%region_6.0_spmd, %region_7.0_spmd} | conditional | flops 10000004 | bytes 1878212 | solution.py:436
  14.4 1.3 %collective-permute-start = (bf16[96,128]{1,0:T(8,128)(2,1)S(1)}, bf16[96,128]{1,0:T(8,128)(2,1)S(1)}, u32[]{:S(2)}, u32[]{:S(2)}) collective-permute-start(bf16[96,128]{1,0:T(8,128)(2,1)S(1)} %get-tuple-element.64), channel_id=1, source_target_pairs={{256,384},{264,392},{272,400},{280,408},{288,416},{296,424},{304,4... | collective-permute-start | bytes 73736 | tf_op jit(solution)/shard_map/cond/branch_1_fun/ppermute | solution.py:427
  15.7 1.3 %collective-permute-start.1 = (bf16[96,128]{1,0:T(8,128)(2,1)S(1)}, bf16[96,128]{1,0:T(8,128)(2,1)S(1)}, u32[]{:S(2)}, u32[]{:S(2)}) collective-permute-start(bf16[96,128]{1,0:T(8,128)(2,1)S(1)} %get-tuple-element.64), channel_id=1, source_target_pairs={{256,448},{264,456},{272,464},{280,472},{288,480},{296,488},{304,4... | collective-permute-start | bytes 73736 | tf_op jit(solution)/shard_map/cond/branch_1_fun/ppermute | solution.py:428
  17.0 10.9 %conditional = (bf16[8,80,128]{2,1,0:T(8,128)(2,1)S(1)}) conditional(s32[]{:T(128)} %convert_element_type.12, () %tuple.36, bf16[8,80,128]{2,1,0:T(8,128)(2,1)S(1)} %get-tuple-element.56), branch_computations={%region_8.0_spmd, %region_9.0_spmd} | conditional | bytes 327688 | solution.py:408
  17.1 10.9 %all_to_all.23 = bf16[8,80,128]{2,1,0:T(8,128)(2,1)S(1)} all-to-all(bf16[8,80,128]{2,1,0:T(8,128)(2,1)S(1)} %param.8), channel_id=1, replica_groups={{0,8,16,24,32,40,48,56},{64,72,80,88,96,104,112,120},{128,136,144,152,1..., dimensions={0} | all-to-all | bytes 327680 | tf_op jit(solution)/shard_map/cond/branch_1_fun/cond/branch_1_fun/all_to_all | solution.py:366
  28.0 0.1 branch_1_fun.6
  28.1 3.4 %collective-permute-start.2 = (bf16[80,128]{1,0:T(8,128)(2,1)S(1)}, bf16[80,128]{1,0:T(8,128)(2,1)S(1)}, u32[]{:S(2)}, u32[]{:S(2)}) collective-permute-start(bf16[80,128]{1,0:T(8,128)(2,1)S(1)} %get-tuple-element.65), channel_id=1, source_target_pairs={{256,320},{264,328},{272,336},{280,344},{288,352},{296,360},{304,3... | collective-permute-start | bytes 61448 | tf_op jit(solution)/shard_map/cond/branch_1_fun/ppermute | solution.py:430
  31.5 1.6 %branch_1_fun.4 = f32[128,512]{1,0:T(8,128)S(1)} custom-call(f32[16,512]{1,0:T(8,128)S(1)} %get-tuple-element.52.rate_ref, f32[16,512]{1,0:T(8,128)S(1)} %get-tuple-element.53.residue_ref, f32[128,512]{1,0:T(8,128)S(1)} %get-tuple-element.54.product_ref), custom_call_target="tpu_custom_call" | custom-call | flops 10000000 | bytes 327680 | tf_op jit(solution)/shard_map/cond/branch_1_fun/pallas_call | solution.py:24
  33.1 0.0 collective-permute-done.2.refs_2_
  33.1 0.0 collective-permute-done.refs_0_
  33.1 0.0 collective-permute-done.1.refs_1_
  33.1 0.1 branch_1_fun.7
  33.2 0.0 collective-permute-done.4.third_ref
  33.2 5.0 %collective-permute-done.5.fourth_ref = bf16[96,128]{1,0:T(8,128)(2,1)S(1)} collective-permute-done((bf16[96,128]{1,0:T(8,128)(2,1)S(1)}, bf16[96,128]{1,0:T(8,128)(2,1)S(1)}, u32[]{:S(2)}, u32[]{:S(2)}) %collective-permute-start.5) | collective-permute-done | bytes 24608 | tf_op jit(solution)/shard_map/ppermute | solution.py:422
  38.3 1.2 %shard_map.59 = bf16[128,512]{1,0:T(8,128)(2,1)} custom-call(f32[64,128]{1,0:T(8,128)S(1)} %get-tuple-element.108.first_before, f32[24,128]{1,0:T(8,128)S(1)} %get-tuple-element.109.first_edge, f32[64,128]{1,0:T(8,128)S(1)} %get-tuple-element.111.second_before, f32[24,128]{1,0:T(8,128)S(1)} %get-tuple-element.112.second_edge, ...), custom_call_target="tpu_custom_call" | custom-call | bytes 751616 | tf_op jit(solution)/shard_map/pallas_call | solution.py:24
  (10 shorter events, 0.1 us)
Async XLA Ops:
  11.6 0.7 %collective-permute-start.3 = (bf16[80,128]{1,0:T(8,128)(2,1)S(1)}, bf16[80,128]{1,0:T(8,128)(2,1)S(1)}, u32[]{:S(2)}, u32[]{:S(2)}) collective-permute-start(bf16[80,128]{1,0:T(8,128)(2,1)S(1)} %get-tuple-element.110), channel_id=1, source_target_pairs={{0,128},{8,136},{16,144},{24,152},{32,160},{40,168},{48,176},{56,1... | collective-permute-start | bytes 61448 | tf_op jit(solution)/shard_map/ppermute | solution.py:418
  12.4 25.9 %collective-permute-start.5 = (bf16[96,128]{1,0:T(8,128)(2,1)S(1)}, bf16[96,128]{1,0:T(8,128)(2,1)S(1)}, u32[]{:S(2)}, u32[]{:S(2)}) collective-permute-start(bf16[96,128]{1,0:T(8,128)(2,1)S(1)} %get-tuple-element.122), channel_id=1, source_target_pairs={{128,480},{136,488},{144,496},{152,504},{160,448},{168,456},{176,4... | collective-permute-start | bytes 73736 | tf_op jit(solution)/shard_map/ppermute | solution.py:422
  13.7 19.6 %collective-permute-start.4 = (bf16[80,128]{1,0:T(8,128)(2,1)S(1)}, bf16[80,128]{1,0:T(8,128)(2,1)S(1)}, u32[]{:S(2)}, u32[]{:S(2)}) collective-permute-start(bf16[80,128]{1,0:T(8,128)(2,1)S(1)} %get-tuple-element.121), channel_id=1, source_target_pairs={{128,256},{136,264},{144,272},{152,280},{160,288},{168,296},{176,3... | collective-permute-start | bytes 61448 | tf_op jit(solution)/shard_map/ppermute | solution.py:423
  14.4 18.7 %collective-permute-start = (bf16[96,128]{1,0:T(8,128)(2,1)S(1)}, bf16[96,128]{1,0:T(8,128)(2,1)S(1)}, u32[]{:S(2)}, u32[]{:S(2)}) collective-permute-start(bf16[96,128]{1,0:T(8,128)(2,1)S(1)} %get-tuple-element.64), channel_id=1, source_target_pairs={{256,384},{264,392},{272,400},{280,408},{288,416},{296,424},{304,4... | collective-permute-start | bytes 73736 | tf_op jit(solution)/shard_map/cond/branch_1_fun/ppermute | solution.py:427
  15.7 17.4 %collective-permute-start.1 = (bf16[96,128]{1,0:T(8,128)(2,1)S(1)}, bf16[96,128]{1,0:T(8,128)(2,1)S(1)}, u32[]{:S(2)}, u32[]{:S(2)}) collective-permute-start(bf16[96,128]{1,0:T(8,128)(2,1)S(1)} %get-tuple-element.64), channel_id=1, source_target_pairs={{256,448},{264,456},{272,464},{280,472},{288,480},{296,488},{304,4... | collective-permute-start | bytes 73736 | tf_op jit(solution)/shard_map/cond/branch_1_fun/ppermute | solution.py:428
  28.1 5.0 %collective-permute-start.2 = (bf16[80,128]{1,0:T(8,128)(2,1)S(1)}, bf16[80,128]{1,0:T(8,128)(2,1)S(1)}, u32[]{:S(2)}, u32[]{:S(2)}) collective-permute-start(bf16[80,128]{1,0:T(8,128)(2,1)S(1)} %get-tuple-element.65), channel_id=1, source_target_pairs={{256,320},{264,328},{272,336},{280,344},{288,352},{296,360},{304,3... | collective-permute-start | bytes 61448 | tf_op jit(solution)/shard_map/cond/branch_1_fun/ppermute | solution.py:430

commit v10 on v9

--- a/solution.py
+++ b/solution.py
@@ -16,10 +16,10 @@
 BF16 = jnp.bfloat16
 
 
-def call(body, outs, *args, scratch=(), flops=0, space=pltpu.VMEM, in_hbm=(), out_hbm=(), aliases=None):
+def call(body, outs, *args, scratch=(), flops=0, space=pltpu.VMEM, in_hbm=(), out_hbm=(), out_any=(), aliases=None):
     shapes = [jax.ShapeDtypeStruct(s, d) for s, d in outs]
     spaces = [pltpu.HBM if i in in_hbm else space for i in range(len(args))]
-    out_spaces = [pl.ANY if i in out_hbm else pltpu.VMEM for i in range(len(outs))]
+    out_spaces = [pltpu.HBM if i in out_hbm else pl.ANY if i in out_any else pltpu.VMEM for i in range(len(outs))]
     moved = sum(a.size * a.dtype.itemsize for a in args)
     return pl.pallas_call(
         body,
@@ -207,13 +207,20 @@
         write(near_scan(block, lanes, got_ref, rate_ref, taps_ref, before_ref, edge_ref), message_ref)
 
 
-def second_scan(block, lanes, got_ref, came_ref, rate_ref, taps_ref, before_ref, edge_ref, *message_refs):
+def second_scan(block, lanes, got_ref, rate_ref, taps_ref, before_ref, edge_ref, message_ref):
     @pl.when(lax.axis_index("ctx") // WIDE == 1)
     def _():
+        message_ref[...] = near_scan(block, lanes, got_ref, rate_ref, taps_ref, before_ref, edge_ref)
+
+
+def relay(block, lanes, came_ref, own_ref, rate_ref, taps_ref, kept_ref, *message_refs):
+    @pl.when(lax.axis_index("ctx") // WIDE == 1)
+    def _():
         rates = rate_ref[...]
-        own = near_scan(block, lanes, got_ref, rate_ref, taps_ref, before_ref, edge_ref)
         state, last = jnp.zeros_like(rates), [jnp.zeros((lanes, LANES), F32)] * 2
-        for run in (came_ref[...].astype(F32), own):
+        came = came_ref[...].astype(F32)
+        kept_ref[...] = came
+        for run in (came, own_ref[...]):
             state, last = step_over(block * WIDE, lanes, rates, taps_ref, state, last, run)
         write(jnp.concatenate([state, *last], axis=0), *message_refs)
 
@@ -342,24 +349,62 @@
     lax.fori_loop(0, lanes, one_lane, 0)
 
 
-def output(first_before, first_edge, second_before, second_edge, upper_before, upper_edge, rate_pack, residue_pack, taps_ref, rate_ref, query_ref, local_ref, low_ref, third_ref, fourth_ref, ahead_ref, mixed_ref, state_ref):
+def leave(mixed_ref, out_ref, sem):
+    copy = pltpu.make_async_copy(mixed_ref, out_ref, sem)
+    copy.start()
+    copy.wait()
+
+
+def convolves_early():
     index = lax.axis_index("ctx")
-    group, run = index // WIDE, index // NEAR
+    return index < WIDE + WIDE // 2
+
+
+def early_inner(rate_ref, residue_ref, product_ref, after_ref, local_ref, filter_ref):
+    @pl.when(convolves_early())
+    def _():
+        inner_conv(rate_ref, residue_ref, product_ref, local_ref, filter_ref)
+
+
+def lower_output(first_before, first_edge, second_before, second_edge, rate_pack, residue_pack, taps_ref, rate_ref, query_ref, residue_ref, product_ref, held_ref, low_ref, out_ref, filter_ref, local_ref, state_ref, mixed_ref, sem):
+    early = convolves_early()
+
+    @pl.when(early)
+    def _():
+        local_ref[...] = held_ref[...]
+
+    @pl.when(jnp.logical_not(early))
+    def _():
+        inner_conv(rate_ref, residue_ref, product_ref, local_ref, filter_ref)
+
+    index = lax.axis_index("ctx")
+    rates = rate_pack[...]
+    second = index >= WIDE
+    state, last = jnp.zeros_like(rates), [jnp.zeros((taps_ref.shape[0] // 9, LANES), F32)] * 2
+    after, after_last = step_over(local_ref.shape[0] * WIDE, len(last[0]), rates, taps_ref, state, last, low_ref[...])
+    state, last = jnp.where(second, after, state), [jnp.where(second, a, b) for a, b in zip(after_last, last)]
+    before = jnp.where(second, second_before[...], first_before[...])
+    edges = jnp.where(second, second_edge[...], first_edge[...])
+    finish(index % WIDE, state, last, edges, before, rate_pack, residue_pack, taps_ref, rate_ref, query_ref, local_ref, mixed_ref, state_ref)
+    leave(mixed_ref, out_ref, sem)
+
+
+def upper_output(before_ref, edge_ref, rate_pack, residue_pack, taps_ref, rate_ref, query_ref, local_ref, third_ref, fourth_ref, ahead_ref, held_ref, out_ref, state_ref, mixed_ref, sem):
+    index = lax.axis_index("ctx")
+    run = index // NEAR
     states = rate_pack.shape[0]
     lanes = taps_ref.shape[0] // 9
-    count = local_ref.shape[0]
-    came = third_ref[...].astype(F32) + fourth_ref[: states + 4 * lanes].astype(F32)
-    state, last = came[:states], (came[states : states + lanes], came[states + lanes : states + 2 * lanes])
-    length = jnp.where(group == 1, WIDE, NEAR * jnp.maximum(run - 4, 1)) * count
-    message = jnp.where(group == 1, low_ref[...].astype(F32), ahead_ref[...])
-    needed = (group == 1) | (run > 4)
-    after, after_last = step_over(length.astype(F32), lanes, rate_pack[...], taps_ref, state, last, message)
-    state, last = jnp.where(needed, after, state), [jnp.where(needed, a, b) for a, b in zip(after_last, last)]
-    place = jnp.where(group < 2, index % WIDE, index % NEAR)
-    pick = lambda a, b, c: jnp.where(group == 0, a[...], jnp.where(group == 1, b[...], c[...]))
-    before = pick(first_before, second_before, upper_before)
-    edges = pick(first_edge, second_edge, upper_edge)
-    finish(place, state, last, edges, before, rate_pack, residue_pack, taps_ref, rate_ref, query_ref, local_ref, mixed_ref, state_ref)
+
+    @pl.when(index >= 2 * WIDE)
+    def _():
+        came = third_ref[...].astype(F32) + fourth_ref[: states + 4 * lanes].astype(F32)
+        state, last = came[:states], (came[states : states + lanes], came[states + lanes : states + 2 * lanes])
+        length = (NEAR * jnp.maximum(run - 4, 1) * local_ref.shape[0]).astype(F32)
+        after, after_last = step_over(length, lanes, rate_pack[...], taps_ref, state, last, ahead_ref[...])
+        needed = run > 4
+        state, last = jnp.where(needed, after, state), [jnp.where(needed, a, b) for a, b in zip(after_last, last)]
+        finish(index % NEAR, state, last, edge_ref, before_ref, rate_pack, residue_pack, taps_ref, rate_ref, query_ref, local_ref, mixed_ref, state_ref)
+        leave(mixed_ref, out_ref, sem)
 
 
 def gather(copies, axis, groups=None):
@@ -397,7 +442,7 @@
     group = lax.shift_right_logical(index, WIDE.bit_length() - 1)
     small, large = ((states + 4 * lanes, LANES), BF16), ((states + 8 * lanes, LANES), BF16)
     kept = [((states, LANES), F32), ((6 * lanes, LANES), F32)]
-    nothing = lambda *shapes: tuple(call(lambda *refs: None, shapes, out_hbm=range(len(shapes))))
+    nothing = lambda *shapes: tuple(call(lambda *refs: None, shapes, out_any=range(len(shapes))))
     hops = lambda *ends: [pair for a, b in ends for pair in zip(a, b)]
     first, second, third, fourth = groups
     scan = lambda body, outs, *args: call(
@@ -414,12 +459,25 @@
             inner_conv, [((count, chans), F32)], rates, weights, product, scratch=[pltpu.VMEM((count, LANES), F32)], flops=10**7
         )[0]
 
-    *first_kept, message = scan(first_scan, [small], gather_in(0, wide, groups))
-    low = lax.ppermute(message, "ctx", hops((first, second)))
-    *second_kept, to_third, to_fourth = scan(second_scan, [small, large], gather_in(1, wide, groups), low)
-    width = WIDE // 4
-    turned = [fourth[WIDE - width * (i // width + 1) + i % width] for i in range(WIDE)]
-    to_fourth = lax.ppermute(to_fourth, "ctx", hops((second, turned)))
+    room = [pltpu.VMEM((count, LANES), F32)]
+    work = [pltpu.VMEM((modes + 2 * SUB, chans), F32), pltpu.VMEM((count, chans), BF16), pltpu.SemaphoreType.DMA]
+    whole = (small[0], F32)
+    held, result = ((count, chans), F32), ((count, chans), BF16)
+
+    def lower(copies):
+        *first_kept, message = scan(first_scan, [small], gather_in(0, copies, groups))
+        low = lax.ppermute(message, "ctx", hops((first, second)))
+        (local,) = call(early_inner, [held], rates, weights, product, message, scratch=room, flops=10**7)
+        copies, local = lax.optimization_barrier((copies, local))
+        *second_kept, message = scan(second_scan, [whole], gather_in(1, copies, groups))
+        onward = call(lambda *refs: relay(count, lanes, *refs), [whole, small, large], low, message, rate_pack, taps_pack)
+        return *first_kept, *second_kept, local, *onward
+
+    *lower_kept, to_third, to_fourth = lax.cond(
+        group < 2, lower, lambda c: nothing(*kept, *kept, held, whole, small, large), wide
+    )
+    half = WIDE // 2
+    to_fourth = lax.ppermute(to_fourth, "ctx", hops((second, fourth[half:] + fourth[:half])))
     to_third = lax.ppermute(to_third, "ctx", hops((second, third)))
 
     def upper(copies):
@@ -429,19 +487,23 @@
         *own, message = scan(fourth_scan, [small], gather_in(3, copies, runs), *own, message)
         following = lax.ppermute(message, "ctx", hops((runs[4], runs[5]), (runs[6], runs[7])))
         (ahead,) = call(
-            lambda *refs: merge(count, lanes, *refs), [(small[0], F32)], across, cross, following, rate_pack, taps_pack
+            lambda *refs: merge(count, lanes, *refs), [whole], across, cross, following, rate_pack, taps_pack
         )
-        return inner(), *own, ahead
-
-    local, *upper_kept, ahead = lax.cond(
-        group >= 2, upper, lambda c: (inner(), *nothing(*kept, (small[0], F32))), near
-    )
+        return *call(lambda *refs: None, [result], out_hbm=(0,)), *own, inner(), ahead
+
+    def rest(copies):
+        common = [rate_pack, residue_pack, taps_pack, rates, query, weights, product]
+        (mixed,) = call(
+            lower_output, [result], *lower_kept[:4], *common, *lower_kept[4:], scratch=room + [pltpu.VMEM(*held)] + work, out_hbm=(0,)
+        )
+        return mixed, *nothing(*kept, held, whole)
+
+    mixed, *own, local, ahead = lax.cond(group >= 2, upper, rest, near)
     (mixed,) = call(
-        output,
-        [((count, chans), BF16)],
-        *first_kept, *second_kept, *upper_kept, rate_pack, residue_pack, taps_pack, rates, query,
-        local, low, to_third, to_fourth, ahead,
-        scratch=[pltpu.VMEM((modes + 2 * SUB, chans), F32)],
+        upper_output,
+        [result],
+        *own, rate_pack, residue_pack, taps_pack, rates, query, local, to_third, to_fourth, ahead, mixed,
+        scratch=work, in_hbm=(11,), out_hbm=(0,), aliases={11: 0},
     )
     return mixed
 

time: 39.7 us -> 39.1 us (0.985)
  the two profiles are of different devices: /device:TPU:416 before, /device:TPU:448 now
where the time goes in v10:
time: 39.1 us; the launch traced here: 38.9 us
  blocking collectives  20.8 us (53%)
  waiting for transfers between devices  6.98 us (18%)
  starting transfers between devices  5.83 us (15%)
  Pallas kernels  4.98 us (13%)
    all_to_all x2, blocking collectives, gather(): lax.all_to_all(copies, axis, 0, 0, tiled=True, axis_index_groups=groups)  20.8 us
    pallas_call x10, Pallas kernels, call(): pl.pallas_call(body, out_shape=shapes, in_specs=[pl.BlockSpec(memory_spac...  4.98 us
    ppermute x1, waiting for transfers between devices, upper(): lax.ppermute(message, 'ctx', hops((runs[4], runs[5]), (runs[6], runs[7])))  3.64 us
    ppermute x1, waiting for transfers between devices, per_device(): lax.ppermute(to_fourth, 'ctx', hops((second, fourth[half:] + fourth[:half...  3.33 us
    ppermute x1, starting transfers between devices, per_device(): lax.ppermute(to_fourth, 'ctx', hops((second, fourth[half:] + fourth[:half...  1.29 us
    ppermute x1, starting transfers between devices, upper(): lax.ppermute(first_message, 'ctx', hops((runs[4], runs[7]), (runs[5], run...  1.29 us
    ppermute x1, starting transfers between devices, upper(): lax.ppermute(first_message, 'ctx', hops((runs[4], runs[6]), (runs[5], run...  1.29 us
    ppermute x1, starting transfers between devices, upper(): lax.ppermute(message, 'ctx', hops((runs[4], runs[5]), (runs[6], runs[7])))  1.29 us
  transfers between devices with their start and end apart: 5, of which 2 were waited for; matrix products, arithmetic and copies ran while one was open for 0% of the time, Pallas kernels for 5%

profile of v10, /device:TPU:448, one launch (start us, length us, event | category | flops | bytes accessed | tf_op | source)
XLA Modules:
  0.0 38.9 jit_solution(11156985281736294609)
XLA Ops:
  0.0 1.1 %shard_map.55 = (bf16[128,512]{1,0:T(8,128)(2,1)S(1)}, f32[1,512]{1,0:T(1,128)S(1)}, f32[3,3,512]{2,1,0:T(4,128)S(1)}, f32[16,512]{1,0:T(8,128)S(1)}, f32[16,512...) custom-call(bf16[128,512]{1,0:T(8,128)(2,1)} %refs_0_, ...), custom_call_target="tpu_custom_call" | custom-call | bytes 217088 | tf_op jit(solution)/shard_map/pallas_call | solution.py:24
  1.1 9.6 %conditional.7 = (f32[8,1,128]{2,1,0:T(1,128)S(1)}) conditional(s32[]{:T(128)} %convert_element_type.21, f32[8,1,128]{2,1,0:T(1,128)S(1)} %get-tuple-element.162, f32[8,1,128]{2,1,0:T(1,128)S(1)} %get-tuple-element.162), branch_computations={%region_0.0_spmd, %region_1.0_spmd} | conditional | bytes 16392 | solution.py:434
  1.1 9.5 %all_to_all.20 = f32[8,1,128]{2,1,0:T(1,128)S(1)} all-to-all(f32[8,1,128]{2,1,0:T(1,128)S(1)} %copy.44), channel_id=1, replica_groups=mesh['ctx'=64,'ch'=8] {'ch'}, dimensions={0} | all-to-all | bytes 8192 | tf_op jit(solution)/shard_map/cond/branch_1_fun/all_to_all | solution.py:411
  10.6 0.9 %shard_map.56 = (bf16[128,512]{1,0:T(8,128)(2,1)S(1)}, f32[128,512]{1,0:T(8,128)S(1)}, bf16[16,80,128]{2,1,0:T(8,128)(2,1)S(1)}, bf16[8,80,128]{2,1,0:T(8,128)(2,1)S(1)}) custom-call(f32[8,1,128]{2,1,0:T(1,128)S(1)} %get-tuple-element.221.refs_0_, bf16[128,512]{1,0:T(8,128)(2,1)S(1)} %get-tuple-element.163.refs_1_, f32[1,512]{1,0:T(1,128)S(1)} %get-tuple-element.164.refs_2_, ...), custom_call_target="tpu_custom_call" | custom-call | bytes 188416 | tf_op jit(solution)/shard_map/pallas_call | solution.py:24
  11.6 1.3 %collective-permute-start.5 = (bf16[96,128]{1,0:T(8,128)(2,1)S(1)}, bf16[96,128]{1,0:T(8,128)(2,1)S(1)}, u32[]{:S(2)}, u32[]{:S(2)}) collective-permute-start(bf16[96,128]{1,0:T(8,128)(2,1)S(1)} %get-tuple-element.188), channel_id=1, source_target_pairs={{128,448},{136,456},{144,464},{152,472},{160,480},{168,488},{176,4... | collective-permute-start | bytes 73736 | tf_op jit(solution)/shard_map/ppermute | solution.py:480
  12.9 0.7 %collective-permute-start.4 = (bf16[80,128]{1,0:T(8,128)(2,1)S(1)}, bf16[80,128]{1,0:T(8,128)(2,1)S(1)}, u32[]{:S(2)}, u32[]{:S(2)}) collective-permute-start(bf16[80,128]{1,0:T(8,128)(2,1)S(1)} %get-tuple-element.187), channel_id=1, source_target_pairs={{128,256},{136,264},{144,272},{152,280},{160,288},{168,296},{176,3... | collective-permute-start | bytes 61448 | tf_op jit(solution)/shard_map/ppermute | solution.py:481
  13.6 20.8 %conditional.9 = (bf16[128,512]{1,0:T(8,128)(2,1)S(1)}, f32[64,128]{1,0:T(8,128)S(1)}, f32[24,128]{1,0:T(8,128)S(1)}, f32[128,512]{1,0:T(8,128)S(1)}, f32[80,128]{1,0:T(8,128)S(1)}) conditional(s32[]{:T(128)} %convert_element_type.22, (f32[64,128]{1,0:T(8,128)S(1)}, f32[24,128]{1,0:T(8,128)S(1)}, f32[64,128]{1,0:T(8,128)S(1)}, ...), branch_computations={%region_8.0_spmd, %region_9.0_spmd} | conditional | flops 10000004 | bytes 1878220 | solution.py:501
  13.7 1.3 %collective-permute-start.2 = (bf16[96,128]{1,0:T(8,128)(2,1)S(1)}, bf16[96,128]{1,0:T(8,128)(2,1)S(1)}, u32[]{:S(2)}, u32[]{:S(2)}) collective-permute-start(bf16[96,128]{1,0:T(8,128)(2,1)S(1)} %get-tuple-element.127), channel_id=1, source_target_pairs={{256,448},{264,456},{272,464},{280,472},{288,480},{296,488},{304,4... | collective-permute-start | bytes 73736 | tf_op jit(solution)/shard_map/cond/branch_1_fun/ppermute | solution.py:486
  15.0 1.3 %collective-permute-start.1 = (bf16[96,128]{1,0:T(8,128)(2,1)S(1)}, bf16[96,128]{1,0:T(8,128)(2,1)S(1)}, u32[]{:S(2)}, u32[]{:S(2)}) collective-permute-start(bf16[96,128]{1,0:T(8,128)(2,1)S(1)} %get-tuple-element.127), channel_id=1, source_target_pairs={{256,384},{264,392},{272,400},{280,408},{288,416},{296,424},{304,4... | collective-permute-start | bytes 73736 | tf_op jit(solution)/shard_map/cond/branch_1_fun/ppermute | solution.py:485
  16.3 11.3 %conditional.2 = (bf16[8,80,128]{2,1,0:T(8,128)(2,1)S(1)}) conditional(s32[]{:T(128)} %convert_element_type.16, () %tuple.44, bf16[8,80,128]{2,1,0:T(8,128)(2,1)S(1)} %get-tuple-element.116), branch_computations={%region_10.0_spmd, %region_11.0_spmd} | conditional | bytes 327688 | solution.py:453
  16.3 11.3 %all_to_all.23 = bf16[8,80,128]{2,1,0:T(8,128)(2,1)S(1)} all-to-all(bf16[8,80,128]{2,1,0:T(8,128)(2,1)S(1)} %param.10), channel_id=1, replica_groups={{0,8,16,24,32,40,48,56},{64,72,80,88,96,104,112,120},{128,136,144,152,1..., dimensions={0} | all-to-all | bytes 327680 | tf_op jit(solution)/shard_map/cond/branch_1_fun/cond/branch_1_fun/all_to_all | solution.py:411
  27.6 0.1 branch_1_fun.15
  27.7 1.3 %collective-permute-start.3 = (bf16[80,128]{1,0:T(8,128)(2,1)S(1)}, bf16[80,128]{1,0:T(8,128)(2,1)S(1)}, u32[]{:S(2)}, u32[]{:S(2)}) collective-permute-start(bf16[80,128]{1,0:T(8,128)(2,1)S(1)} %get-tuple-element.128), channel_id=1, source_target_pairs={{256,320},{264,328},{272,336},{280,344},{288,352},{296,360},{304,3... | collective-permute-start | bytes 61448 | tf_op jit(solution)/shard_map/cond/branch_1_fun/ppermute | solution.py:488
  29.0 1.6 %branch_1_fun.16 = f32[128,512]{1,0:T(8,128)S(1)} custom-call(f32[16,512]{1,0:T(8,128)S(1)} %get-tuple-element.124.rate_ref, f32[16,512]{1,0:T(8,128)S(1)} %get-tuple-element.125.residue_ref, f32[128,512]{1,0:T(8,128)S(1)} %get-tuple-element.126.product_ref), custom_call_target="tpu_custom_call" | custom-call | flops 10000000 | bytes 327680 | tf_op jit(solution)/shard_map/cond/branch_1_fun/pallas_call | solution.py:24
  30.6 3.6 %collective-permute-done.3.refs_2_ = bf16[80,128]{1,0:T(8,128)(2,1)S(1)} collective-permute-done((bf16[80,128]{1,0:T(8,128)(2,1)S(1)}, bf16[80,128]{1,0:T(8,128)(2,1)S(1)}, u32[]{:S(2)}, u32[]{:S(2)}) %collective-permute-start.3) | collective-permute-done | bytes 20512 | tf_op jit(solution)/shard_map/cond/branch_1_fun/ppermute | solution.py:488
  34.3 0.0 collective-permute-done.2.refs_1_
  34.3 0.0 collective-permute-done.1.refs_0_
  34.3 0.1 branch_1_fun.17
  34.4 0.0 copy-start
  34.4 0.0 collective-permute-done.4.third_ref
  34.4 3.3 %collective-permute-done.5.fourth_ref = bf16[96,128]{1,0:T(8,128)(2,1)S(1)} collective-permute-done((bf16[96,128]{1,0:T(8,128)(2,1)S(1)}, bf16[96,128]{1,0:T(8,128)(2,1)S(1)}, u32[]{:S(2)}, u32[]{:S(2)}) %collective-permute-start.5) | collective-permute-done | bytes 24608 | tf_op jit(solution)/shard_map/ppermute | solution.py:480
  37.7 0.0 copy-done
  37.7 1.2 %shard_map.57 = bf16[128,512]{1,0:T(8,128)(2,1)} custom-call(f32[64,128]{1,0:T(8,128)S(1)} %get-tuple-element.184.before_ref, f32[24,128]{1,0:T(8,128)S(1)} %get-tuple-element.185.edge_ref, f32[64,128]{1,0:T(8,128)S(1)} %get-tuple-element.171.rate_pack, f32[64,128]{1,0:T(8,128)S(1)} %get-tuple-element.179.residue_pack, ...), custom_call_target="tpu_custom_call", output_to_operand_aliasing={{}: (11, {})} | custom-call | bytes 772096 | tf_op jit(solution)/shard_map/pallas_call | solution.py:24
  (7 shorter events, 0.1 us)
Async XLA Ops:
  11.6 26.1 %collective-permute-start.5 = (bf16[96,128]{1,0:T(8,128)(2,1)S(1)}, bf16[96,128]{1,0:T(8,128)(2,1)S(1)}, u32[]{:S(2)}, u32[]{:S(2)}) collective-permute-start(bf16[96,128]{1,0:T(8,128)(2,1)S(1)} %get-tuple-element.188), channel_id=1, source_target_pairs={{128,448},{136,456},{144,464},{152,472},{160,480},{168,488},{176,4... | collective-permute-start | bytes 73736 | tf_op jit(solution)/shard_map/ppermute | solution.py:480
  12.9 21.5 %collective-permute-start.4 = (bf16[80,128]{1,0:T(8,128)(2,1)S(1)}, bf16[80,128]{1,0:T(8,128)(2,1)S(1)}, u32[]{:S(2)}, u32[]{:S(2)}) collective-permute-start(bf16[80,128]{1,0:T(8,128)(2,1)S(1)} %get-tuple-element.187), channel_id=1, source_target_pairs={{128,256},{136,264},{144,272},{152,280},{160,288},{168,296},{176,3... | collective-permute-start | bytes 61448 | tf_op jit(solution)/shard_map/ppermute | solution.py:481
  13.7 20.6 %collective-permute-start.2 = (bf16[96,128]{1,0:T(8,128)(2,1)S(1)}, bf16[96,128]{1,0:T(8,128)(2,1)S(1)}, u32[]{:S(2)}, u32[]{:S(2)}) collective-permute-start(bf16[96,128]{1,0:T(8,128)(2,1)S(1)} %get-tuple-element.127), channel_id=1, source_target_pairs={{256,448},{264,456},{272,464},{280,472},{288,480},{296,488},{304,4... | collective-permute-start | bytes 73736 | tf_op jit(solution)/shard_map/cond/branch_1_fun/ppermute | solution.py:486
  15.0 19.3 %collective-permute-start.1 = (bf16[96,128]{1,0:T(8,128)(2,1)S(1)}, bf16[96,128]{1,0:T(8,128)(2,1)S(1)}, u32[]{:S(2)}, u32[]{:S(2)}) collective-permute-start(bf16[96,128]{1,0:T(8,128)(2,1)S(1)} %get-tuple-element.127), channel_id=1, source_target_pairs={{256,384},{264,392},{272,400},{280,408},{288,416},{296,424},{304,4... | collective-permute-start | bytes 73736 | tf_op jit(solution)/shard_map/cond/branch_1_fun/ppermute | solution.py:485
  27.7 6.6 %collective-permute-start.3 = (bf16[80,128]{1,0:T(8,128)(2,1)S(1)}, bf16[80,128]{1,0:T(8,128)(2,1)S(1)}, u32[]{:S(2)}, u32[]{:S(2)}) collective-permute-start(bf16[80,128]{1,0:T(8,128)(2,1)S(1)} %get-tuple-element.128), channel_id=1, source_target_pairs={{256,320},{264,328},{272,336},{280,344},{288,352},{296,360},{304,3... | collective-permute-start | bytes 61448 | tf_op jit(solution)/shard_map/cond/branch_1_fun/ppermute | solution.py:488
  34.4 3.4 %copy-start = (bf16[128,512]{1,0:T(8,128)(2,1)}, bf16[128,512]{1,0:T(8,128)(2,1)S(1)}, u32[]{:S(2)}) copy-start(bf16[128,512]{1,0:T(8,128)(2,1)S(1)} %get-tuple-element.190.held_ref) | copy-start | bytes 393220

commit v11 on v10

--- a/solution.py
+++ b/solution.py
@@ -41,20 +41,22 @@
     count = 5
     held, outs, refs = refs[:count], refs[count : 2 * count], refs[2 * count :]
     sums_ref, taps_pack, rate_pack, residue_pack, sem = refs
-    copies = [pltpu.make_async_copy(source, target, sem.at[i]) for i, (source, target) in enumerate(zip(held, outs))]
+    stream_ref, _, taps_ref, rate_ref, residue_ref = outs
+    lanes = stream_ref.shape[1] // LANES
+    cuts = [pl.ds(l * LANES, LANES) for l in range(lanes)]
+    copies = [pltpu.make_async_copy(held[0].at[:, at], stream_ref.at[:, at], sem.at[i]) for i, at in enumerate(cuts)]
+    copies += [pltpu.make_async_copy(held[i], outs[i], sem.at[lanes + i - 1]) for i in range(1, count)]
     for copy in copies:
         copy.start()
-    copies[0].wait()
-    stream_ref, _, taps_ref, rate_ref, residue_ref = outs
-    lanes = stream_ref.shape[1] // LANES
     total = 0.0
-    for l in range(lanes):
-        values = stream_ref[:, l * LANES : (l + 1) * LANES].astype(F32)
+    for copy, at in zip(copies, cuts):
+        copy.wait()
+        values = stream_ref[:, at].astype(F32)
         total = total + values * values
     sums = jnp.sum(total.T, axis=0, keepdims=True)
     for peer in range(sums_ref.shape[0]):
         sums_ref[peer] = sums
-    for copy in copies[1:]:
+    for copy in copies[lanes:]:
         copy.wait()
     rate_pack[...] = pack(rate_ref)
     residue_pack[...] = pack(residue_ref)
@@ -121,7 +123,7 @@
             end_ref[pl.ds(mode, 1), at] = jnp.sum(total * jnp.exp(-rate * lag), axis=0, keepdims=True)
         return carry
 
-    lax.fori_loop(0, lanes, one_lane, 0)
+    lax.fori_loop(0, lanes, one_lane, 0, unroll=True)
     whole_ref[: lanes * modes] = pack(end_ref)
     for e in range(4):
         for l in range(lanes):
@@ -174,23 +176,27 @@
     return state, [jnp.where(place > 0, a, b) for a, b in zip(inside, last)]
 
 
+def slot(place, size):
+    return size - 1 - place
+
+
 def near_scan(block, lanes, got_ref, rate_ref, taps_ref, before_ref, edge_ref):
     size = got_ref.shape[0]
     place = lax.axis_index("ctx") % size
     states = rate_ref.shape[0]
     rates = rate_ref[...]
-    run = got_ref[0].astype(F32)
+    run = got_ref[slot(0, size)].astype(F32)
     head = run[states : states + 2 * lanes]
     total, last = run[:states], pairs(run, states + 2 * lanes, lanes)
     before = jnp.where(place == 1, total, jnp.zeros_like(total))
     for j in range(1, size):
-        total, last = step_over(block, lanes, rates, taps_ref, total, last, got_ref[j].astype(F32))
+        total, last = step_over(block, lanes, rates, taps_ref, total, last, got_ref[slot(j, size)].astype(F32))
         if j < size - 1:
             before = jnp.where(place == j + 1, total, before)
     before_ref[...] = before
     edge_ref[: 2 * lanes] = head
-    edge_ref[2 * lanes : 4 * lanes] = got_ref[jnp.maximum(place - 1, 0)].astype(F32)[states + 2 * lanes :]
-    edge_ref[4 * lanes :] = got_ref[place].astype(F32)[states : states + 2 * lanes]
+    edge_ref[2 * lanes : 4 * lanes] = got_ref[slot(jnp.maximum(place - 1, 0), size)].astype(F32)[states + 2 * lanes :]
+    edge_ref[4 * lanes :] = got_ref[slot(place, size)].astype(F32)[states : states + 2 * lanes]
     return jnp.concatenate([total, head, *last], axis=0)
 
 
@@ -245,9 +251,11 @@
         write(near_scan(block, lanes, got_ref, rate_ref, taps_ref, before_ref, edge_ref), message_ref)
 
 
-def merge(block, lanes, across_ref, cross_ref, next_ref, rate_ref, taps_ref, ahead_ref):
-    run = lax.axis_index("ctx") // NEAR
+def prepare(block, lanes, across_ref, cross_ref, next_ref, before_ref, edge_ref, rate_ref, taps_ref, residue_ref, rates_ref, weights_ref, rest_ref, decay_ref, head_ref, lead_ref, step_ref, fixed_ref):
+    index = lax.axis_index("ctx")
+    run, place = index // NEAR, index % NEAR
     states = rate_ref.shape[0]
+    modes = states // lanes
     rates = rate_ref[...]
     across, cross, following = [r[: states + 4 * lanes].astype(F32) for r in (across_ref, cross_ref, next_ref)]
     start = jnp.where(run == 5, following, jnp.where(run == 6, across, cross))
@@ -255,7 +263,36 @@
     for needed, message in ((run > 5, jnp.where(run == 6, cross, across)), (run > 6, following)):
         after, after_last = step_over(block * NEAR, lanes, rates, taps_ref, state, last, message)
         state, last = jnp.where(needed, after, state), [jnp.where(needed, a, b) for a, b in zip(after_last, last)]
-    ahead_ref[...] = jnp.concatenate([state, start[states : states + 2 * lanes], *last], axis=0)
+    into, own_last = step_into(block, lanes, place, rates, taps_ref, state, last, edge_ref, before_ref)
+    state = jnp.where(run > 4, into, before_ref[...])
+    length = (block * (NEAR * (run - 4) + place)).astype(F32)
+    away = length > 0
+    own_head = pairs(edge_ref, 4 * lanes, lanes)
+    first, second = first_products(taps_ref, own_last, own_head)
+    ahead = jnp.exp(rates) * spread(second, modes)
+    rest_ref[...] = state * jnp.exp(-rates) + jnp.where(away, spread(first, modes) + ahead, 0.0)
+    for i in range(3):
+        decay_ref[pl.ds(i * states, states)] = jnp.exp(-rates * (length + (1.0 - i)))
+    head_ref[...] = jnp.where(run > 4, start[states : states + 2 * lanes], edge_ref[: 2 * lanes])
+    ahead = jnp.where(away, ahead * residue_ref[...], 0.0)
+    query = [q.astype(BF16).astype(F32) for q in first_rows(taps_ref, 0, own_last, own_head)]
+    fix_rows(lanes, ahead, query, fixed_ref, 0)
+    row = lax.broadcasted_iota(jnp.int32, (SUB, weights_ref.shape[1]), 0).astype(F32)
+    step_ref[...] = jnp.exp(-SUB * rates_ref[...])
+    for mode in range(modes):
+        at = pl.ds(mode, 1)
+        lead_ref[pl.ds(mode * SUB, SUB)] = weights_ref[at] * jnp.exp(-rates_ref[at] * row)
+
+
+def fix_rows(lanes, ahead, query, out_ref, start):
+    modes = ahead.shape[0] // lanes
+    row = lax.broadcasted_iota(jnp.int32, (SUB, LANES), 0)
+    for l in range(lanes):
+        extra = jnp.sum(ahead[l * modes : (l + 1) * modes], axis=0, keepdims=True)
+        take = jnp.where(row == 0, jnp.broadcast_to(extra, row.shape), 0.0)
+        fixed = jnp.where(row == 0, query[0][l : l + 1], jnp.where(row == 1, query[1][l : l + 1], 0.0))
+        out_ref[start : start + SUB, pl.ds(l * LANES, LANES)] = take
+        out_ref[start + SUB : start + 2 * SUB, pl.ds(l * LANES, LANES)] = fixed
 
 
 def add_mode(totals, term, rate):
@@ -317,16 +354,10 @@
     state = state * jnp.exp(-rates) + spread(first, modes) + ahead
     state = state * residue_pack[...]
     ahead = ahead * residue_pack[...]
-    extra = [jnp.sum(ahead[l * modes : (l + 1) * modes], axis=0, keepdims=True) for l in range(lanes)]
-    row = lax.broadcasted_iota(jnp.int32, (SUB, LANES), 0)
-    lead = row.astype(F32)
+    fix_rows(lanes, ahead, own_query, state_ref, modes)
+    lead = lax.broadcasted_iota(jnp.int32, (SUB, LANES), 0).astype(F32)
     for l in range(lanes):
         state_ref[:modes, pl.ds(l * LANES, LANES)] = state[l * modes : (l + 1) * modes]
-        take = jnp.where(row == 0, jnp.broadcast_to(extra[l], row.shape), 0.0)
-        query = jnp.where(row == 0, own_query[0][l : l + 1], jnp.where(row == 1, own_query[1][l : l + 1], 0.0))
-        state_ref[modes : modes + SUB, pl.ds(l * LANES, LANES)] = take
-        state_ref[modes + SUB :, pl.ds(l * LANES, LANES)] = query
-    rows = lax.broadcasted_iota(jnp.int32, (2 * SUB, LANES), 0)
 
     def one_lane(lane, carry):
         at = pl.ds(pl.multiple_of(lane * LANES, LANES), LANES)
@@ -335,18 +366,23 @@
             rate = rate_ref[pl.ds(mode, 1), at]
             term = state_ref[pl.ds(mode, 1), at] * jnp.exp(-rate * lead)
             totals = add_mode(totals, term, rate)
-        totals[0] = totals[0] - state_ref[pl.ds(modes, SUB), at]
-        for i in range(0, blocks, 2):
-            where = pl.ds(i * SUB, 2 * SUB)
-            conv = jnp.concatenate(totals[i : i + 2], axis=0).astype(BF16).astype(F32)
-            query = query_ref[where, at].astype(F32)
-            if i == 0:
-                fixed = state_ref[pl.ds(modes + SUB, SUB), at]
-                query = jnp.where(rows < 2, jnp.concatenate([fixed, fixed], axis=0), query)
-            mixed_ref[where, at] = (query * conv).astype(BF16)
+        gate(totals, at, state_ref, modes, query_ref, mixed_ref)
         return carry
 
     lax.fori_loop(0, lanes, one_lane, 0)
+
+
+def gate(totals, at, fixed_ref, start, query_ref, mixed_ref):
+    totals[0] = totals[0] - fixed_ref[pl.ds(start, SUB), at]
+    rows = lax.broadcasted_iota(jnp.int32, (2 * SUB, LANES), 0)
+    for i in range(0, len(totals), 2):
+        where = pl.ds(i * SUB, 2 * SUB)
+        conv = jnp.concatenate(totals[i : i + 2], axis=0).astype(BF16).astype(F32)
+        query = query_ref[where, at].astype(F32)
+        if i == 0:
+            fixed = fixed_ref[pl.ds(start + SUB, SUB), at]
+            query = jnp.where(rows < 2, jnp.concatenate([fixed, fixed], axis=0), query)
+        mixed_ref[where, at] = (query * conv).astype(BF16)
 
 
 def leave(mixed_ref, out_ref, sem):
@@ -389,22 +425,49 @@
     leave(mixed_ref, out_ref, sem)
 
 
-def upper_output(before_ref, edge_ref, rate_pack, residue_pack, taps_ref, rate_ref, query_ref, local_ref, third_ref, fourth_ref, ahead_ref, held_ref, out_ref, state_ref, mixed_ref, sem):
+def upper_output(rest_ref, decay_ref, head_ref, lead_ref, step_ref, fixed_ref, residue_ref, rate_ref, taps_ref, query_ref, local_ref, third_ref, fourth_ref, held_ref, out_ref, state_ref, mixed_ref, sem):
     index = lax.axis_index("ctx")
-    run = index // NEAR
-    states = rate_pack.shape[0]
+    states = rest_ref.shape[0]
     lanes = taps_ref.shape[0] // 9
+    modes = states // lanes
+    blocks = local_ref.shape[0] // SUB
 
     @pl.when(index >= 2 * WIDE)
     def _():
         came = third_ref[...].astype(F32) + fourth_ref[: states + 4 * lanes].astype(F32)
-        state, last = came[:states], (came[states : states + lanes], came[states + lanes : states + 2 * lanes])
-        length = (NEAR * jnp.maximum(run - 4, 1) * local_ref.shape[0]).astype(F32)
-        after, after_last = step_over(length, lanes, rate_pack[...], taps_ref, state, last, ahead_ref[...])
-        needed = run > 4
-        state, last = jnp.where(needed, after, state), [jnp.where(needed, a, b) for a, b in zip(after_last, last)]
-        finish(index % NEAR, state, last, edge_ref, before_ref, rate_pack, residue_pack, taps_ref, rate_ref, query_ref, local_ref, mixed_ref, state_ref)
-        leave(mixed_ref, out_ref, sem)
+        last = pairs(came, states, lanes)
+        head = pairs(head_ref, 0, lanes)
+        first, second = first_products(taps_ref, last, head)
+        ahead = spread(second, modes)
+        state = rest_ref[...] + came[:states] * decay_ref[:states]
+        state = state + spread(first, modes) * decay_ref[states : 2 * states] + ahead * decay_ref[2 * states :]
+        for l in range(lanes):
+            state_ref[:modes, pl.ds(l * LANES, LANES)] = state[l * modes : (l + 1) * modes]
+        state_ref[modes:] = fixed_ref[...]
+
+        @pl.when(index == 2 * WIDE)
+        def _():
+            query = [q.astype(BF16).astype(F32) for q in first_rows(taps_ref, 0, last, head)]
+            fix_rows(lanes, jnp.exp(rate_ref[...]) * ahead * residue_ref[...], query, state_ref, modes)
+
+        def one_lane(lane, carry):
+            at = pl.ds(pl.multiple_of(lane * LANES, LANES), LANES)
+            totals = [local_ref[pl.ds(i * SUB, SUB), at] for i in range(blocks)]
+            for mode in range(modes):
+                step = jnp.broadcast_to(step_ref[pl.ds(mode, 1), at], (SUB, LANES))
+                term = state_ref[pl.ds(mode, 1), at] * lead_ref[pl.ds(mode * SUB, SUB), at]
+                for i in range(blocks):
+                    totals[i] = totals[i] + term
+                    if i < blocks - 1:
+                        term = term * step
+            gate(totals, at, state_ref, modes, query_ref, mixed_ref)
+            pltpu.make_async_copy(mixed_ref.at[:, at], out_ref.at[:, at], sem.at[lane]).start()
+            return carry
+
+        lax.fori_loop(0, lanes, one_lane, 0, unroll=True)
+        for l in range(lanes):
+            at = pl.ds(l * LANES, LANES)
+            pltpu.make_async_copy(mixed_ref.at[:, at], out_ref.at[:, at], sem.at[l]).wait()
 
 
 def gather(copies, axis, groups=None):
@@ -428,7 +491,7 @@
         [(h.shape, h.dtype) for h in held]
         + [((peers, 1, count), F32), ((9 * lanes, LANES), F32), ((states, LANES), F32), ((states, LANES), F32)],
         *held,
-        scratch=[pltpu.SemaphoreType.DMA((len(held),))],
+        scratch=[pltpu.SemaphoreType.DMA((lanes + len(held) - 1,))],
         space=pltpu.HBM,
     )
     sums = lax.cond(index < ctx, lambda c: gather(c, "ch"), lambda c: c, sums)
@@ -450,6 +513,9 @@
     )
 
     def gather_in(number, copies, members):
+        size = len(members[0])
+        order = sorted(range(size), key=lambda j: slot(j, size))
+        members = [[g[j] for j in order] for g in members]
         return lax.cond(
             group == number, lambda c: gather(c, "ctx", members), lambda c: nothing((c.shape, c.dtype))[0], copies
         )
@@ -480,30 +546,37 @@
     to_fourth = lax.ppermute(to_fourth, "ctx", hops((second, fourth[half:] + fourth[:half])))
     to_third = lax.ppermute(to_third, "ctx", hops((second, third)))
 
+    prepared = [
+        ((states, LANES), F32), ((3 * states, LANES), F32), ((2 * lanes, LANES), F32),
+        ((modes * SUB, chans), F32), ((modes, chans), F32), ((2 * SUB, chans), F32),
+    ]
+
     def upper(copies):
         *own, message, first_message = scan(third_scan, [small, large], gather_in(2, copies, runs))
         across = lax.ppermute(first_message, "ctx", hops((runs[4], runs[6]), (runs[5], runs[7])))
         cross = lax.ppermute(first_message, "ctx", hops((runs[4], runs[7]), (runs[5], runs[6])))
         *own, message = scan(fourth_scan, [small], gather_in(3, copies, runs), *own, message)
         following = lax.ppermute(message, "ctx", hops((runs[4], runs[5]), (runs[6], runs[7])))
-        (ahead,) = call(
-            lambda *refs: merge(count, lanes, *refs), [whole], across, cross, following, rate_pack, taps_pack
+        ready = call(
+            lambda *refs: prepare(count, lanes, *refs),
+            prepared,
+            across, cross, following, *own, rate_pack, taps_pack, residue_pack, rates, weights,
         )
-        return *call(lambda *refs: None, [result], out_hbm=(0,)), *own, inner(), ahead
+        return *call(lambda *refs: None, [result], out_hbm=(0,)), inner(), *ready
 
     def rest(copies):
         common = [rate_pack, residue_pack, taps_pack, rates, query, weights, product]
         (mixed,) = call(
             lower_output, [result], *lower_kept[:4], *common, *lower_kept[4:], scratch=room + [pltpu.VMEM(*held)] + work, out_hbm=(0,)
         )
-        return mixed, *nothing(*kept, held, whole)
-
-    mixed, *own, local, ahead = lax.cond(group >= 2, upper, rest, near)
+        return mixed, *nothing(held, *prepared)
+
+    mixed, local, *ready = lax.cond(group >= 2, upper, rest, near)
     (mixed,) = call(
         upper_output,
         [result],
-        *own, rate_pack, residue_pack, taps_pack, rates, query, local, to_third, to_fourth, ahead, mixed,
-        scratch=work, in_hbm=(11,), out_hbm=(0,), aliases={11: 0},
+        *ready, residue_pack, rate_pack, taps_pack, query, local, to_third, to_fourth, mixed,
+        scratch=work[:2] + [pltpu.SemaphoreType.DMA((lanes,))], in_hbm=(13,), out_hbm=(0,), aliases={13: 0},
     )
     return mixed
 

time: 39.1 us -> 37.7 us (0.964)
  the two profiles are of different devices: /device:TPU:448 before, /device:TPU:384 now
where the time goes in v11:
time: 37.7 us; the launch traced here: 37.4 us
  blocking collectives  19.8 us (53%)
  starting transfers between devices  7.92 us (21%)
  Pallas kernels  4.8 us (13%)
  waiting for transfers between devices  4.67 us (12%)
    all_to_all x2, blocking collectives, gather(): lax.all_to_all(copies, axis, 0, 0, tiled=True, axis_index_groups=groups)  19.8 us
    pallas_call x10, Pallas kernels, call(): pl.pallas_call(body, out_shape=shapes, in_specs=[pl.BlockSpec(memory_spac...  4.8 us
    ppermute x1, waiting for transfers between devices, per_device(): lax.ppermute(to_fourth, 'ctx', hops((second, fourth[half:] + fourth[:half...  4.2 us
    ppermute x1, starting transfers between devices, upper(): lax.ppermute(message, 'ctx', hops((runs[4], runs[5]), (runs[6], runs[7])))  3.38 us
    ppermute x1, starting transfers between devices, per_device(): lax.ppermute(to_fourth, 'ctx', hops((second, fourth[half:] + fourth[:half...  1.29 us
    ppermute x1, starting transfers between devices, upper(): lax.ppermute(first_message, 'ctx', hops((runs[4], runs[7]), (runs[5], run...  1.29 us
    ppermute x1, starting transfers between devices, upper(): lax.ppermute(first_message, 'ctx', hops((runs[4], runs[6]), (runs[5], run...  1.29 us
  transfers between devices with their start and end apart: 5, of which 2 were waited for; matrix products, arithmetic and copies ran while one was open for 0% of the time, Pallas kernels for 5%

profile of v11, /device:TPU:384, one launch (start us, length us, event | category | flops | bytes accessed | tf_op | source)
XLA Modules:
  0.0 37.4 jit_solution(12848496885472633591)
XLA Ops:
  0.0 1.0 %shard_map.55 = (bf16[128,512]{1,0:T(8,128)(2,1)S(1)}, f32[1,512]{1,0:T(1,128)S(1)}, f32[3,3,512]{2,1,0:T(4,128)S(1)}, f32[16,512]{1,0:T(8,128)S(1)}, f32[16,512...) custom-call(bf16[128,512]{1,0:T(8,128)(2,1)} %refs_0_, ...), custom_call_target="tpu_custom_call" | custom-call | bytes 217088 | tf_op jit(solution)/shard_map/pallas_call | solution.py:24
  1.0 9.6 %conditional.7 = (f32[8,1,128]{2,1,0:T(1,128)S(1)}) conditional(s32[]{:T(128)} %convert_element_type.21, f32[8,1,128]{2,1,0:T(1,128)S(1)} %get-tuple-element.177, f32[8,1,128]{2,1,0:T(1,128)S(1)} %get-tuple-element.177), branch_computations={%region_0.0_spmd, %region_1.0_spmd} | conditional | bytes 16392 | solution.py:497
  1.0 9.5 %all_to_all.20 = f32[8,1,128]{2,1,0:T(1,128)S(1)} all-to-all(f32[8,1,128]{2,1,0:T(1,128)S(1)} %copy.50), channel_id=1, replica_groups=mesh['ctx'=64,'ch'=8] {'ch'}, dimensions={0} | all-to-all | bytes 8192 | tf_op jit(solution)/shard_map/cond/branch_1_fun/all_to_all | solution.py:474
  10.6 0.8 %shard_map.56 = (bf16[128,512]{1,0:T(8,128)(2,1)S(1)}, f32[128,512]{1,0:T(8,128)S(1)}, bf16[16,80,128]{2,1,0:T(8,128)(2,1)S(1)}, bf16[8,80,128]{2,1,0:T(8,128)(2,1)S(1)}) custom-call(f32[8,1,128]{2,1,0:T(1,128)S(1)} %get-tuple-element.245.refs_0_, bf16[128,512]{1,0:T(8,128)(2,1)S(1)} %get-tuple-element.178.refs_1_, f32[1,512]{1,0:T(1,128)S(1)} %get-tuple-element.179.refs_2_, ...), custom_call_target="tpu_custom_call" | custom-call | bytes 188416 | tf_op jit(solution)/shard_map/pallas_call | solution.py:24
  11.5 1.3 %collective-permute-start.5 = (bf16[96,128]{1,0:T(8,128)(2,1)S(1)}, bf16[96,128]{1,0:T(8,128)(2,1)S(1)}, u32[]{:S(2)}, u32[]{:S(2)}) collective-permute-start(bf16[96,128]{1,0:T(8,128)(2,1)S(1)} %get-tuple-element.207), channel_id=1, source_target_pairs={{128,448},{136,456},{144,464},{152,472},{160,480},{168,488},{176,4... | collective-permute-start | bytes 73736 | tf_op jit(solution)/shard_map/ppermute | solution.py:546
  12.8 0.7 %collective-permute-start.4 = (bf16[80,128]{1,0:T(8,128)(2,1)S(1)}, bf16[80,128]{1,0:T(8,128)(2,1)S(1)}, u32[]{:S(2)}, u32[]{:S(2)}) collective-permute-start(bf16[80,128]{1,0:T(8,128)(2,1)S(1)} %get-tuple-element.206), channel_id=1, source_target_pairs={{128,256},{136,264},{144,272},{152,280},{160,288},{168,296},{176,3... | collective-permute-start | bytes 61448 | tf_op jit(solution)/shard_map/ppermute | solution.py:547
  13.4 18.7 %conditional.9 = (bf16[128,512]{1,0:T(8,128)(2,1)S(1)}, f32[128,512]{1,0:T(8,128)S(1)}, f32[64,128]{1,0:T(8,128)S(1)}, f32[192,128]{1,0:T(8,128)S(1)}, f32[8,128...) conditional(s32[]{:T(128)} %convert_element_type.22, ...), branch_computations={%region_8.0_spmd, %region_9.0_spmd} | conditional | flops 10000004 | bytes 2021604 | solution.py:574
  13.5 1.3 %collective-permute-start.2 = (bf16[96,128]{1,0:T(8,128)(2,1)S(1)}, bf16[96,128]{1,0:T(8,128)(2,1)S(1)}, u32[]{:S(2)}, u32[]{:S(2)}) collective-permute-start(bf16[96,128]{1,0:T(8,128)(2,1)S(1)} %get-tuple-element.127), channel_id=1, source_target_pairs={{256,448},{264,456},{272,464},{280,472},{288,480},{296,488},{304,4... | collective-permute-start | bytes 73736 | tf_op jit(solution)/shard_map/cond/branch_1_fun/ppermute | solution.py:557
  14.8 1.3 %collective-permute-start.1 = (bf16[96,128]{1,0:T(8,128)(2,1)S(1)}, bf16[96,128]{1,0:T(8,128)(2,1)S(1)}, u32[]{:S(2)}, u32[]{:S(2)}) collective-permute-start(bf16[96,128]{1,0:T(8,128)(2,1)S(1)} %get-tuple-element.127), channel_id=1, source_target_pairs={{256,384},{264,392},{272,400},{280,408},{288,416},{296,424},{304,4... | collective-permute-start | bytes 73736 | tf_op jit(solution)/shard_map/cond/branch_1_fun/ppermute | solution.py:556
  16.1 10.2 %conditional.3 = (bf16[8,80,128]{2,1,0:T(8,128)(2,1)S(1)}) conditional(s32[]{:T(128)} %convert_element_type.17, () %tuple.45, bf16[8,80,128]{2,1,0:T(8,128)(2,1)S(1)} %get-tuple-element.124), branch_computations={%region_12.0_spmd, %region_13.0_spmd} | conditional | bytes 327688 | solution.py:519
  16.1 10.2 %all_to_all.24 = bf16[8,80,128]{2,1,0:T(8,128)(2,1)S(1)} all-to-all(bf16[8,80,128]{2,1,0:T(8,128)(2,1)S(1)} %param.12), channel_id=1, replica_groups={{56,48,40,32,24,16,8,0},{120,112,104,96,88,80,72,64},{184,176,168,160,1..., dimensions={0} | all-to-all | bytes 327680 | tf_op jit(solution)/shard_map/cond/branch_1_fun/cond/branch_1_fun/all_to_all | solution.py:474
  26.4 0.1 branch_1_fun.16
  26.5 3.4 %collective-permute-start.3 = (bf16[80,128]{1,0:T(8,128)(2,1)S(1)}, bf16[80,128]{1,0:T(8,128)(2,1)S(1)}, u32[]{:S(2)}, u32[]{:S(2)}) collective-permute-start(bf16[80,128]{1,0:T(8,128)(2,1)S(1)} %get-tuple-element.131), channel_id=1, source_target_pairs={{256,320},{264,328},{272,336},{280,344},{288,352},{296,360},{304,3... | collective-permute-start | bytes 61448 | tf_op jit(solution)/shard_map/cond/branch_1_fun/ppermute | solution.py:559
  29.9 1.6 %branch_1_fun.14 = f32[128,512]{1,0:T(8,128)S(1)} custom-call(f32[16,512]{1,0:T(8,128)S(1)} %get-tuple-element.120.rate_ref.refs_8_, f32[16,512]{1,0:T(8,128)S(1)} %get-tuple-element.121.residue_ref.refs_9_, f32[128,512]{1,0:T(8,128)S(1)} %get-tuple-element.122.product_ref), custom_call_target="tpu_custom_call" | custom-call | flops 10000000 | bytes 327680 | tf_op jit(solution)/shard_map/cond/branch_1_fun/pallas_call | solution.py:24
  31.5 0.0 collective-permute-done.3.refs_2_
  31.5 0.0 collective-permute-done.2.refs_1_
  31.5 0.5 %collective-permute-done.1.refs_0_ = bf16[96,128]{1,0:T(8,128)(2,1)S(1)} collective-permute-done((bf16[96,128]{1,0:T(8,128)(2,1)S(1)}, bf16[96,128]{1,0:T(8,128)(2,1)S(1)}, u32[]{:S(2)}, u32[]{:S(2)}) %collective-permute-start.1) | collective-permute-done | bytes 24608 | tf_op jit(solution)/shard_map/cond/branch_1_fun/ppermute | solution.py:556
  32.0 0.2 branch_1_fun.17
  32.2 0.0 copy-start
  32.2 0.0 collective-permute-done.4.third_ref
  32.2 4.2 %collective-permute-done.5.fourth_ref = bf16[96,128]{1,0:T(8,128)(2,1)S(1)} collective-permute-done((bf16[96,128]{1,0:T(8,128)(2,1)S(1)}, bf16[96,128]{1,0:T(8,128)(2,1)S(1)}, u32[]{:S(2)}, u32[]{:S(2)}) %collective-permute-start.5) | collective-permute-done | bytes 24608 | tf_op jit(solution)/shard_map/ppermute | solution.py:546
  36.4 0.0 copy-done
  36.4 1.0 %shard_map.57 = bf16[128,512]{1,0:T(8,128)(2,1)} custom-call(f32[64,128]{1,0:T(8,128)S(1)} %get-tuple-element.199.rest_ref, f32[192,128]{1,0:T(8,128)S(1)} %get-tuple-element.200.decay_ref, f32[8,128]{1,0:T(8,128)S(1)} %get-tuple-element.201.head_ref, f32[128,512]{1,0:T(8,128)S(1)} %get-tuple-element.202.lead_ref, ...), custom_call_target="tpu_custom_call", output_to_operand_aliasing={{}: (13, {})} | custom-call | bytes 1116160 | tf_op jit(solution)/shard_map/pallas_call | solution.py:24
  (7 shorter events, 0.1 us)
Async XLA Ops:
  11.5 24.9 %collective-permute-start.5 = (bf16[96,128]{1,0:T(8,128)(2,1)S(1)}, bf16[96,128]{1,0:T(8,128)(2,1)S(1)}, u32[]{:S(2)}, u32[]{:S(2)}) collective-permute-start(bf16[96,128]{1,0:T(8,128)(2,1)S(1)} %get-tuple-element.207), channel_id=1, source_target_pairs={{128,448},{136,456},{144,464},{152,472},{160,480},{168,488},{176,4... | collective-permute-start | bytes 73736 | tf_op jit(solution)/shard_map/ppermute | solution.py:546
  12.8 19.4 %collective-permute-start.4 = (bf16[80,128]{1,0:T(8,128)(2,1)S(1)}, bf16[80,128]{1,0:T(8,128)(2,1)S(1)}, u32[]{:S(2)}, u32[]{:S(2)}) collective-permute-start(bf16[80,128]{1,0:T(8,128)(2,1)S(1)} %get-tuple-element.206), channel_id=1, source_target_pairs={{128,256},{136,264},{144,272},{152,280},{160,288},{168,296},{176,3... | collective-permute-start | bytes 61448 | tf_op jit(solution)/shard_map/ppermute | solution.py:547
  13.5 18.0 %collective-permute-start.2 = (bf16[96,128]{1,0:T(8,128)(2,1)S(1)}, bf16[96,128]{1,0:T(8,128)(2,1)S(1)}, u32[]{:S(2)}, u32[]{:S(2)}) collective-permute-start(bf16[96,128]{1,0:T(8,128)(2,1)S(1)} %get-tuple-element.127), channel_id=1, source_target_pairs={{256,448},{264,456},{272,464},{280,472},{288,480},{296,488},{304,4... | collective-permute-start | bytes 73736 | tf_op jit(solution)/shard_map/cond/branch_1_fun/ppermute | solution.py:557
  14.8 17.2 %collective-permute-start.1 = (bf16[96,128]{1,0:T(8,128)(2,1)S(1)}, bf16[96,128]{1,0:T(8,128)(2,1)S(1)}, u32[]{:S(2)}, u32[]{:S(2)}) collective-permute-start(bf16[96,128]{1,0:T(8,128)(2,1)S(1)} %get-tuple-element.127), channel_id=1, source_target_pairs={{256,384},{264,392},{272,400},{280,408},{288,416},{296,424},{304,4... | collective-permute-start | bytes 73736 | tf_op jit(solution)/shard_map/cond/branch_1_fun/ppermute | solution.py:556
  26.5 5.0 %collective-permute-start.3 = (bf16[80,128]{1,0:T(8,128)(2,1)S(1)}, bf16[80,128]{1,0:T(8,128)(2,1)S(1)}, u32[]{:S(2)}, u32[]{:S(2)}) collective-permute-start(bf16[80,128]{1,0:T(8,128)(2,1)S(1)} %get-tuple-element.131), channel_id=1, source_target_pairs={{256,320},{264,328},{272,336},{280,344},{288,352},{296,360},{304,3... | collective-permute-start | bytes 61448 | tf_op jit(solution)/shard_map/cond/branch_1_fun/ppermute | solution.py:559
  32.2 4.2 %copy-start = (bf16[128,512]{1,0:T(8,128)(2,1)}, bf16[128,512]{1,0:T(8,128)(2,1)S(1)}, u32[]{:S(2)}) copy-start(bf16[128,512]{1,0:T(8,128)(2,1)S(1)} %get-tuple-element.208.held_ref) | copy-start | bytes 393220

commit v12 on v11

--- a/solution.py
+++ b/solution.py
@@ -494,7 +494,7 @@
         scratch=[pltpu.SemaphoreType.DMA((lanes + len(held) - 1,))],
         space=pltpu.HBM,
     )
-    sums = lax.cond(index < ctx, lambda c: gather(c, "ch"), lambda c: c, sums)
+    sums = lax.cond(index < ctx, lambda c: gather(c, "ch", [list(range(peers))[::-1]]), lambda c: c, sums)
     query, product, wide, near = call(
         lambda *refs: block_states(chans * peers, *refs),
         [((count, chans), BF16), ((count, chans), F32), ((WIDE, states + 4 * lanes, LANES), BF16), ((NEAR, states + 4 * lanes, LANES), BF16)],

time: 37.7 us -> 37.3 us (0.989)
  the two profiles are of different devices: /device:TPU:384 before, /device:TPU:416 now
where the time goes in v12:
time: 37.3 us; the launch traced here: 37 us
  blocking collectives  18.5 us (50%)
  starting transfers between devices  7.92 us (21%)
  waiting for transfers between devices  5.53 us (15%)
  Pallas kernels  4.8 us (13%)
    all_to_all x2, blocking collectives, gather(): lax.all_to_all(copies, axis, 0, 0, tiled=True, axis_index_groups=groups)  18.5 us
    ppermute x1, waiting for transfers between devices, per_device(): lax.ppermute(to_fourth, 'ctx', hops((second, fourth[half:] + fourth[:half...  5.3 us
    pallas_call x10, Pallas kernels, call(): pl.pallas_call(body, out_shape=shapes, in_specs=[pl.BlockSpec(memory_spac...  4.8 us
    ppermute x1, starting transfers between devices, upper(): lax.ppermute(message, 'ctx', hops((runs[4], runs[5]), (runs[6], runs[7])))  3.38 us
    ppermute x1, starting transfers between devices, per_device(): lax.ppermute(to_fourth, 'ctx', hops((second, fourth[half:] + fourth[:half...  1.29 us
    ppermute x1, starting transfers between devices, upper(): lax.ppermute(first_message, 'ctx', hops((runs[4], runs[7]), (runs[5], run...  1.29 us
    ppermute x1, starting transfers between devices, upper(): lax.ppermute(first_message, 'ctx', hops((runs[4], runs[6]), (runs[5], run...  1.29 us
  transfers between devices with their start and end apart: 5, of which 2 were waited for; matrix products, arithmetic and copies ran while one was open for 0% of the time, Pallas kernels for 5%

profile of v12, /device:TPU:416, one launch (start us, length us, event | category | flops | bytes accessed | tf_op | source)
XLA Modules:
  0.0 37.0 jit_solution(6379095451363309701)
XLA Ops:
  0.0 1.0 %shard_map.55 = (bf16[128,512]{1,0:T(8,128)(2,1)S(1)}, f32[1,512]{1,0:T(1,128)S(1)}, f32[3,3,512]{2,1,0:T(4,128)S(1)}, f32[16,512]{1,0:T(8,128)S(1)}, f32[16,512...) custom-call(bf16[128,512]{1,0:T(8,128)(2,1)} %refs_0_, ...), custom_call_target="tpu_custom_call" | custom-call | bytes 217088 | tf_op jit(solution)/shard_map/pallas_call | solution.py:24
  1.0 8.3 %conditional.7 = (f32[8,1,128]{2,1,0:T(1,128)S(1)}) conditional(s32[]{:T(128)} %convert_element_type.21, f32[8,1,128]{2,1,0:T(1,128)S(1)} %get-tuple-element.177, f32[8,1,128]{2,1,0:T(1,128)S(1)} %get-tuple-element.177), branch_computations={%region_0.0_spmd, %region_1.0_spmd} | conditional | bytes 16392 | solution.py:497
  1.0 8.3 %all_to_all.20 = f32[8,1,128]{2,1,0:T(1,128)S(1)} all-to-all(f32[8,1,128]{2,1,0:T(1,128)S(1)} %copy.50), channel_id=1, replica_groups={{7,6,5,4,3,2,1,0},{15,14,13,12,11,10,9,8},{23,22,21,20,19,18,17,16},{31..., dimensions={0} | all-to-all | bytes 8192 | tf_op jit(solution)/shard_map/cond/branch_1_fun/all_to_all | solution.py:474
  9.3 0.8 %shard_map.56 = (bf16[128,512]{1,0:T(8,128)(2,1)S(1)}, f32[128,512]{1,0:T(8,128)S(1)}, bf16[16,80,128]{2,1,0:T(8,128)(2,1)S(1)}, bf16[8,80,128]{2,1,0:T(8,128)(2,1)S(1)}) custom-call(f32[8,1,128]{2,1,0:T(1,128)S(1)} %get-tuple-element.245.refs_0_, bf16[128,512]{1,0:T(8,128)(2,1)S(1)} %get-tuple-element.178.refs_1_, f32[1,512]{1,0:T(1,128)S(1)} %get-tuple-element.179.refs_2_, ...), custom_call_target="tpu_custom_call" | custom-call | bytes 188416 | tf_op jit(solution)/shard_map/pallas_call | solution.py:24
  10.2 1.3 %collective-permute-start.5 = (bf16[96,128]{1,0:T(8,128)(2,1)S(1)}, bf16[96,128]{1,0:T(8,128)(2,1)S(1)}, u32[]{:S(2)}, u32[]{:S(2)}) collective-permute-start(bf16[96,128]{1,0:T(8,128)(2,1)S(1)} %get-tuple-element.207), channel_id=1, source_target_pairs={{128,448},{136,456},{144,464},{152,472},{160,480},{168,488},{176,4... | collective-permute-start | bytes 73736 | tf_op jit(solution)/shard_map/ppermute | solution.py:546
  11.5 0.7 %collective-permute-start.4 = (bf16[80,128]{1,0:T(8,128)(2,1)S(1)}, bf16[80,128]{1,0:T(8,128)(2,1)S(1)}, u32[]{:S(2)}, u32[]{:S(2)}) collective-permute-start(bf16[80,128]{1,0:T(8,128)(2,1)S(1)} %get-tuple-element.206), channel_id=1, source_target_pairs={{128,256},{136,264},{144,272},{152,280},{160,288},{168,296},{176,3... | collective-permute-start | bytes 61448 | tf_op jit(solution)/shard_map/ppermute | solution.py:547
  12.2 18.5 %conditional.9 = (bf16[128,512]{1,0:T(8,128)(2,1)S(1)}, f32[128,512]{1,0:T(8,128)S(1)}, f32[64,128]{1,0:T(8,128)S(1)}, f32[192,128]{1,0:T(8,128)S(1)}, f32[8,128...) conditional(s32[]{:T(128)} %convert_element_type.22, ...), branch_computations={%region_8.0_spmd, %region_9.0_spmd} | conditional | flops 10000004 | bytes 2021604 | solution.py:574
  12.3 1.3 %collective-permute-start.2 = (bf16[96,128]{1,0:T(8,128)(2,1)S(1)}, bf16[96,128]{1,0:T(8,128)(2,1)S(1)}, u32[]{:S(2)}, u32[]{:S(2)}) collective-permute-start(bf16[96,128]{1,0:T(8,128)(2,1)S(1)} %get-tuple-element.127), channel_id=1, source_target_pairs={{256,448},{264,456},{272,464},{280,472},{288,480},{296,488},{304,4... | collective-permute-start | bytes 73736 | tf_op jit(solution)/shard_map/cond/branch_1_fun/ppermute | solution.py:557
  13.6 1.3 %collective-permute-start.1 = (bf16[96,128]{1,0:T(8,128)(2,1)S(1)}, bf16[96,128]{1,0:T(8,128)(2,1)S(1)}, u32[]{:S(2)}, u32[]{:S(2)}) collective-permute-start(bf16[96,128]{1,0:T(8,128)(2,1)S(1)} %get-tuple-element.127), channel_id=1, source_target_pairs={{256,384},{264,392},{272,400},{280,408},{288,416},{296,424},{304,4... | collective-permute-start | bytes 73736 | tf_op jit(solution)/shard_map/cond/branch_1_fun/ppermute | solution.py:556
  14.9 10.2 %conditional.3 = (bf16[8,80,128]{2,1,0:T(8,128)(2,1)S(1)}) conditional(s32[]{:T(128)} %convert_element_type.17, () %tuple.45, bf16[8,80,128]{2,1,0:T(8,128)(2,1)S(1)} %get-tuple-element.124), branch_computations={%region_12.0_spmd, %region_13.0_spmd} | conditional | bytes 327688 | solution.py:519
  14.9 10.2 %all_to_all.24 = bf16[8,80,128]{2,1,0:T(8,128)(2,1)S(1)} all-to-all(bf16[8,80,128]{2,1,0:T(8,128)(2,1)S(1)} %param.12), channel_id=1, replica_groups={{56,48,40,32,24,16,8,0},{120,112,104,96,88,80,72,64},{184,176,168,160,1..., dimensions={0} | all-to-all | bytes 327680 | tf_op jit(solution)/shard_map/cond/branch_1_fun/cond/branch_1_fun/all_to_all | solution.py:474
  25.1 0.1 branch_1_fun.16
  25.2 3.4 %collective-permute-start.3 = (bf16[80,128]{1,0:T(8,128)(2,1)S(1)}, bf16[80,128]{1,0:T(8,128)(2,1)S(1)}, u32[]{:S(2)}, u32[]{:S(2)}) collective-permute-start(bf16[80,128]{1,0:T(8,128)(2,1)S(1)} %get-tuple-element.131), channel_id=1, source_target_pairs={{256,320},{264,328},{272,336},{280,344},{288,352},{296,360},{304,3... | collective-permute-start | bytes 61448 | tf_op jit(solution)/shard_map/cond/branch_1_fun/ppermute | solution.py:559
  28.6 1.6 %branch_1_fun.14 = f32[128,512]{1,0:T(8,128)S(1)} custom-call(f32[16,512]{1,0:T(8,128)S(1)} %get-tuple-element.120.rate_ref.refs_8_, f32[16,512]{1,0:T(8,128)S(1)} %get-tuple-element.121.residue_ref.refs_9_, f32[128,512]{1,0:T(8,128)S(1)} %get-tuple-element.122.product_ref), custom_call_target="tpu_custom_call" | custom-call | flops 10000000 | bytes 327680 | tf_op jit(solution)/shard_map/cond/branch_1_fun/pallas_call | solution.py:24
  30.2 0.0 collective-permute-done.3.refs_2_
  30.3 0.0 collective-permute-done.2.refs_1_
  30.3 0.2 collective-permute-done.1.refs_0_
  30.5 0.2 branch_1_fun.17
  30.7 0.0 copy-start
  30.7 0.0 collective-permute-done.4.third_ref
  30.7 5.3 %collective-permute-done.5.fourth_ref = bf16[96,128]{1,0:T(8,128)(2,1)S(1)} collective-permute-done((bf16[96,128]{1,0:T(8,128)(2,1)S(1)}, bf16[96,128]{1,0:T(8,128)(2,1)S(1)}, u32[]{:S(2)}, u32[]{:S(2)}) %collective-permute-start.5) | collective-permute-done | bytes 24608 | tf_op jit(solution)/shard_map/ppermute | solution.py:546
  36.0 0.0 copy-done
  36.0 1.0 %shard_map.57 = bf16[128,512]{1,0:T(8,128)(2,1)} custom-call(f32[64,128]{1,0:T(8,128)S(1)} %get-tuple-element.199.rest_ref, f32[192,128]{1,0:T(8,128)S(1)} %get-tuple-element.200.decay_ref, f32[8,128]{1,0:T(8,128)S(1)} %get-tuple-element.201.head_ref, f32[128,512]{1,0:T(8,128)S(1)} %get-tuple-element.202.lead_ref, ...), custom_call_target="tpu_custom_call", output_to_operand_aliasing={{}: (13, {})} | custom-call | bytes 1116160 | tf_op jit(solution)/shard_map/pallas_call | solution.py:24
  (7 shorter events, 0.1 us)
Async XLA Ops:
  10.2 25.8 %collective-permute-start.5 = (bf16[96,128]{1,0:T(8,128)(2,1)S(1)}, bf16[96,128]{1,0:T(8,128)(2,1)S(1)}, u32[]{:S(2)}, u32[]{:S(2)}) collective-permute-start(bf16[96,128]{1,0:T(8,128)(2,1)S(1)} %get-tuple-element.207), channel_id=1, source_target_pairs={{128,448},{136,456},{144,464},{152,472},{160,480},{168,488},{176,4... | collective-permute-start | bytes 73736 | tf_op jit(solution)/shard_map/ppermute | solution.py:546
  11.5 19.2 %collective-permute-start.4 = (bf16[80,128]{1,0:T(8,128)(2,1)S(1)}, bf16[80,128]{1,0:T(8,128)(2,1)S(1)}, u32[]{:S(2)}, u32[]{:S(2)}) collective-permute-start(bf16[80,128]{1,0:T(8,128)(2,1)S(1)} %get-tuple-element.206), channel_id=1, source_target_pairs={{128,256},{136,264},{144,272},{152,280},{160,288},{168,296},{176,3... | collective-permute-start | bytes 61448 | tf_op jit(solution)/shard_map/ppermute | solution.py:547
  12.3 18.0 %collective-permute-start.2 = (bf16[96,128]{1,0:T(8,128)(2,1)S(1)}, bf16[96,128]{1,0:T(8,128)(2,1)S(1)}, u32[]{:S(2)}, u32[]{:S(2)}) collective-permute-start(bf16[96,128]{1,0:T(8,128)(2,1)S(1)} %get-tuple-element.127), channel_id=1, source_target_pairs={{256,448},{264,456},{272,464},{280,472},{288,480},{296,488},{304,4... | collective-permute-start | bytes 73736 | tf_op jit(solution)/shard_map/cond/branch_1_fun/ppermute | solution.py:557
  13.6 16.9 %collective-permute-start.1 = (bf16[96,128]{1,0:T(8,128)(2,1)S(1)}, bf16[96,128]{1,0:T(8,128)(2,1)S(1)}, u32[]{:S(2)}, u32[]{:S(2)}) collective-permute-start(bf16[96,128]{1,0:T(8,128)(2,1)S(1)} %get-tuple-element.127), channel_id=1, source_target_pairs={{256,384},{264,392},{272,400},{280,408},{288,416},{296,424},{304,4... | collective-permute-start | bytes 73736 | tf_op jit(solution)/shard_map/cond/branch_1_fun/ppermute | solution.py:556
  25.2 5.0 %collective-permute-start.3 = (bf16[80,128]{1,0:T(8,128)(2,1)S(1)}, bf16[80,128]{1,0:T(8,128)(2,1)S(1)}, u32[]{:S(2)}, u32[]{:S(2)}) collective-permute-start(bf16[80,128]{1,0:T(8,128)(2,1)S(1)} %get-tuple-element.131), channel_id=1, source_target_pairs={{256,320},{264,328},{272,336},{280,344},{288,352},{296,360},{304,3... | collective-permute-start | bytes 61448 | tf_op jit(solution)/shard_map/cond/branch_1_fun/ppermute | solution.py:559
  30.7 5.3 %copy-start = (bf16[128,512]{1,0:T(8,128)(2,1)}, bf16[128,512]{1,0:T(8,128)(2,1)S(1)}, u32[]{:S(2)}) copy-start(bf16[128,512]{1,0:T(8,128)(2,1)S(1)} %get-tuple-element.208.held_ref) | copy-start | bytes 393220

commit v13 on v12

--- a/solution.py
+++ b/solution.py
@@ -180,7 +180,11 @@
     return size - 1 - place
 
 
-def near_scan(block, lanes, got_ref, rate_ref, taps_ref, before_ref, edge_ref):
+def first_slot(place, size):
+    return (3 - place // 4) * 4 + place % 4
+
+
+def near_scan(block, lanes, got_ref, rate_ref, taps_ref, before_ref, edge_ref, slot=slot):
     size = got_ref.shape[0]
     place = lax.axis_index("ctx") % size
     states = rate_ref.shape[0]
@@ -210,7 +214,7 @@
 def first_scan(block, lanes, got_ref, rate_ref, taps_ref, before_ref, edge_ref, message_ref):
     @pl.when(lax.axis_index("ctx") // WIDE == 0)
     def _():
-        write(near_scan(block, lanes, got_ref, rate_ref, taps_ref, before_ref, edge_ref), message_ref)
+        write(near_scan(block, lanes, got_ref, rate_ref, taps_ref, before_ref, edge_ref, first_slot), message_ref)
 
 
 def second_scan(block, lanes, got_ref, rate_ref, taps_ref, before_ref, edge_ref, message_ref):
@@ -514,7 +518,8 @@
 
     def gather_in(number, copies, members):
         size = len(members[0])
-        order = sorted(range(size), key=lambda j: slot(j, size))
+        put = slot if number else first_slot
+        order = sorted(range(size), key=lambda j: put(j, size))
         members = [[g[j] for j in order] for g in members]
         return lax.cond(
             group == number, lambda c: gather(c, "ctx", members), lambda c: nothing((c.shape, c.dtype))[0], copies
@@ -543,7 +548,9 @@
         group < 2, lower, lambda c: nothing(*kept, *kept, held, whole, small, large), wide
     )
     half = WIDE // 2
-    to_fourth = lax.ppermute(to_fourth, "ctx", hops((second, fourth[half:] + fourth[:half])))
+    quarter = WIDE // 4
+    turned = fourth[half:] + fourth[quarter:half] + fourth[:quarter]
+    to_fourth = lax.ppermute(to_fourth, "ctx", hops((second, turned)))
     to_third = lax.ppermute(to_third, "ctx", hops((second, third)))
 
     prepared = [

time: 37.3 us -> 37 us (level)
  no operation moved by 1% of the time
where the time goes in v13:
time: 37 us; the launch traced here: 36.7 us
  blocking collectives  18.5 us (50%)
  starting transfers between devices  7.92 us (21%)
  waiting for transfers between devices  5.24 us (14%)
  Pallas kernels  4.8 us (13%)
    all_to_all x2, blocking collectives, gather(): lax.all_to_all(copies, axis, 0, 0, tiled=True, axis_index_groups=groups)  18.5 us
    ppermute x1, waiting for transfers between devices, per_device(): to_fourth = lax.ppermute(to_fourth, 'ctx', hops((second, turned)))  5.01 us
    pallas_call x10, Pallas kernels, call(): pl.pallas_call(body, out_shape=shapes, in_specs=[pl.BlockSpec(memory_spac...  4.8 us
    ppermute x1, starting transfers between devices, upper(): lax.ppermute(message, 'ctx', hops((runs[4], runs[5]), (runs[6], runs[7])))  3.38 us
    ppermute x1, starting transfers between devices, per_device(): to_fourth = lax.ppermute(to_fourth, 'ctx', hops((second, turned)))  1.29 us
    ppermute x1, starting transfers between devices, upper(): lax.ppermute(first_message, 'ctx', hops((runs[4], runs[7]), (runs[5], run...  1.29 us
    ppermute x1, starting transfers between devices, upper(): lax.ppermute(first_message, 'ctx', hops((runs[4], runs[6]), (runs[5], run...  1.29 us
  transfers between devices with their start and end apart: 5, of which 2 were waited for; matrix products, arithmetic and copies ran while one was open for 0% of the time, Pallas kernels for 5%

profile of v13, /device:TPU:416, one launch (start us, length us, event | category | flops | bytes accessed | tf_op | source)
XLA Modules:
  0.0 36.7 jit_solution(7467793105028104703)
XLA Ops:
  0.0 1.0 %shard_map.55 = (bf16[128,512]{1,0:T(8,128)(2,1)S(1)}, f32[1,512]{1,0:T(1,128)S(1)}, f32[3,3,512]{2,1,0:T(4,128)S(1)}, f32[16,512]{1,0:T(8,128)S(1)}, f32[16,512...) custom-call(bf16[128,512]{1,0:T(8,128)(2,1)} %refs_0_, ...), custom_call_target="tpu_custom_call" | custom-call | bytes 217088 | tf_op jit(solution)/shard_map/pallas_call | solution.py:24
  1.0 8.3 %conditional.7 = (f32[8,1,128]{2,1,0:T(1,128)S(1)}) conditional(s32[]{:T(128)} %convert_element_type.21, f32[8,1,128]{2,1,0:T(1,128)S(1)} %get-tuple-element.177, f32[8,1,128]{2,1,0:T(1,128)S(1)} %get-tuple-element.177), branch_computations={%region_0.0_spmd, %region_1.0_spmd} | conditional | bytes 16392 | solution.py:501
  1.0 8.3 %all_to_all.20 = f32[8,1,128]{2,1,0:T(1,128)S(1)} all-to-all(f32[8,1,128]{2,1,0:T(1,128)S(1)} %copy.50), channel_id=1, replica_groups={{7,6,5,4,3,2,1,0},{15,14,13,12,11,10,9,8},{23,22,21,20,19,18,17,16},{31..., dimensions={0} | all-to-all | bytes 8192 | tf_op jit(solution)/shard_map/cond/branch_1_fun/all_to_all | solution.py:478
  9.3 0.8 %shard_map.56 = (bf16[128,512]{1,0:T(8,128)(2,1)S(1)}, f32[128,512]{1,0:T(8,128)S(1)}, bf16[16,80,128]{2,1,0:T(8,128)(2,1)S(1)}, bf16[8,80,128]{2,1,0:T(8,128)(2,1)S(1)}) custom-call(f32[8,1,128]{2,1,0:T(1,128)S(1)} %get-tuple-element.245.refs_0_, bf16[128,512]{1,0:T(8,128)(2,1)S(1)} %get-tuple-element.178.refs_1_, f32[1,512]{1,0:T(1,128)S(1)} %get-tuple-element.179.refs_2_, ...), custom_call_target="tpu_custom_call" | custom-call | bytes 188416 | tf_op jit(solution)/shard_map/pallas_call | solution.py:24
  10.2 1.3 %collective-permute-start.5 = (bf16[96,128]{1,0:T(8,128)(2,1)S(1)}, bf16[96,128]{1,0:T(8,128)(2,1)S(1)}, u32[]{:S(2)}, u32[]{:S(2)}) collective-permute-start(bf16[96,128]{1,0:T(8,128)(2,1)S(1)} %get-tuple-element.207), channel_id=1, source_target_pairs={{128,448},{136,456},{144,464},{152,472},{160,480},{168,488},{176,4... | collective-permute-start | bytes 73736 | tf_op jit(solution)/shard_map/ppermute | solution.py:553
  11.5 0.7 %collective-permute-start.4 = (bf16[80,128]{1,0:T(8,128)(2,1)S(1)}, bf16[80,128]{1,0:T(8,128)(2,1)S(1)}, u32[]{:S(2)}, u32[]{:S(2)}) collective-permute-start(bf16[80,128]{1,0:T(8,128)(2,1)S(1)} %get-tuple-element.206), channel_id=1, source_target_pairs={{128,256},{136,264},{144,272},{152,280},{160,288},{168,296},{176,3... | collective-permute-start | bytes 61448 | tf_op jit(solution)/shard_map/ppermute | solution.py:554
  12.2 18.5 %conditional.9 = (bf16[128,512]{1,0:T(8,128)(2,1)S(1)}, f32[128,512]{1,0:T(8,128)S(1)}, f32[64,128]{1,0:T(8,128)S(1)}, f32[192,128]{1,0:T(8,128)S(1)}, f32[8,128...) conditional(s32[]{:T(128)} %convert_element_type.22, ...), branch_computations={%region_8.0_spmd, %region_9.0_spmd} | conditional | flops 10000004 | bytes 2021604 | solution.py:581
  12.3 1.3 %collective-permute-start.2 = (bf16[96,128]{1,0:T(8,128)(2,1)S(1)}, bf16[96,128]{1,0:T(8,128)(2,1)S(1)}, u32[]{:S(2)}, u32[]{:S(2)}) collective-permute-start(bf16[96,128]{1,0:T(8,128)(2,1)S(1)} %get-tuple-element.127), channel_id=1, source_target_pairs={{256,448},{264,456},{272,464},{280,472},{288,480},{296,488},{304,4... | collective-permute-start | bytes 73736 | tf_op jit(solution)/shard_map/cond/branch_1_fun/ppermute | solution.py:564
  13.6 1.3 %collective-permute-start.1 = (bf16[96,128]{1,0:T(8,128)(2,1)S(1)}, bf16[96,128]{1,0:T(8,128)(2,1)S(1)}, u32[]{:S(2)}, u32[]{:S(2)}) collective-permute-start(bf16[96,128]{1,0:T(8,128)(2,1)S(1)} %get-tuple-element.127), channel_id=1, source_target_pairs={{256,384},{264,392},{272,400},{280,408},{288,416},{296,424},{304,4... | collective-permute-start | bytes 73736 | tf_op jit(solution)/shard_map/cond/branch_1_fun/ppermute | solution.py:563
  14.9 10.2 %conditional.3 = (bf16[8,80,128]{2,1,0:T(8,128)(2,1)S(1)}) conditional(s32[]{:T(128)} %convert_element_type.17, () %tuple.45, bf16[8,80,128]{2,1,0:T(8,128)(2,1)S(1)} %get-tuple-element.124), branch_computations={%region_12.0_spmd, %region_13.0_spmd} | conditional | bytes 327688 | solution.py:524
  14.9 10.2 %all_to_all.24 = bf16[8,80,128]{2,1,0:T(8,128)(2,1)S(1)} all-to-all(bf16[8,80,128]{2,1,0:T(8,128)(2,1)S(1)} %param.12), channel_id=1, replica_groups={{56,48,40,32,24,16,8,0},{120,112,104,96,88,80,72,64},{184,176,168,160,1..., dimensions={0} | all-to-all | bytes 327680 | tf_op jit(solution)/shard_map/cond/branch_1_fun/cond/branch_1_fun/all_to_all | solution.py:478
  25.1 0.1 branch_1_fun.16
  25.2 3.4 %collective-permute-start.3 = (bf16[80,128]{1,0:T(8,128)(2,1)S(1)}, bf16[80,128]{1,0:T(8,128)(2,1)S(1)}, u32[]{:S(2)}, u32[]{:S(2)}) collective-permute-start(bf16[80,128]{1,0:T(8,128)(2,1)S(1)} %get-tuple-element.131), channel_id=1, source_target_pairs={{256,320},{264,328},{272,336},{280,344},{288,352},{296,360},{304,3... | collective-permute-start | bytes 61448 | tf_op jit(solution)/shard_map/cond/branch_1_fun/ppermute | solution.py:566
  28.6 1.6 %branch_1_fun.14 = f32[128,512]{1,0:T(8,128)S(1)} custom-call(f32[16,512]{1,0:T(8,128)S(1)} %get-tuple-element.120.rate_ref.refs_8_, f32[16,512]{1,0:T(8,128)S(1)} %get-tuple-element.121.residue_ref.refs_9_, f32[128,512]{1,0:T(8,128)S(1)} %get-tuple-element.122.product_ref), custom_call_target="tpu_custom_call" | custom-call | flops 10000000 | bytes 327680 | tf_op jit(solution)/shard_map/cond/branch_1_fun/pallas_call | solution.py:24
  30.2 0.0 collective-permute-done.3.refs_2_
  30.3 0.0 collective-permute-done.2.refs_1_
  30.3 0.2 collective-permute-done.1.refs_0_
  30.5 0.2 branch_1_fun.17
  30.7 0.0 copy-start
  30.7 0.0 collective-permute-done.4.third_ref
  30.7 5.0 %collective-permute-done.5.fourth_ref = bf16[96,128]{1,0:T(8,128)(2,1)S(1)} collective-permute-done((bf16[96,128]{1,0:T(8,128)(2,1)S(1)}, bf16[96,128]{1,0:T(8,128)(2,1)S(1)}, u32[]{:S(2)}, u32[]{:S(2)}) %collective-permute-start.5) | collective-permute-done | bytes 24608 | tf_op jit(solution)/shard_map/ppermute | solution.py:553
  35.7 0.0 copy-done
  35.7 1.0 %shard_map.57 = bf16[128,512]{1,0:T(8,128)(2,1)} custom-call(f32[64,128]{1,0:T(8,128)S(1)} %get-tuple-element.199.rest_ref, f32[192,128]{1,0:T(8,128)S(1)} %get-tuple-element.200.decay_ref, f32[8,128]{1,0:T(8,128)S(1)} %get-tuple-element.201.head_ref, f32[128,512]{1,0:T(8,128)S(1)} %get-tuple-element.202.lead_ref, ...), custom_call_target="tpu_custom_call", output_to_operand_aliasing={{}: (13, {})} | custom-call | bytes 1116160 | tf_op jit(solution)/shard_map/pallas_call | solution.py:24
  (7 shorter events, 0.1 us)
Async XLA Ops:
  10.2 25.5 %collective-permute-start.5 = (bf16[96,128]{1,0:T(8,128)(2,1)S(1)}, bf16[96,128]{1,0:T(8,128)(2,1)S(1)}, u32[]{:S(2)}, u32[]{:S(2)}) collective-permute-start(bf16[96,128]{1,0:T(8,128)(2,1)S(1)} %get-tuple-element.207), channel_id=1, source_target_pairs={{128,448},{136,456},{144,464},{152,472},{160,480},{168,488},{176,4... | collective-permute-start | bytes 73736 | tf_op jit(solution)/shard_map/ppermute | solution.py:553
  11.5 19.2 %collective-permute-start.4 = (bf16[80,128]{1,0:T(8,128)(2,1)S(1)}, bf16[80,128]{1,0:T(8,128)(2,1)S(1)}, u32[]{:S(2)}, u32[]{:S(2)}) collective-permute-start(bf16[80,128]{1,0:T(8,128)(2,1)S(1)} %get-tuple-element.206), channel_id=1, source_target_pairs={{128,256},{136,264},{144,272},{152,280},{160,288},{168,296},{176,3... | collective-permute-start | bytes 61448 | tf_op jit(solution)/shard_map/ppermute | solution.py:554
  12.3 18.0 %collective-permute-start.2 = (bf16[96,128]{1,0:T(8,128)(2,1)S(1)}, bf16[96,128]{1,0:T(8,128)(2,1)S(1)}, u32[]{:S(2)}, u32[]{:S(2)}) collective-permute-start(bf16[96,128]{1,0:T(8,128)(2,1)S(1)} %get-tuple-element.127), channel_id=1, source_target_pairs={{256,448},{264,456},{272,464},{280,472},{288,480},{296,488},{304,4... | collective-permute-start | bytes 73736 | tf_op jit(solution)/shard_map/cond/branch_1_fun/ppermute | solution.py:564
  13.6 16.9 %collective-permute-start.1 = (bf16[96,128]{1,0:T(8,128)(2,1)S(1)}, bf16[96,128]{1,0:T(8,128)(2,1)S(1)}, u32[]{:S(2)}, u32[]{:S(2)}) collective-permute-start(bf16[96,128]{1,0:T(8,128)(2,1)S(1)} %get-tuple-element.127), channel_id=1, source_target_pairs={{256,384},{264,392},{272,400},{280,408},{288,416},{296,424},{304,4... | collective-permute-start | bytes 73736 | tf_op jit(solution)/shard_map/cond/branch_1_fun/ppermute | solution.py:563
  25.2 5.0 %collective-permute-start.3 = (bf16[80,128]{1,0:T(8,128)(2,1)S(1)}, bf16[80,128]{1,0:T(8,128)(2,1)S(1)}, u32[]{:S(2)}, u32[]{:S(2)}) collective-permute-start(bf16[80,128]{1,0:T(8,128)(2,1)S(1)} %get-tuple-element.131), channel_id=1, source_target_pairs={{256,320},{264,328},{272,336},{280,344},{288,352},{296,360},{304,3... | collective-permute-start | bytes 61448 | tf_op jit(solution)/shard_map/cond/branch_1_fun/ppermute | solution.py:566
  30.7 5.0 %copy-start = (bf16[128,512]{1,0:T(8,128)(2,1)}, bf16[128,512]{1,0:T(8,128)(2,1)S(1)}, u32[]{:S(2)}) copy-start(bf16[128,512]{1,0:T(8,128)(2,1)S(1)} %get-tuple-element.208.held_ref) | copy-start | bytes 393220

commit v14 on v13

--- a/solution.py
+++ b/solution.py
@@ -181,7 +181,7 @@
 
 
 def first_slot(place, size):
-    return (3 - place // 4) * 4 + place % 4
+    return place % 4 * 4 + 3 - place // 4
 
 
 def near_scan(block, lanes, got_ref, rate_ref, taps_ref, before_ref, edge_ref, slot=slot):

time: 37 us -> 36.9 us (level)
  no operation moved by 1% of the time
where the time goes in v14:
time: 36.9 us; the launch traced here: 36.6 us
  blocking collectives  18.5 us (50%)
  starting transfers between devices  7.92 us (21%)
  waiting for transfers between devices  5.09 us (14%)
  Pallas kernels  4.8 us (13%)
    all_to_all x2, blocking collectives, gather(): lax.all_to_all(copies, axis, 0, 0, tiled=True, axis_index_groups=groups)  18.5 us
    ppermute x1, waiting for transfers between devices, per_device(): to_fourth = lax.ppermute(to_fourth, 'ctx', hops((second, turned)))  4.86 us
    pallas_call x10, Pallas kernels, call(): pl.pallas_call(body, out_shape=shapes, in_specs=[pl.BlockSpec(memory_spac...  4.8 us
    ppermute x1, starting transfers between devices, upper(): lax.ppermute(message, 'ctx', hops((runs[4], runs[5]), (runs[6], runs[7])))  3.38 us
    ppermute x1, starting transfers between devices, per_device(): to_fourth = lax.ppermute(to_fourth, 'ctx', hops((second, turned)))  1.29 us
    ppermute x1, starting transfers between devices, upper(): lax.ppermute(first_message, 'ctx', hops((runs[4], runs[7]), (runs[5], run...  1.29 us
    ppermute x1, starting transfers between devices, upper(): lax.ppermute(first_message, 'ctx', hops((runs[4], runs[6]), (runs[5], run...  1.29 us
  transfers between devices with their start and end apart: 5, of which 2 were waited for; matrix products, arithmetic and copies ran while one was open for 0% of the time, Pallas kernels for 5%

profile of v14, /device:TPU:416, one launch (start us, length us, event | category | flops | bytes accessed | tf_op | source)
XLA Modules:
  0.0 36.6 jit_solution(17921937149471803836)
XLA Ops:
  0.0 1.0 %shard_map.55 = (bf16[128,512]{1,0:T(8,128)(2,1)S(1)}, f32[1,512]{1,0:T(1,128)S(1)}, f32[3,3,512]{2,1,0:T(4,128)S(1)}, f32[16,512]{1,0:T(8,128)S(1)}, f32[16,512...) custom-call(bf16[128,512]{1,0:T(8,128)(2,1)} %refs_0_, ...), custom_call_target="tpu_custom_call" | custom-call | bytes 217088 | tf_op jit(solution)/shard_map/pallas_call | solution.py:24
  1.0 8.3 %conditional.7 = (f32[8,1,128]{2,1,0:T(1,128)S(1)}) conditional(s32[]{:T(128)} %convert_element_type.21, f32[8,1,128]{2,1,0:T(1,128)S(1)} %get-tuple-element.177, f32[8,1,128]{2,1,0:T(1,128)S(1)} %get-tuple-element.177), branch_computations={%region_0.0_spmd, %region_1.0_spmd} | conditional | bytes 16392 | solution.py:501
  1.0 8.3 %all_to_all.20 = f32[8,1,128]{2,1,0:T(1,128)S(1)} all-to-all(f32[8,1,128]{2,1,0:T(1,128)S(1)} %copy.50), channel_id=1, replica_groups={{7,6,5,4,3,2,1,0},{15,14,13,12,11,10,9,8},{23,22,21,20,19,18,17,16},{31..., dimensions={0} | all-to-all | bytes 8192 | tf_op jit(solution)/shard_map/cond/branch_1_fun/all_to_all | solution.py:478
  9.3 0.8 %shard_map.56 = (bf16[128,512]{1,0:T(8,128)(2,1)S(1)}, f32[128,512]{1,0:T(8,128)S(1)}, bf16[16,80,128]{2,1,0:T(8,128)(2,1)S(1)}, bf16[8,80,128]{2,1,0:T(8,128)(2,1)S(1)}) custom-call(f32[8,1,128]{2,1,0:T(1,128)S(1)} %get-tuple-element.245.refs_0_, bf16[128,512]{1,0:T(8,128)(2,1)S(1)} %get-tuple-element.178.refs_1_, f32[1,512]{1,0:T(1,128)S(1)} %get-tuple-element.179.refs_2_, ...), custom_call_target="tpu_custom_call" | custom-call | bytes 188416 | tf_op jit(solution)/shard_map/pallas_call | solution.py:24
  10.2 1.3 %collective-permute-start.5 = (bf16[96,128]{1,0:T(8,128)(2,1)S(1)}, bf16[96,128]{1,0:T(8,128)(2,1)S(1)}, u32[]{:S(2)}, u32[]{:S(2)}) collective-permute-start(bf16[96,128]{1,0:T(8,128)(2,1)S(1)} %get-tuple-element.207), channel_id=1, source_target_pairs={{128,448},{136,456},{144,464},{152,472},{160,480},{168,488},{176,4... | collective-permute-start | bytes 73736 | tf_op jit(solution)/shard_map/ppermute | solution.py:553
  11.5 0.7 %collective-permute-start.4 = (bf16[80,128]{1,0:T(8,128)(2,1)S(1)}, bf16[80,128]{1,0:T(8,128)(2,1)S(1)}, u32[]{:S(2)}, u32[]{:S(2)}) collective-permute-start(bf16[80,128]{1,0:T(8,128)(2,1)S(1)} %get-tuple-element.206), channel_id=1, source_target_pairs={{128,256},{136,264},{144,272},{152,280},{160,288},{168,296},{176,3... | collective-permute-start | bytes 61448 | tf_op jit(solution)/shard_map/ppermute | solution.py:554
  12.2 18.5 %conditional.9 = (bf16[128,512]{1,0:T(8,128)(2,1)S(1)}, f32[128,512]{1,0:T(8,128)S(1)}, f32[64,128]{1,0:T(8,128)S(1)}, f32[192,128]{1,0:T(8,128)S(1)}, f32[8,128...) conditional(s32[]{:T(128)} %convert_element_type.22, ...), branch_computations={%region_8.0_spmd, %region_9.0_spmd} | conditional | flops 10000004 | bytes 2021604 | solution.py:581
  12.3 1.3 %collective-permute-start.2 = (bf16[96,128]{1,0:T(8,128)(2,1)S(1)}, bf16[96,128]{1,0:T(8,128)(2,1)S(1)}, u32[]{:S(2)}, u32[]{:S(2)}) collective-permute-start(bf16[96,128]{1,0:T(8,128)(2,1)S(1)} %get-tuple-element.127), channel_id=1, source_target_pairs={{256,448},{264,456},{272,464},{280,472},{288,480},{296,488},{304,4... | collective-permute-start | bytes 73736 | tf_op jit(solution)/shard_map/cond/branch_1_fun/ppermute | solution.py:564
  13.6 1.3 %collective-permute-start.1 = (bf16[96,128]{1,0:T(8,128)(2,1)S(1)}, bf16[96,128]{1,0:T(8,128)(2,1)S(1)}, u32[]{:S(2)}, u32[]{:S(2)}) collective-permute-start(bf16[96,128]{1,0:T(8,128)(2,1)S(1)} %get-tuple-element.127), channel_id=1, source_target_pairs={{256,384},{264,392},{272,400},{280,408},{288,416},{296,424},{304,4... | collective-permute-start | bytes 73736 | tf_op jit(solution)/shard_map/cond/branch_1_fun/ppermute | solution.py:563
  14.9 10.2 %conditional.3 = (bf16[8,80,128]{2,1,0:T(8,128)(2,1)S(1)}) conditional(s32[]{:T(128)} %convert_element_type.17, () %tuple.45, bf16[8,80,128]{2,1,0:T(8,128)(2,1)S(1)} %get-tuple-element.124), branch_computations={%region_12.0_spmd, %region_13.0_spmd} | conditional | bytes 327688 | solution.py:524
  14.9 10.2 %all_to_all.24 = bf16[8,80,128]{2,1,0:T(8,128)(2,1)S(1)} all-to-all(bf16[8,80,128]{2,1,0:T(8,128)(2,1)S(1)} %param.12), channel_id=1, replica_groups={{56,48,40,32,24,16,8,0},{120,112,104,96,88,80,72,64},{184,176,168,160,1..., dimensions={0} | all-to-all | bytes 327680 | tf_op jit(solution)/shard_map/cond/branch_1_fun/cond/branch_1_fun/all_to_all | solution.py:478
  25.1 0.1 branch_1_fun.16
  25.2 3.4 %collective-permute-start.3 = (bf16[80,128]{1,0:T(8,128)(2,1)S(1)}, bf16[80,128]{1,0:T(8,128)(2,1)S(1)}, u32[]{:S(2)}, u32[]{:S(2)}) collective-permute-start(bf16[80,128]{1,0:T(8,128)(2,1)S(1)} %get-tuple-element.131), channel_id=1, source_target_pairs={{256,320},{264,328},{272,336},{280,344},{288,352},{296,360},{304,3... | collective-permute-start | bytes 61448 | tf_op jit(solution)/shard_map/cond/branch_1_fun/ppermute | solution.py:566
  28.6 1.6 %branch_1_fun.14 = f32[128,512]{1,0:T(8,128)S(1)} custom-call(f32[16,512]{1,0:T(8,128)S(1)} %get-tuple-element.120.rate_ref.refs_8_, f32[16,512]{1,0:T(8,128)S(1)} %get-tuple-element.121.residue_ref.refs_9_, f32[128,512]{1,0:T(8,128)S(1)} %get-tuple-element.122.product_ref), custom_call_target="tpu_custom_call" | custom-call | flops 10000000 | bytes 327680 | tf_op jit(solution)/shard_map/cond/branch_1_fun/pallas_call | solution.py:24
  30.2 0.0 collective-permute-done.3.refs_2_
  30.3 0.0 collective-permute-done.2.refs_1_
  30.3 0.2 collective-permute-done.1.refs_0_
  30.5 0.2 branch_1_fun.17
  30.7 0.0 copy-start
  30.7 0.0 collective-permute-done.4.third_ref
  30.7 4.9 %collective-permute-done.5.fourth_ref = bf16[96,128]{1,0:T(8,128)(2,1)S(1)} collective-permute-done((bf16[96,128]{1,0:T(8,128)(2,1)S(1)}, bf16[96,128]{1,0:T(8,128)(2,1)S(1)}, u32[]{:S(2)}, u32[]{:S(2)}) %collective-permute-start.5) | collective-permute-done | bytes 24608 | tf_op jit(solution)/shard_map/ppermute | solution.py:553
  35.6 0.0 copy-done
  35.6 1.0 %shard_map.57 = bf16[128,512]{1,0:T(8,128)(2,1)} custom-call(f32[64,128]{1,0:T(8,128)S(1)} %get-tuple-element.199.rest_ref, f32[192,128]{1,0:T(8,128)S(1)} %get-tuple-element.200.decay_ref, f32[8,128]{1,0:T(8,128)S(1)} %get-tuple-element.201.head_ref, f32[128,512]{1,0:T(8,128)S(1)} %get-tuple-element.202.lead_ref, ...), custom_call_target="tpu_custom_call", output_to_operand_aliasing={{}: (13, {})} | custom-call | bytes 1116160 | tf_op jit(solution)/shard_map/pallas_call | solution.py:24
  (7 shorter events, 0.1 us)
Async XLA Ops:
  10.2 25.4 %collective-permute-start.5 = (bf16[96,128]{1,0:T(8,128)(2,1)S(1)}, bf16[96,128]{1,0:T(8,128)(2,1)S(1)}, u32[]{:S(2)}, u32[]{:S(2)}) collective-permute-start(bf16[96,128]{1,0:T(8,128)(2,1)S(1)} %get-tuple-element.207), channel_id=1, source_target_pairs={{128,448},{136,456},{144,464},{152,472},{160,480},{168,488},{176,4... | collective-permute-start | bytes 73736 | tf_op jit(solution)/shard_map/ppermute | solution.py:553
  11.5 19.2 %collective-permute-start.4 = (bf16[80,128]{1,0:T(8,128)(2,1)S(1)}, bf16[80,128]{1,0:T(8,128)(2,1)S(1)}, u32[]{:S(2)}, u32[]{:S(2)}) collective-permute-start(bf16[80,128]{1,0:T(8,128)(2,1)S(1)} %get-tuple-element.206), channel_id=1, source_target_pairs={{128,256},{136,264},{144,272},{152,280},{160,288},{168,296},{176,3... | collective-permute-start | bytes 61448 | tf_op jit(solution)/shard_map/ppermute | solution.py:554
  12.3 18.0 %collective-permute-start.2 = (bf16[96,128]{1,0:T(8,128)(2,1)S(1)}, bf16[96,128]{1,0:T(8,128)(2,1)S(1)}, u32[]{:S(2)}, u32[]{:S(2)}) collective-permute-start(bf16[96,128]{1,0:T(8,128)(2,1)S(1)} %get-tuple-element.127), channel_id=1, source_target_pairs={{256,448},{264,456},{272,464},{280,472},{288,480},{296,488},{304,4... | collective-permute-start | bytes 73736 | tf_op jit(solution)/shard_map/cond/branch_1_fun/ppermute | solution.py:564
  13.6 16.9 %collective-permute-start.1 = (bf16[96,128]{1,0:T(8,128)(2,1)S(1)}, bf16[96,128]{1,0:T(8,128)(2,1)S(1)}, u32[]{:S(2)}, u32[]{:S(2)}) collective-permute-start(bf16[96,128]{1,0:T(8,128)(2,1)S(1)} %get-tuple-element.127), channel_id=1, source_target_pairs={{256,384},{264,392},{272,400},{280,408},{288,416},{296,424},{304,4... | collective-permute-start | bytes 73736 | tf_op jit(solution)/shard_map/cond/branch_1_fun/ppermute | solution.py:563
  25.2 5.0 %collective-permute-start.3 = (bf16[80,128]{1,0:T(8,128)(2,1)S(1)}, bf16[80,128]{1,0:T(8,128)(2,1)S(1)}, u32[]{:S(2)}, u32[]{:S(2)}) collective-permute-start(bf16[80,128]{1,0:T(8,128)(2,1)S(1)} %get-tuple-element.131), channel_id=1, source_target_pairs={{256,320},{264,328},{272,336},{280,344},{288,352},{296,360},{304,3... | collective-permute-start | bytes 61448 | tf_op jit(solution)/shard_map/cond/branch_1_fun/ppermute | solution.py:566
  30.7 4.9 %copy-start = (bf16[128,512]{1,0:T(8,128)(2,1)}, bf16[128,512]{1,0:T(8,128)(2,1)S(1)}, u32[]{:S(2)}) copy-start(bf16[128,512]{1,0:T(8,128)(2,1)S(1)} %get-tuple-element.208.held_ref) | copy-start | bytes 393220

commit v15 on v13

--- a/solution.py
+++ b/solution.py
@@ -177,7 +177,7 @@
 
 
 def slot(place, size):
-    return size - 1 - place
+    return place // 4 * 4 + 3 - place % 4 if size == WIDE else size - 1 - place
 
 
 def first_slot(place, size):

time: 37 us -> 37 us (level)
  no operation moved by 1% of the time
where the time goes in v15:
time: 37 us; the launch traced here: 36.7 us
  blocking collectives  18.5 us (50%)
  starting transfers between devices  7.92 us (21%)
  waiting for transfers between devices  5.25 us (14%)
  Pallas kernels  4.8 us (13%)
    all_to_all x2, blocking collectives, gather(): lax.all_to_all(copies, axis, 0, 0, tiled=True, axis_index_groups=groups)  18.5 us
    ppermute x1, waiting for transfers between devices, per_device(): to_fourth = lax.ppermute(to_fourth, 'ctx', hops((second, turned)))  5.01 us
    pallas_call x10, Pallas kernels, call(): pl.pallas_call(body, out_shape=shapes, in_specs=[pl.BlockSpec(memory_spac...  4.8 us
    ppermute x1, starting transfers between devices, upper(): lax.ppermute(message, 'ctx', hops((runs[4], runs[5]), (runs[6], runs[7])))  3.38 us
    ppermute x1, starting transfers between devices, per_device(): to_fourth = lax.ppermute(to_fourth, 'ctx', hops((second, turned)))  1.29 us
    ppermute x1, starting transfers between devices, upper(): lax.ppermute(first_message, 'ctx', hops((runs[4], runs[7]), (runs[5], run...  1.29 us
    ppermute x1, starting transfers between devices, upper(): lax.ppermute(first_message, 'ctx', hops((runs[4], runs[6]), (runs[5], run...  1.29 us
  transfers between devices with their start and end apart: 5, of which 2 were waited for; matrix products, arithmetic and copies ran while one was open for 0% of the time, Pallas kernels for 5%

profile of v15, /device:TPU:416, one launch (start us, length us, event | category | flops | bytes accessed | tf_op | source)
XLA Modules:
  0.0 36.7 jit_solution(12594338119105766056)
XLA Ops:
  0.0 1.0 %shard_map.55 = (bf16[128,512]{1,0:T(8,128)(2,1)S(1)}, f32[1,512]{1,0:T(1,128)S(1)}, f32[3,3,512]{2,1,0:T(4,128)S(1)}, f32[16,512]{1,0:T(8,128)S(1)}, f32[16,512...) custom-call(bf16[128,512]{1,0:T(8,128)(2,1)} %refs_0_, ...), custom_call_target="tpu_custom_call" | custom-call | bytes 217088 | tf_op jit(solution)/shard_map/pallas_call | solution.py:24
  1.0 8.3 %conditional.7 = (f32[8,1,128]{2,1,0:T(1,128)S(1)}) conditional(s32[]{:T(128)} %convert_element_type.21, f32[8,1,128]{2,1,0:T(1,128)S(1)} %get-tuple-element.177, f32[8,1,128]{2,1,0:T(1,128)S(1)} %get-tuple-element.177), branch_computations={%region_0.0_spmd, %region_1.0_spmd} | conditional | bytes 16392 | solution.py:501
  1.0 8.3 %all_to_all.20 = f32[8,1,128]{2,1,0:T(1,128)S(1)} all-to-all(f32[8,1,128]{2,1,0:T(1,128)S(1)} %copy.50), channel_id=1, replica_groups={{7,6,5,4,3,2,1,0},{15,14,13,12,11,10,9,8},{23,22,21,20,19,18,17,16},{31..., dimensions={0} | all-to-all | bytes 8192 | tf_op jit(solution)/shard_map/cond/branch_1_fun/all_to_all | solution.py:478
  9.3 0.8 %shard_map.56 = (bf16[128,512]{1,0:T(8,128)(2,1)S(1)}, f32[128,512]{1,0:T(8,128)S(1)}, bf16[16,80,128]{2,1,0:T(8,128)(2,1)S(1)}, bf16[8,80,128]{2,1,0:T(8,128)(2,1)S(1)}) custom-call(f32[8,1,128]{2,1,0:T(1,128)S(1)} %get-tuple-element.245.refs_0_, bf16[128,512]{1,0:T(8,128)(2,1)S(1)} %get-tuple-element.178.refs_1_, f32[1,512]{1,0:T(1,128)S(1)} %get-tuple-element.179.refs_2_, ...), custom_call_target="tpu_custom_call" | custom-call | bytes 188416 | tf_op jit(solution)/shard_map/pallas_call | solution.py:24
  10.2 1.3 %collective-permute-start.5 = (bf16[96,128]{1,0:T(8,128)(2,1)S(1)}, bf16[96,128]{1,0:T(8,128)(2,1)S(1)}, u32[]{:S(2)}, u32[]{:S(2)}) collective-permute-start(bf16[96,128]{1,0:T(8,128)(2,1)S(1)} %get-tuple-element.207), channel_id=1, source_target_pairs={{128,448},{136,456},{144,464},{152,472},{160,480},{168,488},{176,4... | collective-permute-start | bytes 73736 | tf_op jit(solution)/shard_map/ppermute | solution.py:553
  11.5 0.7 %collective-permute-start.4 = (bf16[80,128]{1,0:T(8,128)(2,1)S(1)}, bf16[80,128]{1,0:T(8,128)(2,1)S(1)}, u32[]{:S(2)}, u32[]{:S(2)}) collective-permute-start(bf16[80,128]{1,0:T(8,128)(2,1)S(1)} %get-tuple-element.206), channel_id=1, source_target_pairs={{128,256},{136,264},{144,272},{152,280},{160,288},{168,296},{176,3... | collective-permute-start | bytes 61448 | tf_op jit(solution)/shard_map/ppermute | solution.py:554
  12.2 18.5 %conditional.9 = (bf16[128,512]{1,0:T(8,128)(2,1)S(1)}, f32[128,512]{1,0:T(8,128)S(1)}, f32[64,128]{1,0:T(8,128)S(1)}, f32[192,128]{1,0:T(8,128)S(1)}, f32[8,128...) conditional(s32[]{:T(128)} %convert_element_type.22, ...), branch_computations={%region_8.0_spmd, %region_9.0_spmd} | conditional | flops 10000004 | bytes 2021604 | solution.py:581
  12.3 1.3 %collective-permute-start.2 = (bf16[96,128]{1,0:T(8,128)(2,1)S(1)}, bf16[96,128]{1,0:T(8,128)(2,1)S(1)}, u32[]{:S(2)}, u32[]{:S(2)}) collective-permute-start(bf16[96,128]{1,0:T(8,128)(2,1)S(1)} %get-tuple-element.127), channel_id=1, source_target_pairs={{256,448},{264,456},{272,464},{280,472},{288,480},{296,488},{304,4... | collective-permute-start | bytes 73736 | tf_op jit(solution)/shard_map/cond/branch_1_fun/ppermute | solution.py:564
  13.6 1.3 %collective-permute-start.1 = (bf16[96,128]{1,0:T(8,128)(2,1)S(1)}, bf16[96,128]{1,0:T(8,128)(2,1)S(1)}, u32[]{:S(2)}, u32[]{:S(2)}) collective-permute-start(bf16[96,128]{1,0:T(8,128)(2,1)S(1)} %get-tuple-element.127), channel_id=1, source_target_pairs={{256,384},{264,392},{272,400},{280,408},{288,416},{296,424},{304,4... | collective-permute-start | bytes 73736 | tf_op jit(solution)/shard_map/cond/branch_1_fun/ppermute | solution.py:563
  14.9 10.2 %conditional.3 = (bf16[8,80,128]{2,1,0:T(8,128)(2,1)S(1)}) conditional(s32[]{:T(128)} %convert_element_type.17, () %tuple.45, bf16[8,80,128]{2,1,0:T(8,128)(2,1)S(1)} %get-tuple-element.124), branch_computations={%region_12.0_spmd, %region_13.0_spmd} | conditional | bytes 327688 | solution.py:524
  14.9 10.2 %all_to_all.24 = bf16[8,80,128]{2,1,0:T(8,128)(2,1)S(1)} all-to-all(bf16[8,80,128]{2,1,0:T(8,128)(2,1)S(1)} %param.12), channel_id=1, replica_groups={{56,48,40,32,24,16,8,0},{120,112,104,96,88,80,72,64},{184,176,168,160,1..., dimensions={0} | all-to-all | bytes 327680 | tf_op jit(solution)/shard_map/cond/branch_1_fun/cond/branch_1_fun/all_to_all | solution.py:478
  25.1 0.1 branch_1_fun.16
  25.2 3.4 %collective-permute-start.3 = (bf16[80,128]{1,0:T(8,128)(2,1)S(1)}, bf16[80,128]{1,0:T(8,128)(2,1)S(1)}, u32[]{:S(2)}, u32[]{:S(2)}) collective-permute-start(bf16[80,128]{1,0:T(8,128)(2,1)S(1)} %get-tuple-element.131), channel_id=1, source_target_pairs={{256,320},{264,328},{272,336},{280,344},{288,352},{296,360},{304,3... | collective-permute-start | bytes 61448 | tf_op jit(solution)/shard_map/cond/branch_1_fun/ppermute | solution.py:566
  28.6 1.6 %branch_1_fun.14 = f32[128,512]{1,0:T(8,128)S(1)} custom-call(f32[16,512]{1,0:T(8,128)S(1)} %get-tuple-element.120.rate_ref.refs_8_, f32[16,512]{1,0:T(8,128)S(1)} %get-tuple-element.121.residue_ref.refs_9_, f32[128,512]{1,0:T(8,128)S(1)} %get-tuple-element.122.product_ref), custom_call_target="tpu_custom_call" | custom-call | flops 10000000 | bytes 327680 | tf_op jit(solution)/shard_map/cond/branch_1_fun/pallas_call | solution.py:24
  30.2 0.0 collective-permute-done.3.refs_2_
  30.3 0.0 collective-permute-done.2.refs_1_
  30.3 0.2 collective-permute-done.1.refs_0_
  30.5 0.2 branch_1_fun.17
  30.7 0.0 copy-start
  30.7 0.0 collective-permute-done.4.third_ref
  30.7 5.0 %collective-permute-done.5.fourth_ref = bf16[96,128]{1,0:T(8,128)(2,1)S(1)} collective-permute-done((bf16[96,128]{1,0:T(8,128)(2,1)S(1)}, bf16[96,128]{1,0:T(8,128)(2,1)S(1)}, u32[]{:S(2)}, u32[]{:S(2)}) %collective-permute-start.5) | collective-permute-done | bytes 24608 | tf_op jit(solution)/shard_map/ppermute | solution.py:553
  35.7 0.0 copy-done
  35.7 1.0 %shard_map.57 = bf16[128,512]{1,0:T(8,128)(2,1)} custom-call(f32[64,128]{1,0:T(8,128)S(1)} %get-tuple-element.199.rest_ref, f32[192,128]{1,0:T(8,128)S(1)} %get-tuple-element.200.decay_ref, f32[8,128]{1,0:T(8,128)S(1)} %get-tuple-element.201.head_ref, f32[128,512]{1,0:T(8,128)S(1)} %get-tuple-element.202.lead_ref, ...), custom_call_target="tpu_custom_call", output_to_operand_aliasing={{}: (13, {})} | custom-call | bytes 1116160 | tf_op jit(solution)/shard_map/pallas_call | solution.py:24
  (7 shorter events, 0.1 us)
Async XLA Ops:
  10.2 25.5 %collective-permute-start.5 = (bf16[96,128]{1,0:T(8,128)(2,1)S(1)}, bf16[96,128]{1,0:T(8,128)(2,1)S(1)}, u32[]{:S(2)}, u32[]{:S(2)}) collective-permute-start(bf16[96,128]{1,0:T(8,128)(2,1)S(1)} %get-tuple-element.207), channel_id=1, source_target_pairs={{128,448},{136,456},{144,464},{152,472},{160,480},{168,488},{176,4... | collective-permute-start | bytes 73736 | tf_op jit(solution)/shard_map/ppermute | solution.py:553
  11.5 19.2 %collective-permute-start.4 = (bf16[80,128]{1,0:T(8,128)(2,1)S(1)}, bf16[80,128]{1,0:T(8,128)(2,1)S(1)}, u32[]{:S(2)}, u32[]{:S(2)}) collective-permute-start(bf16[80,128]{1,0:T(8,128)(2,1)S(1)} %get-tuple-element.206), channel_id=1, source_target_pairs={{128,256},{136,264},{144,272},{152,280},{160,288},{168,296},{176,3... | collective-permute-start | bytes 61448 | tf_op jit(solution)/shard_map/ppermute | solution.py:554
  12.3 18.0 %collective-permute-start.2 = (bf16[96,128]{1,0:T(8,128)(2,1)S(1)}, bf16[96,128]{1,0:T(8,128)(2,1)S(1)}, u32[]{:S(2)}, u32[]{:S(2)}) collective-permute-start(bf16[96,128]{1,0:T(8,128)(2,1)S(1)} %get-tuple-element.127), channel_id=1, source_target_pairs={{256,448},{264,456},{272,464},{280,472},{288,480},{296,488},{304,4... | collective-permute-start | bytes 73736 | tf_op jit(solution)/shard_map/cond/branch_1_fun/ppermute | solution.py:564
  13.6 16.9 %collective-permute-start.1 = (bf16[96,128]{1,0:T(8,128)(2,1)S(1)}, bf16[96,128]{1,0:T(8,128)(2,1)S(1)}, u32[]{:S(2)}, u32[]{:S(2)}) collective-permute-start(bf16[96,128]{1,0:T(8,128)(2,1)S(1)} %get-tuple-element.127), channel_id=1, source_target_pairs={{256,384},{264,392},{272,400},{280,408},{288,416},{296,424},{304,4... | collective-permute-start | bytes 73736 | tf_op jit(solution)/shard_map/cond/branch_1_fun/ppermute | solution.py:563
  25.2 5.0 %collective-permute-start.3 = (bf16[80,128]{1,0:T(8,128)(2,1)S(1)}, bf16[80,128]{1,0:T(8,128)(2,1)S(1)}, u32[]{:S(2)}, u32[]{:S(2)}) collective-permute-start(bf16[80,128]{1,0:T(8,128)(2,1)S(1)} %get-tuple-element.131), channel_id=1, source_target_pairs={{256,320},{264,328},{272,336},{280,344},{288,352},{296,360},{304,3... | collective-permute-start | bytes 61448 | tf_op jit(solution)/shard_map/cond/branch_1_fun/ppermute | solution.py:566
  30.7 5.0 %copy-start = (bf16[128,512]{1,0:T(8,128)(2,1)}, bf16[128,512]{1,0:T(8,128)(2,1)S(1)}, u32[]{:S(2)}) copy-start(bf16[128,512]{1,0:T(8,128)(2,1)S(1)} %get-tuple-element.208.held_ref) | copy-start | bytes 393220
